TPU v7x, 32 devices: a whole 2x2x4 slice. The times are simulated.
32 devices in a mesh: groups: 2 (over x), gx: 8 (over z, y), gy: 2 (over core).
Axes of the slice: x: 2, y: 2, z: 4, core: 2. Of those that a mesh axis runs over, the one named last changes fastest.
Arguments:
- fixed: bfloat16 [1024, 256, 128], P(('groups', 'gx'), 'gy'), parts along dimension 0, may hold values from -6 to 6
- moving: bfloat16 [1024, 256, 128], P(('groups', 'gx'), 'gy'), parts along dimension 0, may hold values from -6 to 6
- source_x: int32 [4, 8, 4, 2], P('groups'), parts along dimension 0, may hold values from 0 to 7, as said below
- source_z: int32 [4, 8, 4, 2], P('groups'), parts along dimension 0, may hold values from 0 to 1
Outputs:
- field: float32 [3, 1024, 256, 128], P(None, ('groups', 'gx'), 'gy'), parts along dimension 1
- mismatch: float32 [1024, 256, 128], P(('groups', 'gx'), 'gy'), parts along dimension 0
There are 2 independent parts, one for each index of `groups`. A program takes and returns all parts, laid end to end along the dimension named above; each array names one. Nothing has to cross between parts.
Inputs may be any that keep to these rules, and one draw needn't show every extreme that they name: `source_x`: in every iteration, the 4 target blocks that share one x index and one aligned group of 2 y indices (b from 2 * g to 2 * g + 1) name different source x indices.
All inputs are finite; a program needn't handle non-finite values.
Results may differ from a plain program's by a relative error of at most 0.0003.
Values may be sent and summed in bfloat16 or wider, within the bound.
No kernel may reach another device: no remote copies, remote signals or barrier semaphores. Data moves between devices by JAX's collectives and lax.ppermute only.
A program may use at most 256 MiB of HBM per device.

v0:
```python
import jax
import jax.numpy as jnp
from jax import lax
from jax.sharding import PartitionSpec as P

BLK = 64
ITERS = 2
RADIUS = 4


STIFF = 0.05


def with_halo(value, sides, width):
    for axis, dim in sides:
        size, length = (lax.axis_size(axis), value.shape[dim])
        up = [(i, (i + 1) % size) for i in range(size - 1)]
        down = [(j, i) for i, j in up]
        last = lax.slice_in_dim(value, length - width, length, axis=dim)
        leading = lax.slice_in_dim(value, 0, width, axis=dim)
        before = lax.ppermute(last, axis, up)
        after = lax.ppermute(leading, axis, down)
        value = jnp.concatenate([before, value, after], axis=dim)
    return value


def gauss_taps():
    offsets = jnp.arange(-RADIUS, RADIUS + 1).astype(jnp.float32)
    weights = jnp.exp(-offsets * offsets / 4.5)
    return weights / jnp.sum(weights)


def tent_weight(offset):
    return jnp.maximum(0.0, 1.0 - jnp.abs(offset))


def warp_block(source, displace):
    extent = displace.shape[1]
    result = jnp.zeros(displace.shape[1:], jnp.float32)
    for shift_x in (-1, 0, 1):
        weight_x = tent_weight(displace[0] - shift_x)
        for shift_y in (-1, 0, 1):
            weight_xy = weight_x * tent_weight(displace[1] - shift_y)
            for shift_z in (-1, 0, 1):
                weight = weight_xy * tent_weight(displace[2] - shift_z)
                starts = (2 + shift_x, 2 + shift_y, 2 + shift_z)
                section = lax.slice(
                    source, starts, (starts[0] + extent, starts[1] + extent, starts[2] + extent)
                )
                result = result + weight * section.astype(jnp.float32)
    return result


def central(padded):
    along_x = (padded[2:, 1:-1, 1:-1] - padded[:-2, 1:-1, 1:-1]) * 0.5
    along_y = (padded[1:-1, 2:, 1:-1] - padded[1:-1, :-2, 1:-1]) * 0.5
    along_z = (padded[1:-1, 1:-1, 2:] - padded[1:-1, 1:-1, :-2]) * 0.5
    return jnp.stack([along_x, along_y, along_z])


def filter_padded(padded, axis_pos, length, kernel_taps):
    result = kernel_taps[0] * lax.slice_in_dim(padded, 0, length, axis=axis_pos)
    for offset in range(1, 2 * RADIUS + 1):
        result = result + kernel_taps[offset] * lax.slice_in_dim(
            padded, offset, offset + length, axis=axis_pos
        )
    return result


def smooth_along(values, axis_pos, kernel_taps):
    widths = [(0, 0)] * values.ndim
    widths[axis_pos] = (RADIUS, RADIUS)
    return filter_padded(jnp.pad(values, widths), axis_pos, values.shape[axis_pos], kernel_taps)


def local(fixed, moving, source_x, source_z):
    tile_x, tile_y, tile_z = fixed.shape
    groups_y = tile_y // BLK
    groups_z = tile_z // BLK
    block_count = groups_y * groups_z
    extent = BLK + 4
    rank_count = lax.axis_size("gx")
    column = lax.axis_index("gx")
    row_index = lax.axis_index("gy")
    kernel_taps = gauss_taps()
    rimmed = with_halo(jnp.stack([fixed, moving]), (("gx", 1), ("gy", 2)), 2)
    fixed_rim = rimmed[0, 1:-1, 1:-1]
    fixed_float = fixed.astype(jnp.float32)
    moving_pad = jnp.pad(rimmed[1], ((0, 0), (0, 0), (2, 2)))
    sources = jnp.stack(
        [
            moving_pad[
                :, block_y * BLK : block_y * BLK + extent, block_z * BLK : block_z * BLK + extent
            ].reshape(-1)
            for block_y in range(groups_y)
            for block_z in range(groups_z)
        ]
    )
    local_x = lax.dynamic_slice_in_dim(source_x, row_index * groups_y, groups_y, 2)
    local_z = lax.dynamic_slice_in_dim(source_z, row_index * groups_y, groups_y, 2)
    depth_ids = jnp.arange(groups_z, dtype=jnp.int32)
    field = jnp.zeros((3, tile_x, tile_y, tile_z), jnp.float32)
    mismatch = jnp.zeros((tile_x, tile_y, tile_z), jnp.float32)
    for segment in range(ITERS):
        owned = (local_x[segment] == column).astype(jnp.float32)
        chosen = (local_z[segment][..., None] == depth_ids).astype(jnp.float32)
        selector = (
            jnp.sum(owned[..., None] * chosen, axis=2)
            .reshape(rank_count, block_count)
            .astype(jnp.bfloat16)
        )
        incoming = lax.all_to_all(
            jnp.dot(selector, sources, preferred_element_type=jnp.float32).astype(jnp.bfloat16),
            "gx",
            split_axis=0,
            concat_axis=0,
            tiled=True,
        )
        wanted = lax.dynamic_index_in_dim(local_x[segment], column, 0, keepdims=False).reshape(-1)
        picked = jnp.take(incoming, wanted, axis=0).reshape(block_count, extent, extent, extent)
        rows_out = []
        for block_y in range(groups_y):
            parts_z = []
            for block_z in range(groups_z):
                displace = field[
                    :, :, block_y * BLK : (block_y + 1) * BLK, block_z * BLK : (block_z + 1) * BLK
                ]
                parts_z.append(warp_block(picked[block_y * groups_z + block_z], displace))
            rows_out.append(jnp.concatenate(parts_z, axis=2))
        warped = jnp.concatenate(rows_out, axis=1)
        warped_pad = with_halo(warped, (("gx", 0), ("gy", 1)), 1)
        mismatch = fixed_float - warped
        grad_fixed = central(jnp.pad(fixed_rim.astype(jnp.float32), ((0, 0), (0, 0), (1, 1))))
        mean_grad = 0.5 * (grad_fixed + central(jnp.pad(warped_pad, ((0, 0), (0, 0), (1, 1)))))
        denominator = jnp.sum(mean_grad * mean_grad, axis=0) + mismatch * mismatch + STIFF
        summed = field + mismatch * mean_grad / denominator
        widened = with_halo(summed, (("gx", 1), ("gy", 2)), RADIUS)
        summed = filter_padded(widened, 1, tile_x, kernel_taps)
        summed = filter_padded(summed, 2, tile_y, kernel_taps)
        field = smooth_along(summed, 3, kernel_taps)
    return (field, mismatch)


def solution(mesh):
    return jax.shard_map(
        local,
        mesh=mesh,
        in_specs=(
            P(("groups", "gx"), "gy", None),
            P(("groups", "gx"), "gy", None),
            P("groups", None, None, None),
            P("groups", None, None, None),
        ),
        out_specs=(P(None, ("groups", "gx"), "gy", None), P(("groups", "gx"), "gy", None)),
        check_vma=False,
    )
```

profile of v0, /device:TPU:23, one launch (start us, length us, event | category | flops | bytes accessed | tf_op | source)
XLA Modules:
  0.0 1168.1 jit_solution(9102642486236718718)
XLA Ops:
  46.9 11.8 %fusion = bf16[8,1,314432]{2,0,1:T(8,128)(2,1)} fusion(bf16[8,4]{0,1:T(4,128)(2,1)S(1)} %bitcast.703, bf16[1,314432]{1,0:T(2,128)(2,1)} %stack_reshape.15, bf16[1,314432]{1,0:T(2,128)(2,1)} %stack_reshape.14, bf16[1,314432]{1,0:T(2,128)(2,1)} %stack_reshape.13, bf16[1,314432]{1,0:T(2,128)(2,1)} %stack_reshape.12), kind=kOutput, calls=%fused_computation.8 | convolution fusion | flops 32700928 | bytes 7546432 | tf_op jit(solution)/shard_map/dot_general | solution.py:113
  85.0 11.9 %fusion.1 = bf16[8,1,314432]{2,0,1:T(8,128)(2,1)} fusion(bf16[8,4]{0,1:T(4,128)(2,1)S(1)} %bitcast.702, bf16[1,314432]{1,0:T(2,128)(2,1)} %stack_reshape.15, bf16[1,314432]{1,0:T(2,128)(2,1)} %stack_reshape.14, bf16[1,314432]{1,0:T(2,128)(2,1)} %stack_reshape.13, bf16[1,314432]{1,0:T(2,128)(2,1)} %stack_reshape.12), kind=kOutput, calls=%fused_computation.9 | convolution fusion | flops 32700928 | bytes 7546432 | tf_op jit(solution)/shard_map/dot_general | solution.py:113
  125.3 64.2 %all-to-all-done = bf16[8,2,157216]{2,1,0:T(2,128)(2,1)} async-done(((bf16[8,2,157216]{2,1,0:T(2,128)(2,1)}), bf16[8,2,157216]{2,1,0:T(2,128)(2,1)}, u32[]{:S(2)}, u32[]{:S(2)}) %all-to-all-start) | async-done | bytes 5030944 | tf_op jit(solution)/shard_map/all_to_all | solution.py:112
  197.1 18.2 %reshape.529 = bf16[8,1,314432]{2,1,0:T(2,128)(2,1)} reshape(bf16[8,2,157216]{2,1,0:T(2,128)(2,1)} %all-to-all-done) | data formatting | bytes 10061824
  224.2 80.6 %all-to-all-done.1 = bf16[8,2,157216]{2,1,0:T(2,128)(2,1)} async-done(((bf16[8,2,157216]{2,1,0:T(2,128)(2,1)}), bf16[8,2,157216]{2,1,0:T(2,128)(2,1)}, u32[]{:S(2)}, u32[]{:S(2)}) %all-to-all-start.1) | async-done | bytes 5030944 | tf_op jit(solution)/shard_map/all_to_all | solution.py:112
  304.8 18.2 %reshape.531 = bf16[8,1,314432]{2,1,0:T(2,128)(2,1)} reshape(bf16[8,2,157216]{2,1,0:T(2,128)(2,1)} %all-to-all-done.1) | data formatting | bytes 10061824
  343.8 12.4 %maximum_select_fusion = bf16[4,314432]{1,0:T(4,128)(2,1)S(1)} fusion(bf16[4,104768]{1,0:T(4,128)(2,1)S(1)} %gather_fusion.2, bf16[4,104832]{1,0:T(4,128)(2,1)} %gather_fusion.1, bf16[4,104832]{1,0:T(4,128)(2,1)} %gather_fusion, pred[4]{0:T(512)(128)(4,1)S(1)} %get-tuple-element.65), kind=kLoop, calls=%fused_computation.235 | loop fusion | flops 8804096 | bytes 5030916 | tf_op jit(solution)/shard_map/jit(_take)/select_n | solution.py:120
  356.3 16.2 %slice_reduce_fusion.7 = (bf16[314432]{0:T(1024)(128)(2,1)}, bf16[314432]{0:T(1024)(128)(2,1)}, bf16[314432]{0:T(1024)(128)(2,1)}, bf16[314432]{0:T(1024)(128)(2,1)}) fusion(bf16[4,314432]{1,0:T(4,128)(2,1)S(1)} %maximum_select_fusion), kind=kLoop, calls=%fused_computation.521 | loop fusion | bytes 5030912 | tf_op jit(solution)/shard_map/slice | solution.py:128
  524.5 24.0 %maximum_select_fusion.1 = bf16[4,314432]{1,0:T(4,128)(2,1)S(1)} fusion(bf16[4,104768]{1,0:T(4,128)(2,1)S(1)} %copy-done.25, bf16[4,104832]{1,0:T(4,128)(2,1)S(1)} %copy-done.27, bf16[4,104832]{1,0:T(4,128)(2,1)S(1)} %copy-done.26, pred[4]{0:T(512)(128)(4,1)S(1)} %copy-done.35), kind=kLoop, calls=%fused_computation.236 | loop fusion | flops 8804096 | bytes 5030916 | tf_op jit(solution)/shard_map/jit(_take)/select_n | solution.py:120
  563.2 16.5 %slice_reduce_fusion.3 = (bf16[314432]{0:T(1024)(128)(2,1)S(1)}, bf16[314432]{0:T(1024)(128)(2,1)}, bf16[314432]{0:T(1024)(128)(2,1)}, bf16[314432]{0:T(1024)(128)(2,1)}) fusion(bf16[4,314432]{1,0:T(4,128)(2,1)S(1)} %maximum_select_fusion.1), kind=kLoop, calls=%fused_computation.517 | loop fusion | bytes 5030912 | tf_op jit(solution)/shard_map/slice | solution.py:128
  592.2 12.7 %pad_maximum_fusion = f32[3,72,136,128]{3,2,1,0:T(8,128)} fusion(f32[3,72,4,128]{3,2,1,0:T(4,128)} %collective-permute-done.11, f32[3,4,128,128]{3,2,1,0:T(8,128)} %copy-done.28, f32[3,64,128,128]{3,2,1,0:T(8,128)} %copy-done.1, f32[3,4,128,128]{3,2,1,0:T(8,128)S(1)} %collective-permute-done.8, f32[3,72,4,128]{3,2,1,0:T(4,128)} %collective-permute-done.10), kind=kLoop, calls=%fused_computation.26 | loop fusion | flops 15040512 | bytes 30081024 | tf_op jit(solution)/shard_map/concatenate | solution.py:23
  604.9 47.7 %fusion.10 = f32[3,64,136,128]{3,2,1,0:T(8,128)} fusion(f32[3,72,136,128]{3,2,1,0:T(8,128)} %pad_maximum_fusion, f32[]{:T(128)} %bitcast.23, f32[]{:T(128)} %bitcast.22, f32[]{:T(128)} %bitcast.21, f32[]{:T(128)} %bitcast.20, f32[]{:T(128)} %bitcast.19, f32[]{:T(128)} %bitcast.18, f32[]{:T(128)} %bitcast.17, f32[]{:T(128)} %bitcast.16, f32[]{:T(128)} %bitcast), kind=kLoop, calls=%fused_computation.48 | loop fusion | flops 56819712 | bytes 133693472 | tf_op jit(solution)/shard_map/add | solution.py:64
  652.6 54.0 %fusion.58 = f32[3,64,128,128]{3,2,1,0:T(8,128)} fusion(f32[3,64,136,128]{3,2,1,0:T(8,128)} %fusion.10, f32[]{:T(128)} %bitcast.23, f32[]{:T(128)} %bitcast.22, f32[]{:T(128)} %bitcast.21, f32[]{:T(128)} %bitcast.20, f32[]{:T(128)} %bitcast.19, f32[]{:T(128)} %bitcast.18, f32[]{:T(128)} %bitcast.17, f32[]{:T(128)} %bitcast.16, f32[]{:T(128)} %bitcast), kind=kLoop, calls=%fused_computation.114 | loop fusion | flops 53477376 | bytes 125829152 | tf_op jit(solution)/shard_map/add | solution.py:64
  706.6 50.2 %fusion.26 = f32[3,64,128,128]{3,2,1,0:T(8,128)} fusion(f32[3,64,128,128]{3,2,1,0:T(8,128)} %fusion.58, f32[]{:T(128)} %bitcast.23, f32[]{:T(128)} %bitcast.22, f32[]{:T(128)} %bitcast.21, f32[]{:T(128)} %bitcast.20, f32[]{:T(128)} %bitcast.19, f32[]{:T(128)} %bitcast.18, f32[]{:T(128)} %bitcast.17, f32[]{:T(128)} %bitcast.16, f32[]{:T(128)} %bitcast), kind=kLoop, calls=%fused_computation.72 | loop fusion | flops 53477376 | bytes 25165860 | tf_op jit(solution)/shard_map/add | solution.py:64
  756.7 39.8 %fusion.129 = f32[64,64,64]{2,1,0:T(8,128)S(1)} fusion(f32[3,64,128,128]{3,2,1,0:T(8,128)} %fusion.26, bf16[68,68,68]{2,1,0:T(8,128)(2,1)} %squeeze.55), kind=kLoop, calls=%fused_computation.299 | loop fusion | flops 39059456 | bytes 18350080 | tf_op jit(solution)/shard_map/add | solution.py:50
  796.6 15.3 %fusion.181 = f32[64,64,64]{2,1,0:T(8,128)S(1)} fusion(f32[3,64,128,128]{3,2,1,0:T(8,128)S(1)} %copy-done.2, bf16[68,68,68]{2,1,0:T(8,128)(2,1)S(1)} %squeeze.53), kind=kLoop, calls=%fused_computation.405 | loop fusion | flops 39059456 | bytes 18350080 | tf_op jit(solution)/shard_map/add | solution.py:50
  811.9 15.6 %fusion.103 = f32[64,64,64]{2,1,0:T(8,128)S(1)} fusion(f32[3,64,128,128]{3,2,1,0:T(8,128)S(1)} %copy-done.2, bf16[68,68,68]{2,1,0:T(8,128)(2,1)S(1)} %squeeze.56), kind=kLoop, calls=%fused_computation.246 | loop fusion | flops 39059456 | bytes 18350080 | tf_op jit(solution)/shard_map/add | solution.py:50
  827.5 15.7 %fusion.155 = f32[64,64,64]{2,1,0:T(8,128)S(1)} fusion(f32[3,64,128,128]{3,2,1,0:T(8,128)S(1)} %copy-done.2, bf16[68,68,68]{2,1,0:T(8,128)(2,1)S(1)} %copy-done), kind=kLoop, calls=%fused_computation.352 | loop fusion | flops 39059456 | bytes 18350080 | tf_op jit(solution)/shard_map/add | solution.py:50
  867.5 12.7 %select_maximum_fusion = f32[66,130,130]{2,1,0:T(8,128)} fusion(f32[66,1,128]{2,1,0:T(1,128)S(1)} %collective-permute-done.14, f32[66,1,128]{2,1,0:T(1,128)S(1)} %collective-permute-done.15, f32[1,128,128]{2,1,0:T(8,128)S(1)} %collective-permute-done.12, f32[1,128,128]{2,1,0:T(8,128)S(1)} %collective-permute-done.13, f32[64,64,64]{2,1,0:T(8,128)S(1)} %fusion.103, ...), kind=kLoop, calls=%fused_computation.139 | loop fusion | flops 20077200 | bytes 8854560 | tf_op jit(solution)/shard_map/concatenate | solution.py:23
  905.2 58.0 %divide_add_fusion = f32[3,64,128,128]{3,2,1,0:T(8,128)S(1)} fusion(f32[64,128,128]{2,1,0:T(8,128)} %add_add_fusion, f32[64,128,128]{2,1,0:T(8,128)} %get-tuple-element.13, f32[1,64,128,128]{3,2,1,0:T(8,128)} %fusion.73, f32[1,64,128,128]{3,2,1,0:T(8,128)} %fusion.76, f32[1,64,128,128]{3,2,1,0:T(8,128)} %copy-done.19, ...), kind=kLoop, calls=%fused_computation.133 | loop fusion | flops 78643200 | bytes 58720292 | tf_op jit(solution)/shard_map/add | solution.py:136
  968.6 32.7 %collective-permute-done.16 = f32[3,4,128,128]{3,2,1,0:T(8,128)S(1)} collective-permute-done((f32[3,4,128,128]{3,2,1,0:T(8,128)S(1)}, f32[3,4,128,128]{3,2,1,0:T(8,128)S(1)}, u32[]{:S(2)}, u32[]{:S(2)}) %collective-permute-start.16) | collective-permute-done | bytes 786464 | tf_op jit(solution)/shard_map/ppermute | solution.py:21
  1015.2 47.7 %fusion.2 = f32[3,64,136,128]{3,2,1,0:T(8,128)} fusion(f32[3,72,136,128]{3,2,1,0:T(8,128)} %pad_maximum_fusion.1, f32[]{:T(128)} %bitcast.23, f32[]{:T(128)} %bitcast.22, f32[]{:T(128)} %bitcast.21, f32[]{:T(128)} %bitcast.20, f32[]{:T(128)} %bitcast.19, f32[]{:T(128)} %bitcast.18, f32[]{:T(128)} %bitcast.17, f32[]{:T(128)} %bitcast.16, f32[]{:T(128)} %bitcast), kind=kLoop, calls=%fused_computation.31 | loop fusion | flops 56819712 | bytes 133693472 | tf_op jit(solution)/shard_map/add | solution.py:64
  1062.9 54.1 %fusion.50 = f32[3,64,128,128]{3,2,1,0:T(8,128)} fusion(f32[3,64,136,128]{3,2,1,0:T(8,128)} %fusion.2, f32[]{:T(128)} %bitcast.23, f32[]{:T(128)} %bitcast.22, f32[]{:T(128)} %bitcast.21, f32[]{:T(128)} %bitcast.20, f32[]{:T(128)} %bitcast.19, f32[]{:T(128)} %bitcast.18, f32[]{:T(128)} %bitcast.17, f32[]{:T(128)} %bitcast.16, f32[]{:T(128)} %bitcast), kind=kLoop, calls=%fused_computation.97 | loop fusion | flops 53477376 | bytes 125829152 | tf_op jit(solution)/shard_map/add | solution.py:64
  1117.0 50.7 %fusion.42 = f32[3,64,128,128]{3,2,1,0:T(8,128)} fusion(f32[3,64,128,128]{3,2,1,0:T(8,128)} %fusion.50, f32[]{:T(128)} %bitcast.23, f32[]{:T(128)} %bitcast.22, f32[]{:T(128)} %bitcast.21, f32[]{:T(128)} %bitcast.20, f32[]{:T(128)} %bitcast.19, f32[]{:T(128)} %bitcast.18, f32[]{:T(128)} %bitcast.17, f32[]{:T(128)} %bitcast.16, f32[]{:T(128)} %bitcast), kind=kLoop, calls=%fused_computation.88 | loop fusion | flops 53477376 | bytes 25165860 | tf_op jit(solution)/shard_map/add | solution.py:64
  (192 shorter events, 385.4 us)
Async XLA Ops:
  1.8 6.3 collective-permute-start
  4.9 6.6 collective-permute-start.1
  12.7 5.9 collective-permute-start.2
  14.0 4.9 collective-permute-start.3
  76.9 112.6 %all-to-all-start = ((bf16[8,2,157216]{2,1,0:T(2,128)(2,1)}), bf16[8,2,157216]{2,1,0:T(2,128)(2,1)}, u32[]{:S(2)}, u32[]{:S(2)}) async-start(bf16[8,2,157216]{2,1,0:T(2,128)(2,1)} %reshape.528), calls=%async_computation | async-start | bytes 10067968 | tf_op jit(solution)/shard_map/all_to_all | solution.py:112
  189.5 115.2 %all-to-all-start.1 = ((bf16[8,2,157216]{2,1,0:T(2,128)(2,1)}), bf16[8,2,157216]{2,1,0:T(2,128)(2,1)}, u32[]{:S(2)}, u32[]{:S(2)}) async-start(bf16[8,2,157216]{2,1,0:T(2,128)(2,1)} %reshape.530), calls=%async_computation.1 | async-start | bytes 10067968 | tf_op jit(solution)/shard_map/all_to_all | solution.py:112
  428.6 28.2 %collective-permute-start.5 = (f32[1,128,128]{2,1,0:T(8,128)S(1)}, f32[1,128,128]{2,1,0:T(8,128)S(1)}, u32[]{:S(2)}, u32[]{:S(2)}) collective-permute-start(f32[1,128,128]{2,1,0:T(8,128)S(1)} %get-tuple-element.41), channel_id=1, source_target_pairs={{0,2},{2,4},{4,6},{6,8},{8,10},{10,12},{12,14},{1,3},{3,5},{5,7},{... | collective-permute-start | bytes 196616 | tf_op jit(solution)/shard_map/ppermute | solution.py:21
  434.5 22.3 %collective-permute-start.4 = (f32[1,128,128]{2,1,0:T(8,128)S(1)}, f32[1,128,128]{2,1,0:T(8,128)S(1)}, u32[]{:S(2)}, u32[]{:S(2)}) collective-permute-start(f32[1,128,128]{2,1,0:T(8,128)S(1)} %get-tuple-element.42), channel_id=1, source_target_pairs={{2,0},{4,2},{6,4},{8,6},{10,8},{12,10},{14,12},{3,1},{5,3},{7,5},{... | collective-permute-start | bytes 196616 | tf_op jit(solution)/shard_map/ppermute | solution.py:22
  458.3 10.1 collective-permute-start.7
  459.9 8.6 collective-permute-start.6
  517.7 39.7 %copy-start.1 = (f32[3,64,128,128]{3,2,1,0:T(8,128)}, f32[3,64,128,128]{3,2,1,0:T(8,128)S(1)}, u32[]{:S(2)}) copy-start(f32[3,64,128,128]{3,2,1,0:T(8,128)S(1)} %multiply_divide_fusion) | copy-start | bytes 37748740
  517.9 38.3 %collective-permute-start.8 = (f32[3,4,128,128]{3,2,1,0:T(8,128)S(1)}, f32[3,4,128,128]{3,2,1,0:T(8,128)S(1)}, u32[]{:S(2)}, u32[]{:S(2)}) collective-permute-start(f32[3,4,128,128]{3,2,1,0:T(8,128)S(1)} %get-tuple-element.24), channel_id=1, source_target_pairs={{0,2},{2,4},{4,6},{6,8},{8,10},{10,12},{12,14},{1,3},{3,5},{5,7},{... | collective-permute-start | bytes 2359304 | tf_op jit(solution)/shard_map/ppermute | solution.py:21
  522.6 33.6 %collective-permute-start.9 = (f32[3,4,128,128]{3,2,1,0:T(8,128)S(1)}, f32[3,4,128,128]{3,2,1,0:T(8,128)S(1)}, u32[]{:S(2)}, u32[]{:S(2)}) collective-permute-start(f32[3,4,128,128]{3,2,1,0:T(8,128)S(1)} %get-tuple-element.25), channel_id=1, source_target_pairs={{2,0},{4,2},{6,4},{8,6},{10,8},{12,10},{14,12},{3,1},{5,3},{7,5},{... | collective-permute-start | bytes 2359304 | tf_op jit(solution)/shard_map/ppermute | solution.py:22
  557.3 34.8 %collective-permute-start.10 = (f32[3,72,4,128]{3,2,1,0:T(4,128)}, f32[3,72,4,128]{3,2,1,0:T(4,128)}, u32[]{:S(2)}, u32[]{:S(2)}) collective-permute-start(f32[3,72,4,128]{3,2,1,0:T(4,128)} %get-tuple-element.20), channel_id=1, source_target_pairs={{0,1},{2,3},{4,5},{6,7},{8,9},{10,11},{12,13},{14,15},{16,17},{18,... | collective-permute-start | bytes 1327112 | tf_op jit(solution)/shard_map/ppermute | solution.py:21
  558.6 33.6 %collective-permute-start.11 = (f32[3,72,4,128]{3,2,1,0:T(4,128)}, f32[3,72,4,128]{3,2,1,0:T(4,128)}, u32[]{:S(2)}, u32[]{:S(2)}) collective-permute-start(f32[3,72,4,128]{3,2,1,0:T(4,128)} %get-tuple-element.21), channel_id=1, source_target_pairs={{1,0},{3,2},{5,4},{7,6},{9,8},{11,10},{13,12},{15,14},{17,16},{19,... | collective-permute-start | bytes 1327112 | tf_op jit(solution)/shard_map/ppermute | solution.py:22
  756.7 39.8 %copy-start.2 = (f32[3,64,128,128]{3,2,1,0:T(8,128)S(1)}, f32[3,64,128,128]{3,2,1,0:T(8,128)}, u32[]{:S(2)}) copy-start(f32[3,64,128,128]{3,2,1,0:T(8,128)} %fusion.26) | copy-start | bytes 37748740
  847.5 7.4 collective-permute-start.13
  852.9 6.0 collective-permute-start.12
  859.1 8.3 collective-permute-start.15
  860.4 7.1 collective-permute-start.14
  963.3 38.0 %collective-permute-start.16 = (f32[3,4,128,128]{3,2,1,0:T(8,128)S(1)}, f32[3,4,128,128]{3,2,1,0:T(8,128)S(1)}, u32[]{:S(2)}, u32[]{:S(2)}) collective-permute-start(f32[3,4,128,128]{3,2,1,0:T(8,128)S(1)} %get-tuple-element.22), channel_id=1, source_target_pairs={{0,2},{2,4},{4,6},{6,8},{8,10},{10,12},{12,14},{1,3},{3,5},{5,7},{... | collective-permute-start | bytes 2359304 | tf_op jit(solution)/shard_map/ppermute | solution.py:21
  965.3 36.1 %collective-permute-start.17 = (f32[3,4,128,128]{3,2,1,0:T(8,128)S(1)}, f32[3,4,128,128]{3,2,1,0:T(8,128)S(1)}, u32[]{:S(2)}, u32[]{:S(2)}) collective-permute-start(f32[3,4,128,128]{3,2,1,0:T(8,128)S(1)} %get-tuple-element.23), channel_id=1, source_target_pairs={{2,0},{4,2},{6,4},{8,6},{10,8},{12,10},{14,12},{3,1},{5,3},{7,5},{... | collective-permute-start | bytes 2359304 | tf_op jit(solution)/shard_map/ppermute | solution.py:22
  1001.5 4.4 collective-permute-start.18
  1002.8 4.5 collective-permute-start.19
  (36 other events, 312.0 us)
where the time goes:
time: 1180 us; the launch traced here: 1170 us
  other arithmetic  688 us (58%)
  waiting for transfers between devices  195 us (17%)
  local copies, waits for them, and re-layouts  191 us (16%)
  starting transfers between devices  69.3 us (6%)
  matrix products  23.7 us (2%)
    add x6, other arithmetic, filter_padded(): result + kernel_taps[offset] * lax.slice_in_dim(padded, offset, offset +...  304 us
    all_to_all x2, waiting for transfers between devices, local(): lax.all_to_all(jnp.dot(selector, sources, preferred_element_type=jnp.floa...  145 us
    add x8, other arithmetic, warp_block(): result = result + weight * section.astype(jnp.float32)  127 us
    unnamed x82, local copies, waits for them, and re-layouts  71 us
    add x1, other arithmetic, local(): summed = field + mismatch * mean_grad / denominator  58 us
    concatenate x6, other arithmetic, with_halo(): value = jnp.concatenate([before, value, after], axis=dim)  46.6 us
    another operation x7, other arithmetic, central(): return jnp.stack([along_x, along_y, along_z])  45.8 us
    ppermute x10, waiting for transfers between devices, with_halo(): before = lax.ppermute(last, axis, up)  41.2 us
  transfers between devices with their start and end apart: 22, of which 9 were waited for; matrix products, arithmetic and copies ran while one was open for 13% of the time, Pallas kernels for 0%

commit v1 on v0

v1 whole, which is shorter than its diff:
```python
import functools

import jax
import jax.numpy as jnp
import numpy as np
from jax import lax
from jax.experimental import pallas as pl
from jax.experimental.pallas import tpu as pltpu
from jax.sharding import PartitionSpec as P

BLK = 64
RADIUS = 4
STIFF = 0.05
LANES = 128
CH = 8
LIMIT = 56 * 1024 * 1024
F32 = jnp.float32
BF16 = jnp.bfloat16


def taps():
    k = np.arange(-RADIUS, RADIUS + 1).astype(np.float32)
    w = np.exp(-k * k / np.float32(4.5)).astype(np.float32)
    return (w / np.sum(w)).astype(np.float32)


def band():
    w = taps()
    full = np.zeros((LANES, LANES), np.float32)
    for i in range(LANES):
        for k in range(-RADIUS, RADIUS + 1):
            if 0 <= i + k < LANES:
                full[i + k, i] = w[k + RADIUS]
    high = jnp.asarray(full).astype(BF16)
    low = (jnp.asarray(full) - high.astype(F32)).astype(BF16)
    row = jnp.concatenate([high, low], 1)
    return jnp.concatenate([row, row], 0)


def swap_halves(x):
    return pltpu.roll(x.astype(F32), 64, x.ndim - 1).astype(x.dtype)


def lane_of(shape):
    return lax.broadcasted_iota(jnp.int32, shape, len(shape) - 1)


class Table:
    def __init__(self, shape):
        self.shape = shape
        self.size = int(np.prod(shape))

    def at(self, t, d, b, c):
        _, n, yb, zb = self.shape
        return ((t * n + d) * yb + b) * zb + c

    def x(self, ref, t, d, b, c):
        return ref[self.at(t, d, b, c)]

    def z(self, ref, t, d, b, c):
        return ref[self.size + self.at(t, d, b, c)]

    def column(self, ref):
        return ref[2 * self.size]

    def row(self, ref):
        return ref[2 * self.size + 1]


def wanted_block(table, ref, t, d):
    a, g = table.column(ref), table.row(ref)
    blk_y, blk_z = jnp.int32(0), jnp.int32(0)
    for b in range(2):
        for c in range(2):
            hit = table.x(ref, t, d, g * 2 + b, c) == a
            blk_y = jnp.where(hit, b, blk_y)
            blk_z = jnp.where(hit, table.z(ref, t, d, g * 2 + b, c), blk_z)
    return blk_y, blk_z


def pack_body(table, t, shell, ref, mov, *refs):
    d = pl.program_id(0)
    blk_y, blk_z = wanted_block(table, ref, t, d)
    if shell:
        shells, out = refs
    else:
        (out,) = refs
    y0 = pl.multiple_of(blk_y * BLK, BLK)
    keep = (lane_of((BLK, LANES)) < 64) == (blk_z == 0)

    def step(x, carry):
        same = mov[x + 32 * blk_z, pl.ds(y0, BLK), :].astype(F32)
        other = mov[x + 32 * (1 - blk_z), pl.ds(y0, BLK), :].astype(F32)
        got = jnp.where(keep, same, pltpu.roll(other, 64, 1)).astype(BF16)
        out[0, pl.ds(pl.multiple_of(x * BLK, BLK), BLK), :] = got
        return carry

    lax.fori_loop(0, 32, step, 0, unroll=4)
    if shell:
        out[0, 2048:, :] = shells[blk_y * 2 + blk_z]


def pack(table, tab, t, moving, shells=None):
    n = table.shape[1]
    rows = 2048 if shells is None else 2048 + shells.shape[1]
    whole = lambda nd: (lambda d, r: (0,) * nd)
    specs = [pl.BlockSpec(moving.shape, whole(3))]
    args = [moving]
    if shells is not None:
        specs.append(pl.BlockSpec(shells.shape, whole(3)))
        args.append(shells)
    return pl.pallas_call(
        functools.partial(pack_body, table, t, shells is not None),
        out_shape=jax.ShapeDtypeStruct((n, rows, LANES), BF16),
        grid_spec=pltpu.PrefetchScalarGridSpec(
            num_scalar_prefetch=1,
            grid=(n,),
            in_specs=specs,
            out_specs=pl.BlockSpec((1, rows, LANES), lambda d, r: (d, 0, 0)),
        ),
        compiler_params=pltpu.CompilerParams(vmem_limit_bytes=LIMIT),
        cost_estimate=pl.CostEstimate(flops=n * rows * 512, bytes_accessed=n * rows * 256 + 2 * moving.size, transcendentals=0),
        name="pack%d" % t,
    )(tab, *args)


def pick_body(ref, p, q, out):
    low = lane_of((BLK, LANES)) < 64

    def step(x, carry):
        a = p[0, pl.ds(pl.multiple_of(x * BLK, BLK), BLK), :].astype(F32)
        b = q[0, pl.ds(pl.multiple_of(x * BLK, BLK), BLK), :].astype(F32)
        out[x] = jnp.where(low, a, pltpu.roll(b, 64, 1)).astype(BF16)
        out[x + 32] = jnp.where(low, pltpu.roll(a, 64, 1), b).astype(BF16)
        return carry

    lax.fori_loop(0, 32, step, 0, unroll=4)


def slot_spec(table, t, c, rows):
    def where(b, *rest):
        ref = rest[-1]
        return (table.x(ref, t, table.column(ref), table.row(ref) * 2 + b, c), 0, 0)

    return pl.BlockSpec((1, rows, LANES), where)


def pick(table, tab, t, slots, shape):
    rows = slots.shape[1]
    return pl.pallas_call(
        pick_body,
        out_shape=jax.ShapeDtypeStruct(shape, BF16),
        grid_spec=pltpu.PrefetchScalarGridSpec(
            num_scalar_prefetch=1,
            grid=(2,),
            in_specs=[slot_spec(table, t, 0, rows), slot_spec(table, t, 1, rows)],
            out_specs=pl.BlockSpec((64, BLK, LANES), lambda b, r: (0, b, 0)),
        ),
        compiler_params=pltpu.CompilerParams(vmem_limit_bytes=LIMIT),
        cost_estimate=pl.CostEstimate(flops=2 * 64 * 128 * 128, bytes_accessed=8 << 20, transcendentals=0),
        name="pick",
    )(tab, slots, slots)


XC = 16


def warp_body(table, t, ref, p, q, fixed, field, out, near, up, down, edge):
    b, chunk = pl.program_id(0), pl.program_id(1)

    @pl.when(chunk == 0)
    def _():
        low = lane_of((BLK, LANES)) < 64

        def both(rows, size):
            a = p[0, pl.ds(rows, size), :].astype(F32)
            c = q[0, pl.ds(rows, size), :].astype(F32)
            mask = low if size == BLK else lane_of((size, LANES)) < 64
            return (
                jnp.where(mask, a, pltpu.roll(c, 64, 1)),
                jnp.where(mask, pltpu.roll(a, 64, 1), c),
            )

        def step(x, carry):
            first, second = both(pl.multiple_of(x * BLK, BLK), BLK)
            near[x + 1, 8:72, :] = first
            near[x + 33, 8:72, :] = second
            return carry

        lax.fori_loop(0, 32, step, 0, unroll=2)
        first, second = both(2048, BLK)
        near[0, 8:72, :] = first
        near[65, 8:72, :] = second
        first, second = both(2112, 80)
        edge[0] = first
        edge[1] = second

        a, g = table.column(ref), table.row(ref)
        spot_p = jnp.where(table.z(ref, t, a, g * 2 + b, 0) == 0, 63, 0)
        spot_q = jnp.where(table.z(ref, t, a, g * 2 + b, 1) == 0, 127, 64)
        face_p = p[0, 2192:2272, :].astype(F32)
        face_q = q[0, 2192:2272, :].astype(F32)
        lane = lane_of((80, LANES))

        def widen(i, carry):
            near[i, 7:8, :] = edge[0, pl.ds(i, 1), :]
            near[i, 72:73, :] = edge[1, pl.ds(i, 1), :]
            value = near[i]
            at_p = pltpu.roll(face_p, lax.rem(spot_p - i + 256, 128), 1)
            at_q = pltpu.roll(face_q, lax.rem(spot_q - i + 256, 128), 1)
            fill = jnp.where(lane == spot_p, at_p, jnp.where(lane == spot_q, at_q, 0.0))
            up[i] = jnp.where((lane == 63) | (lane == 127), fill, pltpu.roll(value, 127, 1))
            down[i] = jnp.where((lane == 0) | (lane == 64), fill, pltpu.roll(value, 1, 1))
            return carry

        lax.fori_loop(0, 66, widen, 0)

    def plane(x, carry):
        xi = chunk * XC + x
        for tile in range(8):
            r = 8 * tile
            fx, fy, fz = field[0, x, r : r + 8, :], field[1, x, r : r + 8, :], field[2, x, r : r + 8, :]
            px, py, pz = fx > 0, fy > 0, fz > 0
            wx, wy, wz = jnp.abs(fx), jnp.abs(fy), jnp.abs(fz)
            per_x = []
            for kx in range(3):
                per_y = []
                for ky in range(3):
                    y0 = 7 + r + ky
                    here = near[xi + kx, y0 : y0 + 8, :]
                    beside = jnp.where(pz, up[xi + kx, y0 : y0 + 8, :], down[xi + kx, y0 : y0 + 8, :])
                    per_y.append((here, beside))
                far = [jnp.where(py, per_y[2][i], per_y[0][i]) for i in range(2)]
                per_x.append((per_y[1], far))
            corner = [
                [
                    per_x[1][j][i] if s == 0 else jnp.where(px, per_x[2][j][i], per_x[0][j][i])
                    for j in range(2)
                    for i in range(2)
                ]
                for s in range(2)
            ]
            lines = []
            for s in range(2):
                c00, c01, c10, c11 = corner[s]
                l0 = c00 + wz * (c01 - c00)
                l1 = c10 + wz * (c11 - c10)
                lines.append(l0 + wy * (l1 - l0))
            warped = lines[0] + wx * (lines[1] - lines[0])
            out[x, r : r + 8, :] = fixed[x, r : r + 8, :].astype(F32) - warped
        return carry

    lax.fori_loop(0, XC, plane, 0)


def warp(table, tab, t, slots, fixed, field):
    rows = slots.shape[1]
    tile_x, tile_y, tile_z = fixed.shape

    block = pl.BlockSpec((XC, BLK, LANES), lambda b, c, r: (c, b, 0))
    return pl.pallas_call(
        functools.partial(warp_body, table, t),
        out_shape=jax.ShapeDtypeStruct(fixed.shape, F32),
        grid_spec=pltpu.PrefetchScalarGridSpec(
            num_scalar_prefetch=1,
            grid=(2, tile_x // XC),
            in_specs=[
                slot_spec(table, t, 0, rows),
                slot_spec(table, t, 1, rows),
                block,
                pl.BlockSpec((3, XC, BLK, LANES), lambda b, c, r: (0, c, b, 0)),
            ],
            out_specs=block,
            scratch_shapes=[pltpu.VMEM((66, 80, LANES), F32)] * 3 + [pltpu.VMEM((2, 80, LANES), F32)],
        ),
        compiler_params=pltpu.CompilerParams(vmem_limit_bytes=LIMIT),
        cost_estimate=pl.CostEstimate(flops=60 << 20, bytes_accessed=22 << 20, transcendentals=0),
        name="warp",
    )(tab, slots, slots, fixed, field)


def put_planes(is_warped, g, count, start, total, diff, value, value_y, fixed, fixed_y):
    def step(i, carry):
        f, v = fixed[i].astype(F32), value[i].astype(F32)
        fy, vy = fixed_y[i].astype(F32), value_y[i].astype(F32)
        fy = jnp.where(g == 1, fy[8:16], fy[0:8])
        if vy.shape[0] == 16:
            vy = jnp.where(g == 1, vy[8:16], vy[0:8])
        if is_warped:
            s, m, sy, my = f + v, f - v, fy + vy, fy - vy
        else:
            s, m, sy, my = 2.0 * f - v, v, 2.0 * fy - vy, vy
        zero = jnp.zeros_like(sy)
        j = start + i
        total[j, 16:144, :] = s
        diff[j, 16:144, :] = m
        total[j, 8:16, :] = jnp.where(g == 1, sy, zero)
        total[j, 144:152, :] = jnp.where(g == 0, sy, zero)
        diff[j, 8:16, :] = jnp.where(g == 1, my, zero)
        diff[j, 144:152, :] = jnp.where(g == 0, my, zero)
        return carry

    lax.fori_loop(0, count, step, 0)


def update_planes(g, count, base, start, total, diff, summed, prior, prior_y, source):
    lane = lane_of((8, LANES))

    def step(i, carry):
        j = start + i
        for t in range(18):
            r = 8 + 8 * t
            here = total[j, r : r + 8, :]
            gx = total[j + 1, r : r + 8, :] - total[j - 1, r : r + 8, :]
            gy = total[j, r + 1 : r + 9, :] - total[j, r - 1 : r + 7, :]
            gz = jnp.where(lane < LANES - 1, pltpu.roll(here, LANES - 1, 1), 0.0) - jnp.where(
                lane > 0, pltpu.roll(here, 1, 1), 0.0
            )
            m = diff[j, r : r + 8, :]
            size = (gx * gx + gy * gy) + (gz * gz + (16.0 * m * m + 16.0 * STIFF))
            inv = pl.reciprocal(size, approx=True)
            inv = inv * (2.0 - size * inv)
            scale = (4.0 * m) * inv
            for c, grad in enumerate((gx, gy, gz)):
                value = scale * grad
                if prior is not None:
                    if 1 <= t <= 16:
                        value = value + prior[c, source + i, 8 * t - 8 : 8 * t, :]
                    else:
                        own = (g == 1) if t == 0 else (g == 0)
                        value = value + jnp.where(own, prior_y[c, source + i, 0:8, :], 0.0)
                summed[c, base + i, r - 8 : r, :] = value
        return carry

    lax.fori_loop(0, count, step, 0)


def smooth_planes(before, after, summed, along, wide, weights, out):
    w = [float(v) for v in taps()]

    def tap_sum(values):
        acc = w[RADIUS] * values[RADIUS]
        for k in range(RADIUS):
            acc = acc + w[k] * (values[k] + values[2 * RADIUS - k])
        return acc

    def rows(t, carry):
        r = pl.ds(pl.multiple_of(8 * t, 8), 8)
        for c in range(3):
            planes = [summed[c, before + j, r, :] for j in range(CH)]
            planes += [summed[c, after + j, r, :] for j in range(CH)]
            for o in range(CH):
                along[c, o, r, :] = tap_sum(planes[o : o + 2 * RADIUS + 1])
        return carry

    lax.fori_loop(0, 18, rows, 0)

    def plane(o, carry):
        for c in range(3):
            for t in range(8):
                r = 16 * t + 4
                acc = tap_sum([along[c, o, r + k : r + k + 16, :] for k in range(2 * RADIUS + 1)])
                high = acc.astype(BF16)
                wide[c * 128 + 16 * t : c * 128 + 16 * t + 16, 0:LANES] = high
                wide[c * 128 + 16 * t : c * 128 + 16 * t + 16, LANES:] = (acc - high.astype(F32)).astype(BF16)
        got = jnp.dot(wide[...], weights[...], preferred_element_type=F32)
        for c in range(3):
            part = got[c * 128 : c * 128 + 128]
            out[c, o] = part[:, :LANES] + part[:, LANES:]
        return carry

    lax.fori_loop(0, CH, plane, 0)


def scratch(planes):
    return [
        pltpu.VMEM((planes, 160, LANES), F32),
        pltpu.VMEM((planes, 160, LANES), F32),
        pltpu.VMEM((3, 16, 144, LANES), F32),
        pltpu.VMEM((3, CH, 144, LANES), F32),
        pltpu.VMEM((384, 256), BF16),
    ]


def inner_body(table, is_warped, ref, weights, value, value_y, fixed, fixed_y, *refs):
    prior, prior_y = (None, None) if is_warped else refs[:2]
    out, total, diff, summed, along, wide = refs[0 if is_warped else 2 :]
    k = pl.program_id(0)
    g = table.row(ref)
    cur = lax.rem(k, 2) * CH
    put_planes(is_warped, g, CH + 2, 0, total, diff, value, value_y, fixed, fixed_y)
    update_planes(g, CH, cur, 1, total, diff, summed, prior, prior_y, 0)

    @pl.when(k > 0)
    def _():
        smooth_planes(CH - cur, cur, summed, along, wide, weights, out)


def inner(table, tab, weights, value, value_y, fixed, fixed_y, prior=None, prior_y=None):
    tile_x = fixed.shape[0]
    is_warped = prior is None

    def window(array, planes, first):
        dims = array.shape
        if len(dims) == 3:
            return pl.BlockSpec(
                (pl.Element(planes), pl.Element(dims[1]), pl.Element(dims[2])), lambda k, r: (k * CH + first, 0, 0)
            )
        return pl.BlockSpec(
            (pl.Element(dims[0]), pl.Element(planes), pl.Element(dims[2]), pl.Element(dims[3])),
            lambda k, r: (0, k * CH + first, 0, 0),
        )

    specs = [pl.BlockSpec(weights.shape, lambda k, r: (0, 0))]
    args = [weights]
    for array in (value, value_y, fixed, fixed_y):
        specs.append(window(array, CH + 2, 3))
        args.append(array)
    if not is_warped:
        for array in (prior, prior_y):
            specs.append(window(array, CH, 4))
            args.append(array)
    return pl.pallas_call(
        functools.partial(inner_body, table, is_warped),
        out_shape=jax.ShapeDtypeStruct((3,) + fixed.shape, F32),
        grid_spec=pltpu.PrefetchScalarGridSpec(
            num_scalar_prefetch=1,
            grid=(tile_x // CH - 1,),
            in_specs=specs,
            out_specs=pl.BlockSpec((3, CH) + fixed.shape[1:], lambda k, r: (0, jnp.maximum(k, 1), 0, 0)),
            scratch_shapes=scratch(CH + 2),
        ),
        compiler_params=pltpu.CompilerParams(vmem_limit_bytes=LIMIT),
        cost_estimate=pl.CostEstimate(flops=200 << 20, bytes_accessed=30 << 20, transcendentals=0),
        name="inner%d" % (not is_warped),
    )(tab, *args)


def rim_body(table, is_warped, ref, weights, value, value_y, fixed, fixed_y, *refs):
    halo = refs[:4]
    refs = refs[4:]
    if is_warped:
        prior = prior_y = None
    else:
        prior, prior_y, prior_low, prior_high = refs[:4]
        refs = refs[4:]
    _, out, total, diff, summed, along, wide = refs
    k = pl.program_id(0)
    g = table.row(ref)
    put_planes(is_warped, g, 13, 5 * (1 - k), total, diff, value, value_y, fixed, fixed_y)

    def side(at, value_x, fixed_x):
        v_main, v_y = value_x.at[:, :128, :], value_x.at[:, 128:, :]
        f_main, f_y = fixed_x.at[:, :128, :], fixed_x.at[:, 128:, :]
        put_planes(is_warped, g, 5, at, total, diff, v_main, v_y, f_main, f_y)

    @pl.when(k == 0)
    def _():
        side(0, halo[0], halo[2])

    @pl.when(k == 1)
    def _():
        side(13, halo[1], halo[3])

    if is_warped:
        update_planes(g, 16, 0, 1, total, diff, summed, None, None, 0)
    else:
        update_planes(g, 12, 4 * (1 - k), 1 + 4 * (1 - k), total, diff, summed, prior, prior_y, 0)

        def outside(at, prior_x):
            update_planes(
                g, 4, at, 1 + at, total, diff, summed, prior_x.at[:, :, :128, :], prior_x.at[:, :, 128:, :], 0
            )

        @pl.when(k == 0)
        def _():
            outside(0, prior_low)

        @pl.when(k == 1)
        def _():
            outside(12, prior_high)

    smooth_planes(0, CH, summed, along, wide, weights, out)


def rim(table, tab, weights, field, value, value_y, fixed, fixed_y, halo, prior=None, prior_y=None, prior_x=()):
    tile_x = fixed.shape[0]
    is_warped = prior is None

    def window(array, planes):
        dims = array.shape
        if len(dims) == 3:
            return pl.BlockSpec(
                (pl.Element(planes), pl.Element(dims[1]), pl.Element(dims[2])),
                lambda k, r: (k * (tile_x - planes), 0, 0),
            )
        return pl.BlockSpec(
            (pl.Element(dims[0]), pl.Element(planes), pl.Element(dims[2]), pl.Element(dims[3])),
            lambda k, r: (0, k * (tile_x - planes), 0, 0),
        )

    def whole(array):
        return pl.BlockSpec(array.shape, lambda k, r: (0,) * array.ndim)

    specs, args = [whole(weights)], [weights]
    for array in (value, value_y, fixed, fixed_y):
        specs.append(window(array, 13))
        args.append(array)
    for array in halo:
        specs.append(whole(array))
        args.append(array)
    if not is_warped:
        for array in (prior, prior_y):
            specs.append(window(array, 12))
            args.append(array)
        for array in prior_x:
            specs.append(whole(array))
            args.append(array)
    specs.append(pl.BlockSpec(memory_space=pl.ANY))
    args.append(field)
    last = tile_x // CH - 1
    return pl.pallas_call(
        functools.partial(rim_body, table, is_warped),
        out_shape=jax.ShapeDtypeStruct(field.shape, F32),
        grid_spec=pltpu.PrefetchScalarGridSpec(
            num_scalar_prefetch=1,
            grid=(2,),
            in_specs=specs,
            out_specs=pl.BlockSpec((3, CH) + fixed.shape[1:], lambda k, r: (0, k * last, 0, 0)),
            scratch_shapes=scratch(18),
        ),
        input_output_aliases={len(args): 0},
        compiler_params=pltpu.CompilerParams(vmem_limit_bytes=LIMIT),
        cost_estimate=pl.CostEstimate(flops=60 << 20, bytes_accessed=10 << 20, transcendentals=0),
        name="rim%d" % (not is_warped),
    )(tab, *args)


def swap_y(value, g, rows):
    length = value.shape[-2]
    first = lax.slice_in_dim(value, 0, rows, axis=value.ndim - 2)
    last = lax.slice_in_dim(value, length - rows, length, axis=value.ndim - 2)
    return lax.ppermute(jnp.where(g == 0, last, first), "gy", [(0, 1), (1, 0)])


def shift_x(value, value_y, width):
    size = lax.axis_size("gx")
    axis = value.ndim - 3
    length = value.shape[axis]
    up = [(i, i + 1) for i in range(size - 1)]
    down = [(j, i) for i, j in up]

    def part(start):
        return jnp.concatenate(
            [lax.slice_in_dim(v, start, start + width, axis=axis) for v in (value, value_y)], axis=value.ndim - 2
        )

    return lax.ppermute(part(length - width), "gx", up), lax.ppermute(part(0), "gx", down)


def shell_rows(moving, moving_y, low, high, g):
    last, first = moving_y.shape[1] - 1, 0

    def extend(main, rows_y):
        below = jnp.where(g == 1, rows_y[:, last : last + 1], 0)
        above = jnp.where(g == 0, rows_y[:, first : first + 1], 0)
        return jnp.concatenate([below, main, above], axis=1)

    planes = jnp.concatenate([low[:, :128], moving, high[:, :128]], axis=0)
    planes_y = jnp.concatenate([low[:, 128:], moving_y, high[:, 128:]], axis=0)
    ext = extend(planes, planes_y)
    faces = []
    for b in range(2):
        for c in range(2):
            z = slice(c * BLK, c * BLK + BLK)
            y = slice(b * BLK + 1, b * BLK + 1 + BLK)
            side_x = jnp.concatenate([ext[0, y, z], ext[65, y, z]], axis=1)
            side_y = jnp.concatenate([ext[:, b * BLK, z], ext[:, b * BLK + BLK + 1, z]], axis=1)
            side_z = ext[:, b * BLK : b * BLK + BLK + 2, BLK - c].T
            faces.append(
                jnp.concatenate(
                    [side_x, jnp.pad(side_y, ((0, 14), (0, 0))), jnp.pad(side_z, ((7, 7), (0, 62)))], axis=0
                )
            )
    return jnp.stack(faces)


def local(fixed, moving, source_x, source_z):
    g = lax.axis_index("gy")
    table = Table(source_x.shape)
    tab = jnp.concatenate(
        [
            source_x.reshape(-1),
            source_z.reshape(-1),
            jnp.stack([lax.axis_index("gx"), g]).astype(jnp.int32),
        ]
    )
    weights = band()

    def send(slots):
        return lax.all_to_all(slots, "gx", split_axis=0, concat_axis=0, tiled=True)

    slots0 = send(pack(table, tab, 0, moving))

    both = jnp.stack([fixed, moving])
    both_y = swap_y(both, g, 16)
    low, high = shift_x(both, both_y, 5)
    fixed_y = both_y[0]
    fixed_x = (low[0], high[0])
    shells = shell_rows(moving, both_y[1], low[1, 4:], high[1, :1], g)
    ready1 = pack(table, tab, 1, moving, shells)

    slots0, ready1 = lax.optimization_barrier((slots0, ready1))
    slots1 = send(ready1)

    warped = pick(table, tab, 0, slots0, fixed.shape)
    warped_y = swap_y(warped, g, 16)
    warped_x = shift_x(warped, warped_y, 5)
    field = inner(table, tab, weights, warped, warped_y, fixed, fixed_y)
    field = rim(table, tab, weights, field, warped, warped_y, fixed, fixed_y, (*warped_x, *fixed_x))
    field_y = swap_y(field, g, 8)
    field_x = shift_x(field, field_y, 4)

    mismatch = warp(table, tab, 1, slots1, fixed, field)
    mismatch_y = swap_y(mismatch, g, 8)
    mismatch_x = shift_x(mismatch, mismatch_y, 5)
    last = inner(table, tab, weights, mismatch, mismatch_y, fixed, fixed_y, field, field_y)
    last = rim(
        table, tab, weights, last, mismatch, mismatch_y, fixed, fixed_y, (*mismatch_x, *fixed_x), field, field_y, field_x
    )
    return (last, mismatch)


def solution(mesh):
    return jax.shard_map(
        local,
        mesh=mesh,
        in_specs=(
            P(("groups", "gx"), "gy", None),
            P(("groups", "gx"), "gy", None),
            P("groups", None, None, None),
            P("groups", None, None, None),
        ),
        out_specs=(P(None, ("groups", "gx"), "gy", None), P(("groups", "gx"), "gy", None)),
        check_vma=False,
    )
```

time: 1180 us -> 376 us (0.32)
  other arithmetic: 688 us -> 10.4 us
  local copies, waits for them, and re-layouts: 191 us -> 33.9 us
  Pallas kernels: 0 us -> 149 us
  waiting for transfers between devices: 195 us -> 93.7 us
  matrix products: 23.7 us -> 0 us
  starting transfers between devices: 69.3 us -> 84.3 us
    add x17 -> x0, other arithmetic: 500 us -> none  [the longest x6 304 us: filter_padded(): result + kernel_taps[offset] * lax.slice_in_dim(padded, offset, offset +...]
    pallas_call x0 -> x8, Pallas kernels: none -> 149 us  [the longest x2 64.3 us: inner(): pl.pallas_call(functools.partial(inner_body, table, is_warped), out_shape...]
    all_to_all x2, waiting for transfers between devices: 145 us -> 0.01 us  [send(): return lax.all_to_all(slots, 'gx', split_axis=0, concat_axis=0, tiled=True)]
    unnamed x82 -> x25, local copies, waits for them, and re-layouts: 71 us -> 13.1 us
    concatenate x6 -> x12, other arithmetic: 46.6 us -> 1.25 us  [the longest x1 0.67 us: local(): jnp.concatenate([source_x.reshape(-1), source_z.reshape(-1), jnp.stack([l...]
    another operation x7 -> x5, other arithmetic: 45.8 us -> 1.07 us  [shell_rows(): return jnp.stack(faces)]
    ppermute x20 -> x12, waiting for transfers between devices: 50.4 us -> 93.7 us  [the longest x4 64.1 us: shift_x(): lax.ppermute(part(length - width), 'gx', up)]
    gather x10 -> x0, local copies, waits for them, and re-layouts: 36.3 us -> none  [local(): jnp.take(incoming, wanted, axis=0)]
  transfers between devices with their start and end apart: 22 -> 14, of which waited for: 9 -> 6; matrix products, arithmetic and copies ran while one was open for 13% -> 10% of each run, Pallas kernels for 0% -> 33%
where the time goes in v1:
time: 376 us; the launch traced here: 372 us
  Pallas kernels  149 us (40%)
  waiting for transfers between devices  93.7 us (25%)
  starting transfers between devices  84.3 us (22%)
  local copies, waits for them, and re-layouts  33.9 us (9%)
  other arithmetic  10.4 us (3%)
    pallas_call x2, Pallas kernels, inner(): pl.pallas_call(functools.partial(inner_body, table, is_warped), out_shape...  64.3 us
    ppermute x4, waiting for transfers between devices, shift_x(): lax.ppermute(part(length - width), 'gx', up)  64.1 us
    ppermute x4, starting transfers between devices, shift_x(): lax.ppermute(part(0), 'gx', down)  35.9 us
    all_to_all x2, starting transfers between devices, send(): return lax.all_to_all(slots, 'gx', split_axis=0, concat_axis=0, tiled=True)  33.1 us
    pallas_call x1, Pallas kernels, warp(): pl.pallas_call(functools.partial(warp_body, table, t), out_shape=jax.Shap...  31.3 us
    pallas_call x2, Pallas kernels, rim(): pl.pallas_call(functools.partial(rim_body, table, is_warped), out_shape=j...  30.5 us
    ppermute x4, waiting for transfers between devices, shift_x(): lax.ppermute(part(0), 'gx', down)  27.7 us
    pallas_call x2, Pallas kernels, pack(): pl.pallas_call(functools.partial(pack_body, table, t, shells is not None)...  18.3 us
  transfers between devices with their start and end apart: 14, of which 6 were waited for; matrix products, arithmetic and copies ran while one was open for 10% of the time, Pallas kernels for 33%

profile of v1, /device:TPU:23, one launch (start us, length us, event | category | flops | bytes accessed | tf_op | source)
XLA Modules:
  0.0 372.2 jit_solution(1275802405850236001)
XLA Ops:
  3.2 9.1 %pack0.1 = bf16[8,2048,128]{2,1,0:T(8,128)(2,1)} custom-call(s32[258]{0:T(512)} %pad_add_fusion.ref, bf16[64,128,128]{2,1,0:T(8,128)(2,1)} %mov.3), custom_call_target="tpu_custom_call" | custom-call | flops 8388608 | bytes 6291456 | tf_op jit(solution)/shard_map/pack0/pallas_call | solution.py:112
  12.4 5.7 %all-to-all-start = ((bf16[8,2048,128]{2,1,0:T(8,128)(2,1)}), bf16[8,2048,128]{2,1,0:T(8,128)(2,1)}, u32[]{:S(2)}, u32[]{:S(2)}) async-start(bf16[8,2048,128]{2,1,0:T(8,128)(2,1)} %pack0.1), calls=%async_computation | async-start | bytes 8388608 | tf_op jit(solution)/shard_map/all_to_all | solution.py:601
  22.3 3.1 collective-permute-start.1
  25.4 8.8 %copy.79 = bf16[64,128,128]{0,1,2:T(8,128)(2,1)} copy(bf16[64,128,128]{2,1,0:T(8,128)(2,1)} %mov.3) | data formatting | bytes 4194304 | tf_op args[1]
  34.2 2.2 collective-permute-start.2
  37.1 44.4 %collective-permute-done.1 = bf16[2,5,144,128]{3,2,1,0:T(8,128)(2,1)S(1)} collective-permute-done((bf16[2,5,144,128]{3,2,1,0:T(8,128)(2,1)S(1)}, bf16[2,5,144,128]{3,2,1,0:T(8,128)(2,1)S(1)}, u32[]{:S(2)}, u32[]{:S(2)}) %collective-permute-start.1) | collective-permute-done | bytes 368672 | tf_op jit(solution)/shard_map/ppermute | solution.py:558
  81.5 13.2 %collective-permute-done.2 = bf16[2,5,144,128]{3,2,1,0:T(8,128)(2,1)S(1)} collective-permute-done((bf16[2,5,144,128]{3,2,1,0:T(8,128)(2,1)S(1)}, bf16[2,5,144,128]{3,2,1,0:T(8,128)(2,1)S(1)}, u32[]{:S(2)}, u32[]{:S(2)}) %collective-permute-start.2) | collective-permute-done | bytes 368672 | tf_op jit(solution)/shard_map/ppermute | solution.py:558
  95.4 6.8 %copy.80 = bf16[1,128,128]{0,1,2:T(8,128)(2,1)} copy(bf16[1,128,128]{2,1,0:T(8,128)(2,1)S(1)} %slice.247) | data formatting | bytes 65536 | tf_op jit(solution)/shard_map/slice | solution.py:569
  102.1 6.8 %copy.78 = bf16[1,128,128]{0,1,2:T(8,128)(2,1)} copy(bf16[1,128,128]{2,1,0:T(8,128)(2,1)S(1)} %slice.246) | data formatting | bytes 65536 | tf_op jit(solution)/shard_map/slice | solution.py:569
  108.9 2.1 pad_maximum_fusion.15
  114.1 9.1 %pack1.1 = bf16[8,2272,128]{2,1,0:T(8,128)(2,1)} custom-call(s32[258]{0:T(512)} %pad_add_fusion.ref, bf16[64,128,128]{2,1,0:T(8,128)(2,1)} %mov.3, bf16[4,224,128]{2,1,0:T(8,128)(2,1)} %pad_maximum_fusion.6.refs_0_), custom_call_target="tpu_custom_call" | custom-call | flops 9306112 | bytes 6750208 | tf_op jit(solution)/shard_map/pack1/pallas_call | solution.py:112
  123.2 27.4 %all-to-all-start.1 = ((bf16[8,2272,128]{2,1,0:T(8,128)(2,1)}), bf16[8,2272,128]{2,1,0:T(8,128)(2,1)}, u32[]{:S(2)}, u32[]{:S(2)}) async-start(bf16[8,2272,128]{2,1,0:T(8,128)(2,1)} %pack1.1), calls=%async_computation.1 | async-start | bytes 9306112 | tf_op jit(solution)/shard_map/all_to_all | solution.py:601
  150.6 4.6 %pick.1.value = bf16[64,128,128]{2,1,0:T(8,128)(2,1)} custom-call(s32[258]{0:T(512)} %pad_add_fusion.ref, bf16[8,2048,128]{2,1,0:T(8,128)(2,1)} %all-to-all-done.p.q, bf16[8,2048,128]{2,1,0:T(8,128)(2,1)} %all-to-all-done.p.q), custom_call_target="tpu_custom_call" | custom-call | flops 2097152 | bytes 8388608 | tf_op jit(solution)/shard_map/pick/pallas_call | solution.py:150
  159.2 3.1 collective-permute-start.4
  162.3 2.2 collective-permute-start.5
  165.2 31.6 %inner0.1.refs_4_ = f32[3,64,128,128]{3,2,1,0:T(8,128)} custom-call(s32[258]{0:T(512)} %pad_add_fusion.ref, bf16[256,256]{1,0:T(8,128)(2,1)} %constant.38.weights, bf16[64,128,128]{2,1,0:T(8,128)(2,1)} %pick.1.value, bf16[64,16,128]{2,1,0:T(8,128)(2,1)} %copy-done.4, bf16[64,128,128]{2,1,0:T(8,128)(2,1)} %fixed.9, bf16[64,16,128]{2,1,0:T(8,128)(2,1)} %get-tuple-element.26.fixed_y), custom_call_target="tpu_custom_call" | custom-call | flops 209715200 | bytes 31457280 | tf_op jit(solution)/shard_map/inner0/pallas_call | solution.py:423
  196.8 19.6 %collective-permute-done.4.refs_0_ = bf16[5,144,128]{2,1,0:T(8,128)(2,1)S(1)} collective-permute-done((bf16[5,144,128]{2,1,0:T(8,128)(2,1)S(1)}, bf16[5,144,128]{2,1,0:T(8,128)(2,1)S(1)}, u32[]{:S(2)}, u32[]{:S(2)}) %collective-permute-start.4) | collective-permute-done | bytes 184352 | tf_op jit(solution)/shard_map/ppermute | solution.py:558
  216.4 14.5 %collective-permute-done.5.refs_1_ = bf16[5,144,128]{2,1,0:T(8,128)(2,1)S(1)} collective-permute-done((bf16[5,144,128]{2,1,0:T(8,128)(2,1)S(1)}, bf16[5,144,128]{2,1,0:T(8,128)(2,1)S(1)}, u32[]{:S(2)}, u32[]{:S(2)}) %collective-permute-start.5) | collective-permute-done | bytes 184352 | tf_op jit(solution)/shard_map/ppermute | solution.py:558
  231.6 14.4 %rim0.1.field.refs_0_.refs_4_ = f32[3,64,128,128]{3,2,1,0:T(8,128)} custom-call(s32[258]{0:T(512)} %pad_add_fusion.ref, bf16[256,256]{1,0:T(8,128)(2,1)} %constant.38.weights, bf16[64,128,128]{2,1,0:T(8,128)(2,1)} %pick.1.value, bf16[64,16,128]{2,1,0:T(8,128)(2,1)} %copy-done.4, bf16[64,128,128]{2,1,0:T(8,128)(2,1)} %fixed.9, ...), custom_call_target="tpu_custom_call", output_to_operand_aliasing={{}: (10, {})} | custom-call | flops 62914560 | bytes 10485760 | tf_op jit(solution)/shard_map/rim0/pallas_call | solution.py:522
  253.1 31.3 %warp.1.value = f32[64,128,128]{2,1,0:T(8,128)} custom-call(s32[258]{0:T(512)} %pad_add_fusion.ref, bf16[8,2272,128]{2,1,0:T(8,128)(2,1)} %all-to-all-done.1.p.q, bf16[8,2272,128]{2,1,0:T(8,128)(2,1)} %all-to-all-done.1.p.q, bf16[64,128,128]{2,1,0:T(8,128)(2,1)} %fixed.9, f32[3,64,128,128]{3,2,1,0:T(8,128)} %rim0.1.field.refs_0_.refs_4_), custom_call_target="tpu_custom_call" | custom-call | flops 62914560 | bytes 23068672 | tf_op jit(solution)/shard_map/warp/pallas_call | solution.py:261
  286.6 27.0 %collective-permute-start.11 = (f32[3,4,136,128]{3,2,1,0:T(8,128)S(1)}, f32[3,4,136,128]{3,2,1,0:T(8,128)S(1)}, u32[]{:S(2)}, u32[]{:S(2)}) collective-permute-start(f32[3,4,136,128]{3,2,1,0:T(8,128)S(1)} %pad_maximum_fusion.1), channel_id=1, source_target_pairs={{2,0},{4,2},{6,4},{8,6},{10,8},{12,10},{14,12},{3,1},{5,3},{7,5},{... | collective-permute-start | bytes 2506760 | tf_op jit(solution)/shard_map/ppermute | solution.py:558
  316.8 4.5 %collective-permute-start.8 = (f32[5,136,128]{2,1,0:T(8,128)S(1)}, f32[5,136,128]{2,1,0:T(8,128)S(1)}, u32[]{:S(2)}, u32[]{:S(2)}) collective-permute-start(f32[5,136,128]{2,1,0:T(8,128)S(1)} %pad_maximum_fusion.5), channel_id=1, source_target_pairs={{2,0},{4,2},{6,4},{8,6},{10,8},{12,10},{14,12},{3,1},{5,3},{7,5},{... | collective-permute-start | bytes 1044488 | tf_op jit(solution)/shard_map/ppermute | solution.py:558
  321.4 32.7 %inner1.1.refs_8_ = f32[3,64,128,128]{3,2,1,0:T(8,128)} custom-call(s32[258]{0:T(512)} %pad_add_fusion.ref, bf16[256,256]{1,0:T(8,128)(2,1)} %constant.38.weights, f32[64,128,128]{2,1,0:T(8,128)} %warp.1.value, f32[64,8,128]{2,1,0:T(8,128)} %copy-done.3, bf16[64,128,128]{2,1,0:T(8,128)(2,1)} %fixed.9, bf16[64,16,128]{2,1,0:T(8,128)(2,1)} %get-tuple-element.26.fixed_y, ...), custom_call_target="tpu_custom_call" | custom-call | flops 209715200 | bytes 31457280 | tf_op jit(solution)/shard_map/inner1/pallas_call | solution.py:423
  356.1 16.1 %rim1.1 = f32[3,64,128,128]{3,2,1,0:T(8,128)} custom-call(s32[258]{0:T(512)} %pad_add_fusion.ref, bf16[256,256]{1,0:T(8,128)(2,1)} %constant.38.weights, f32[64,128,128]{2,1,0:T(8,128)} %warp.1.value, f32[64,8,128]{2,1,0:T(8,128)} %copy-done.3, bf16[64,128,128]{2,1,0:T(8,128)(2,1)} %fixed.9, ...), custom_call_target="tpu_custom_call", output_to_operand_aliasing={{}: (14, {})} | custom-call | flops 62914560 | bytes 10485760 | tf_op jit(solution)/shard_map/rim1/pallas_call | solution.py:522
  (94 shorter events, 30.9 us)
Async XLA Ops:
  12.4 5.7 %copy-start = (bf16[64,128,128]{2,1,0:T(8,128)(2,1)S(1)}, bf16[64,128,128]{2,1,0:T(8,128)(2,1)}, u32[]{:S(2)}) copy-start(bf16[64,128,128]{2,1,0:T(8,128)(2,1)} %fixed.9) | copy-start | bytes 6291460
  12.4 110.8 %all-to-all-start = ((bf16[8,2048,128]{2,1,0:T(8,128)(2,1)}), bf16[8,2048,128]{2,1,0:T(8,128)(2,1)}, u32[]{:S(2)}, u32[]{:S(2)}) async-start(bf16[8,2048,128]{2,1,0:T(8,128)(2,1)} %pack0.1), calls=%async_computation | async-start | bytes 8388608 | tf_op jit(solution)/shard_map/all_to_all | solution.py:601
  18.1 4.2 %copy-start.1 = (bf16[64,128,128]{2,1,0:T(8,128)(2,1)S(1)}, bf16[64,128,128]{2,1,0:T(8,128)(2,1)}, u32[]{:S(2)}) copy-start(bf16[64,128,128]{2,1,0:T(8,128)(2,1)} %mov.3) | copy-start | bytes 6291460
  19.4 2.8 collective-permute-start
  22.3 59.2 %collective-permute-start.1 = (bf16[2,5,144,128]{3,2,1,0:T(8,128)(2,1)S(1)}, bf16[2,5,144,128]{3,2,1,0:T(8,128)(2,1)S(1)}, u32[]{:S(2)}, u32[]{:S(2)}) collective-permute-start(bf16[2,5,144,128]{3,2,1,0:T(8,128)(2,1)S(1)} %get-tuple-element.20), channel_id=1, source_target_pairs={{0,2},{2,4},{4,6},{6,8},{8,10},{10,12},{12,14},{1,3},{3,5},{5,7},{... | collective-permute-start | bytes 1105928 | tf_op jit(solution)/shard_map/ppermute | solution.py:558
  34.2 60.5 %collective-permute-start.2 = (bf16[2,5,144,128]{3,2,1,0:T(8,128)(2,1)S(1)}, bf16[2,5,144,128]{3,2,1,0:T(8,128)(2,1)S(1)}, u32[]{:S(2)}, u32[]{:S(2)}) collective-permute-start(bf16[2,5,144,128]{3,2,1,0:T(8,128)(2,1)S(1)} %get-tuple-element.21), channel_id=1, source_target_pairs={{2,0},{4,2},{6,4},{8,6},{10,8},{12,10},{14,12},{3,1},{5,3},{7,5},{... | collective-permute-start | bytes 1105928 | tf_op jit(solution)/shard_map/ppermute | solution.py:558
  123.2 129.9 %all-to-all-start.1 = ((bf16[8,2272,128]{2,1,0:T(8,128)(2,1)}), bf16[8,2272,128]{2,1,0:T(8,128)(2,1)}, u32[]{:S(2)}, u32[]{:S(2)}) async-start(bf16[8,2272,128]{2,1,0:T(8,128)(2,1)} %pack1.1), calls=%async_computation.1 | async-start | bytes 9306112 | tf_op jit(solution)/shard_map/all_to_all | solution.py:601
  156.3 2.8 collective-permute-start.3
  159.1 6.1 %copy-start.4 = (bf16[64,16,128]{2,1,0:T(8,128)(2,1)}, bf16[64,16,128]{2,1,0:T(8,128)(2,1)S(1)}, u32[]{:S(2)}) copy-start(bf16[64,16,128]{2,1,0:T(8,128)(2,1)S(1)} %collective-permute-done.3.value_y) | copy-start | bytes 786436
  159.2 57.3 %collective-permute-start.4 = (bf16[5,144,128]{2,1,0:T(8,128)(2,1)S(1)}, bf16[5,144,128]{2,1,0:T(8,128)(2,1)S(1)}, u32[]{:S(2)}, u32[]{:S(2)}) collective-permute-start(bf16[5,144,128]{2,1,0:T(8,128)(2,1)S(1)} %pad_maximum_fusion.7), channel_id=1, source_target_pairs={{0,2},{2,4},{4,6},{6,8},{8,10},{10,12},{12,14},{1,3},{3,5},{5,7},{... | collective-permute-start | bytes 552968 | tf_op jit(solution)/shard_map/ppermute | solution.py:558
  162.3 68.6 %collective-permute-start.5 = (bf16[5,144,128]{2,1,0:T(8,128)(2,1)S(1)}, bf16[5,144,128]{2,1,0:T(8,128)(2,1)S(1)}, u32[]{:S(2)}, u32[]{:S(2)}) collective-permute-start(bf16[5,144,128]{2,1,0:T(8,128)(2,1)S(1)} %pad_maximum_fusion.8), channel_id=1, source_target_pairs={{2,0},{4,2},{6,4},{8,6},{10,8},{12,10},{14,12},{3,1},{5,3},{7,5},{... | collective-permute-start | bytes 552968 | tf_op jit(solution)/shard_map/ppermute | solution.py:558
  216.4 14.5 %copy-start.9 = (bf16[5,144,128]{2,1,0:T(8,128)(2,1)}, bf16[5,144,128]{2,1,0:T(8,128)(2,1)S(1)}, u32[]{:S(2)}) copy-start(bf16[5,144,128]{2,1,0:T(8,128)(2,1)S(1)} %collective-permute-done.4.refs_0_) | copy-start | bytes 552964
  247.4 3.6 collective-permute-start.9
  251.1 33.3 %copy-start.2 = (f32[3,64,8,128]{3,2,1,0:T(8,128)}, f32[3,64,8,128]{3,2,1,0:T(8,128)S(1)}, u32[]{:S(2)}) copy-start(f32[3,64,8,128]{3,2,1,0:T(8,128)S(1)} %collective-permute-done.9.refs_1_.refs_5_) | copy-start | bytes 2359300
  251.1 102.9 %collective-permute-start.10 = (f32[3,4,136,128]{3,2,1,0:T(8,128)S(1)}, f32[3,4,136,128]{3,2,1,0:T(8,128)S(1)}, u32[]{:S(2)}, u32[]{:S(2)}) collective-permute-start(f32[3,4,136,128]{3,2,1,0:T(8,128)S(1)} %pad_maximum_fusion), channel_id=1, source_target_pairs={{0,2},{2,4},{4,6},{6,8},{8,10},{10,12},{12,14},{1,3},{3,5},{5,7},{... | collective-permute-start | bytes 2506760 | tf_op jit(solution)/shard_map/ppermute | solution.py:558
  285.5 29.3 %collective-permute-start.6 = (f32[64,8,128]{2,1,0:T(8,128)S(1)}, f32[64,8,128]{2,1,0:T(8,128)S(1)}, u32[]{:S(2)}, u32[]{:S(2)}) collective-permute-start(f32[64,8,128]{2,1,0:T(8,128)S(1)} %slice_select_fusion.1), channel_id=1, source_target_pairs={{0,1},{1,0},{2,3},{3,2},{4,5},{5,4},{6,7},{7,6},{8,9},{9,8},{10,11... | collective-permute-start | bytes 786440 | tf_op jit(solution)/shard_map/ppermute | solution.py:543
  286.6 67.4 %collective-permute-start.11 = (f32[3,4,136,128]{3,2,1,0:T(8,128)S(1)}, f32[3,4,136,128]{3,2,1,0:T(8,128)S(1)}, u32[]{:S(2)}, u32[]{:S(2)}) collective-permute-start(f32[3,4,136,128]{3,2,1,0:T(8,128)S(1)} %pad_maximum_fusion.1), channel_id=1, source_target_pairs={{2,0},{4,2},{6,4},{8,6},{10,8},{12,10},{14,12},{3,1},{5,3},{7,5},{... | collective-permute-start | bytes 2506760 | tf_op jit(solution)/shard_map/ppermute | solution.py:558
  314.8 6.6 %copy-start.3 = (f32[64,8,128]{2,1,0:T(8,128)}, f32[64,8,128]{2,1,0:T(8,128)S(1)}, u32[]{:S(2)}) copy-start(f32[64,8,128]{2,1,0:T(8,128)S(1)} %collective-permute-done.6.value_y) | copy-start | bytes 786436
  314.8 39.2 %collective-permute-start.7 = (f32[5,136,128]{2,1,0:T(8,128)S(1)}, f32[5,136,128]{2,1,0:T(8,128)S(1)}, u32[]{:S(2)}, u32[]{:S(2)}) collective-permute-start(f32[5,136,128]{2,1,0:T(8,128)S(1)} %pad_maximum_fusion.4), channel_id=1, source_target_pairs={{0,2},{2,4},{4,6},{6,8},{8,10},{10,12},{12,14},{1,3},{3,5},{5,7},{... | collective-permute-start | bytes 1044488 | tf_op jit(solution)/shard_map/ppermute | solution.py:558
  316.8 37.3 %collective-permute-start.8 = (f32[5,136,128]{2,1,0:T(8,128)S(1)}, f32[5,136,128]{2,1,0:T(8,128)S(1)}, u32[]{:S(2)}, u32[]{:S(2)}) collective-permute-start(f32[5,136,128]{2,1,0:T(8,128)S(1)} %pad_maximum_fusion.5), channel_id=1, source_target_pairs={{2,0},{4,2},{6,4},{8,6},{10,8},{12,10},{14,12},{3,1},{5,3},{7,5},{... | collective-permute-start | bytes 1044488 | tf_op jit(solution)/shard_map/ppermute | solution.py:558
  354.0 0.9 copy-start.5
  354.1 1.2 copy-start.6
  354.1 1.3 copy-start.7
  355.3 0.7 copy-start.8
  (1 other events, 0.7 us)

commit v2 on v1

--- a/solution.py
+++ b/solution.py
@@ -13,6 +13,7 @@
 STIFF = 0.05
 LANES = 128
 CH = 8
+SMALL = pl.CostEstimate(flops=1 << 16, bytes_accessed=1 << 16, transcendentals=0)
 LIMIT = 56 * 1024 * 1024
 F32 = jnp.float32
 BF16 = jnp.bfloat16
@@ -37,10 +38,6 @@
     return jnp.concatenate([row, row], 0)
 
 
-def swap_halves(x):
-    return pltpu.roll(x.astype(F32), 64, x.ndim - 1).astype(x.dtype)
-
-
 def lane_of(shape):
     return lax.broadcasted_iota(jnp.int32, shape, len(shape) - 1)
 
@@ -67,196 +64,281 @@
         return ref[2 * self.size + 1]
 
 
-def wanted_block(table, ref, t, d):
-    a, g = table.column(ref), table.row(ref)
-    blk_y, blk_z = jnp.int32(0), jnp.int32(0)
+def wanted_block(table, ref, t, d, column):
+    g = table.row(ref)
+    blk_y, blk_z, out_z = jnp.int32(0), jnp.int32(0), jnp.int32(0)
     for b in range(2):
         for c in range(2):
-            hit = table.x(ref, t, d, g * 2 + b, c) == a
+            hit = table.x(ref, t, d, g * 2 + b, c) == column
             blk_y = jnp.where(hit, b, blk_y)
             blk_z = jnp.where(hit, table.z(ref, t, d, g * 2 + b, c), blk_z)
-    return blk_y, blk_z
-
-
-def pack_body(table, t, shell, ref, mov, *refs):
-    d = pl.program_id(0)
-    blk_y, blk_z = wanted_block(table, ref, t, d)
+            out_z = jnp.where(hit, c, out_z)
+    return blk_y, blk_z, out_z
+
+
+MAIN = 32 * BLK
+GROUP = 8
+PART = 32
+
+
+def pack_body(table, t, far, count, shell, ref, *refs):
+    n = table.shape[1]
+    half = n // 2
+    a = table.column(ref)
+    here = (a >= half).astype(jnp.int32)
+    column = a if not far else jnp.where(a >= half, a - half, a + half)
+    blk_y, blk_z, out_z = wanted_block(table, ref, t, here * half + pl.program_id(0), column)
+    parts, out = refs[:count], refs[-1]
     if shell:
-        shells, out = refs
-    else:
-        (out,) = refs
+        out = out.at[0]
     y0 = pl.multiple_of(blk_y * BLK, BLK)
-    keep = (lane_of((BLK, LANES)) < 64) == (blk_z == 0)
-
-    def step(x, carry):
-        same = mov[x + 32 * blk_z, pl.ds(y0, BLK), :].astype(F32)
-        other = mov[x + 32 * (1 - blk_z), pl.ds(y0, BLK), :].astype(F32)
-        got = jnp.where(keep, same, pltpu.roll(other, 64, 1)).astype(BF16)
-        out[0, pl.ds(pl.multiple_of(x * BLK, BLK), BLK), :] = got
+    keep = (lane_of((GROUP, BLK, LANES)) < 64) == (blk_z == 0)
+    turn = jnp.where(blk_z == out_z, 0, PART // 2)
+    for k, mov in enumerate(parts):
+        for x in range(0, PART // 2, GROUP):
+            same = mov[pl.ds(x + turn, GROUP), pl.ds(y0, BLK), :]
+            other = mov[pl.ds(x + PART // 2 - turn, GROUP), pl.ds(y0, BLK), :]
+            other = pltpu.roll(other.reshape(GROUP * BLK, LANES), 64, 1).reshape(GROUP, BLK, LANES)
+            got = jnp.where(keep, same.astype(F32), other.astype(F32)).astype(BF16)
+            row = (k * PART // 2 + x) * BLK
+            out[0, row : row + GROUP * BLK, :] = got.reshape(GROUP * BLK, LANES)
+    if shell:
+        out[0, MAIN:, :] = refs[count][blk_y * 2 + blk_z]
+
+
+def pack(table, tab, t, far, parts, shells=None, into=None):
+    half = table.shape[1] // 2
+    args, specs = [], []
+    for part in parts:
+        for i in range(part.shape[0] // PART):
+            args.append(part)
+            specs.append(pl.BlockSpec((PART,) + part.shape[1:], lambda d, r, i=i: (i, 0, 0)))
+    count = len(args)
+    rows = count * PART // 2 * BLK
+    shape = (half, rows, LANES)
+    out_spec = pl.BlockSpec((1, rows, LANES), lambda d, r: (d, 0, 0))
+    aliases = {}
+    if shells is not None:
+        rows = rows + shells.shape[1]
+        shape = (half, 2, rows, LANES)
+        args.append(shells)
+        specs.append(pl.BlockSpec(shells.shape, lambda d, r: (0, 0, 0)))
+        out_spec = pl.BlockSpec((1, 1, rows, LANES), lambda d, r: (d, int(far), 0, 0))
+    if into is not None:
+        aliases = {1 + len(args): 0}
+        args.append(into)
+        specs.append(pl.BlockSpec(memory_space=pl.ANY))
+    return pl.pallas_call(
+        functools.partial(pack_body, table, t, far, count, shells is not None),
+        out_shape=jax.ShapeDtypeStruct(shape, BF16),
+        grid_spec=pltpu.PrefetchScalarGridSpec(
+            num_scalar_prefetch=1, grid=(half,), in_specs=specs, out_specs=out_spec
+        ),
+        input_output_aliases=aliases,
+        compiler_params=pltpu.CompilerParams(vmem_limit_bytes=LIMIT),
+        cost_estimate=SMALL,
+        name="pack%d%s" % (t, "far" if far else "own"),
+    )(tab, *args)
+
+
+def fetch(table, t, ref, own, far, slots, sems):
+    n = table.shape[1]
+    half = n // 2
+    a, g = table.column(ref), table.row(ref)
+    for b in range(2):
+        for c in range(2):
+            source = table.x(ref, t, a, g * 2 + b, c)
+            near = (source >= half) == (a >= half)
+            index = jnp.where(source >= half, source - half, source)
+            k = 2 * b + c
+
+            @pl.when(near)
+            def _():
+                pltpu.make_async_copy(own(index), slots.at[k], sems.at[k]).start()
+
+            @pl.when(jnp.logical_not(near))
+            def _():
+                start = 0
+                for array in far(index):
+                    piece = slots.at[k, start : start + array.shape[0]]
+                    pltpu.make_async_copy(array, piece, sems.at[k]).start()
+                    start += array.shape[0]
+
+
+def await_slot(own, slots, sems, k):
+    pltpu.make_async_copy(own(0), slots.at[k], sems.at[k]).wait()
+
+
+def main_rows(p, q, put_first, put_second):
+    low = lane_of((GROUP * BLK, LANES)) < 64
+
+    def step(i, carry):
+        row = i * GROUP
+        rows = pl.ds(pl.multiple_of(row * BLK, GROUP * BLK), GROUP * BLK)
+        u, v = p[rows, :].astype(F32), q[rows, :].astype(F32)
+        x = row + lax.div(row, PART // 2) * (PART // 2)
+        put_first(x, jnp.where(low, u, v).reshape(GROUP, BLK, LANES))
+        second = pltpu.roll(jnp.where(low, v, u).astype(BF16), 64, 1)
+        put_second(x + PART // 2, second.reshape(GROUP, BLK, LANES))
         return carry
 
-    lax.fori_loop(0, 32, step, 0, unroll=4)
-    if shell:
-        out[0, 2048:, :] = shells[blk_y * 2 + blk_z]
-
-
-def pack(table, tab, t, moving, shells=None):
-    n = table.shape[1]
-    rows = 2048 if shells is None else 2048 + shells.shape[1]
-    whole = lambda nd: (lambda d, r: (0,) * nd)
-    specs = [pl.BlockSpec(moving.shape, whole(3))]
-    args = [moving]
-    if shells is not None:
-        specs.append(pl.BlockSpec(shells.shape, whole(3)))
-        args.append(shells)
+    lax.fori_loop(0, 32 // GROUP, step, 0)
+
+
+def pick_body(table, t, ref, own_ref, far_a, far_b, out, slots, sems):
+    b = pl.program_id(0)
+    own, far = lambda i: own_ref.at[i], lambda i: [far_a.at[i], far_b.at[i]]
+
+    @pl.when(b == 0)
+    def _():
+        fetch(table, t, ref, own, far, slots, sems)
+
+    await_slot(own, slots, sems, 2 * b)
+    await_slot(own, slots, sems, 2 * b + 1)
+
+    def put(x, value):
+        out[pl.ds(x, GROUP)] = value.astype(BF16)
+
+    main_rows(slots.at[2 * b], slots.at[2 * b + 1], put, put)
+
+
+def pick(table, tab, t, own, far, shape):
+    rows = own.shape[1]
     return pl.pallas_call(
-        functools.partial(pack_body, table, t, shells is not None),
-        out_shape=jax.ShapeDtypeStruct((n, rows, LANES), BF16),
-        grid_spec=pltpu.PrefetchScalarGridSpec(
-            num_scalar_prefetch=1,
-            grid=(n,),
-            in_specs=specs,
-            out_specs=pl.BlockSpec((1, rows, LANES), lambda d, r: (d, 0, 0)),
-        ),
-        compiler_params=pltpu.CompilerParams(vmem_limit_bytes=LIMIT),
-        cost_estimate=pl.CostEstimate(flops=n * rows * 512, bytes_accessed=n * rows * 256 + 2 * moving.size, transcendentals=0),
-        name="pack%d" % t,
-    )(tab, *args)
-
-
-def pick_body(ref, p, q, out):
-    low = lane_of((BLK, LANES)) < 64
-
-    def step(x, carry):
-        a = p[0, pl.ds(pl.multiple_of(x * BLK, BLK), BLK), :].astype(F32)
-        b = q[0, pl.ds(pl.multiple_of(x * BLK, BLK), BLK), :].astype(F32)
-        out[x] = jnp.where(low, a, pltpu.roll(b, 64, 1)).astype(BF16)
-        out[x + 32] = jnp.where(low, pltpu.roll(a, 64, 1), b).astype(BF16)
-        return carry
-
-    lax.fori_loop(0, 32, step, 0, unroll=4)
-
-
-def slot_spec(table, t, c, rows):
-    def where(b, *rest):
-        ref = rest[-1]
-        return (table.x(ref, t, table.column(ref), table.row(ref) * 2 + b, c), 0, 0)
-
-    return pl.BlockSpec((1, rows, LANES), where)
-
-
-def pick(table, tab, t, slots, shape):
-    rows = slots.shape[1]
-    return pl.pallas_call(
-        pick_body,
+        functools.partial(pick_body, table, t),
         out_shape=jax.ShapeDtypeStruct(shape, BF16),
         grid_spec=pltpu.PrefetchScalarGridSpec(
             num_scalar_prefetch=1,
             grid=(2,),
-            in_specs=[slot_spec(table, t, 0, rows), slot_spec(table, t, 1, rows)],
+            in_specs=[pl.BlockSpec(memory_space=pl.ANY)] * 3,
             out_specs=pl.BlockSpec((64, BLK, LANES), lambda b, r: (0, b, 0)),
+            scratch_shapes=[pltpu.VMEM((4, rows, LANES), BF16), pltpu.SemaphoreType.DMA((4,))],
         ),
         compiler_params=pltpu.CompilerParams(vmem_limit_bytes=LIMIT),
-        cost_estimate=pl.CostEstimate(flops=2 * 64 * 128 * 128, bytes_accessed=8 << 20, transcendentals=0),
+        cost_estimate=pl.CostEstimate(flops=2 * 64 * 128 * 128, bytes_accessed=4 << 20, transcendentals=0),
         name="pick",
-    )(tab, slots, slots)
+    )(tab, own, *far)
 
 
 XC = 16
-
-
-def warp_body(table, t, ref, p, q, fixed, field, out, near, up, down, edge):
+SPAN = 6
+
+
+def warp_body(table, t, ref, received, fixed, field, out, near, up, down, edge, turn, slots, sems):
     b, chunk = pl.program_id(0), pl.program_id(1)
+    own, far = lambda i: received.at[i, 0], lambda i: [received.at[i, 1]]
+
+    @pl.when((b == 0) & (chunk == 0))
+    def _():
+        fetch(table, t, ref, own, far, slots, sems)
 
     @pl.when(chunk == 0)
     def _():
-        low = lane_of((BLK, LANES)) < 64
-
-        def both(rows, size):
-            a = p[0, pl.ds(rows, size), :].astype(F32)
-            c = q[0, pl.ds(rows, size), :].astype(F32)
-            mask = low if size == BLK else lane_of((size, LANES)) < 64
-            return (
-                jnp.where(mask, a, pltpu.roll(c, 64, 1)),
-                jnp.where(mask, pltpu.roll(a, 64, 1), c),
-            )
-
-        def step(x, carry):
-            first, second = both(pl.multiple_of(x * BLK, BLK), BLK)
-            near[x + 1, 8:72, :] = first
-            near[x + 33, 8:72, :] = second
-            return carry
-
-        lax.fori_loop(0, 32, step, 0, unroll=2)
-        first, second = both(2048, BLK)
+        await_slot(own, slots, sems, 2 * b)
+        await_slot(own, slots, sems, 2 * b + 1)
+        p, q = slots.at[2 * b], slots.at[2 * b + 1]
+
+        def put(x, value):
+            near[pl.ds(x + 1, GROUP), 8:72, :] = value.astype(F32)
+
+        main_rows(p, q, put, put)
+
+        def both(start, size):
+            u = p[start : start + size, :].astype(F32)
+            v = q[start : start + size, :].astype(F32)
+            mask = lane_of((size, LANES)) < 64
+            return jnp.where(mask, u, pltpu.roll(v, 64, 1)), jnp.where(mask, pltpu.roll(u, 64, 1), v)
+
+        first, second = both(MAIN, BLK)
         near[0, 8:72, :] = first
         near[65, 8:72, :] = second
-        first, second = both(2112, 80)
+        first, second = both(MAIN + 64, 80)
         edge[0] = first
         edge[1] = second
 
         a, g = table.column(ref), table.row(ref)
-        spot_p = jnp.where(table.z(ref, t, a, g * 2 + b, 0) == 0, 63, 0)
-        spot_q = jnp.where(table.z(ref, t, a, g * 2 + b, 1) == 0, 127, 64)
-        face_p = p[0, 2192:2272, :].astype(F32)
-        face_q = q[0, 2192:2272, :].astype(F32)
+        z_p = table.z(ref, t, a, g * 2 + b, 0)
+        z_q = table.z(ref, t, a, g * 2 + b, 1)
+        row = lax.broadcasted_iota(jnp.int32, (128, 256), 0)
+        col = lax.broadcasted_iota(jnp.int32, (128, 256), 1)
+        inside = ((row == col + 1) & (col != 63)) | ((row == col - 129) & (col != 192))
+        turn[0:128, :] = jnp.where(inside & ((col < 128) | (col > 128)), 1.0, 0.0).astype(BF16)
+        turn[128:256, :] = jnp.where(col == jnp.where(z_p == 0, 63, 128), 1.0, 0.0).astype(BF16)
+        turn[256:384, :] = jnp.where(col == jnp.where(z_q == 0, 127, 192), 1.0, 0.0).astype(BF16)
+        face_p = p[MAIN + 144 : MAIN + 224, :].astype(F32)
+        face_q = q[MAIN + 144 : MAIN + 224, :].astype(F32)
         lane = lane_of((80, LANES))
 
-        def widen(i, carry):
-            near[i, 7:8, :] = edge[0, pl.ds(i, 1), :]
-            near[i, 72:73, :] = edge[1, pl.ds(i, 1), :]
-            value = near[i]
-            at_p = pltpu.roll(face_p, lax.rem(spot_p - i + 256, 128), 1)
-            at_q = pltpu.roll(face_q, lax.rem(spot_q - i + 256, 128), 1)
-            fill = jnp.where(lane == spot_p, at_p, jnp.where(lane == spot_q, at_q, 0.0))
-            up[i] = jnp.where((lane == 63) | (lane == 127), fill, pltpu.roll(value, 127, 1))
-            down[i] = jnp.where((lane == 0) | (lane == 64), fill, pltpu.roll(value, 1, 1))
+        def widen(j, carry):
+            parts = []
+            for k in range(SPAN):
+                i = j * SPAN + k
+                near[i, 7:8, :] = edge[0, pl.ds(i, 1), :]
+                near[i, 72:73, :] = edge[1, pl.ds(i, 1), :]
+                here = lane == i
+                parts.append(
+                    jnp.concatenate(
+                        [
+                            near[i].astype(BF16),
+                            jnp.where(here, face_p, 0.0).astype(BF16),
+                            jnp.where(here, face_q, 0.0).astype(BF16),
+                        ],
+                        axis=1,
+                    )
+                )
+            got = jnp.dot(jnp.concatenate(parts, axis=0), turn[...], preferred_element_type=F32)
+            got = got.reshape(SPAN, 80, 256)
+            up[pl.ds(j * SPAN, SPAN)] = got[:, :, :LANES]
+            down[pl.ds(j * SPAN, SPAN)] = got[:, :, LANES:]
             return carry
 
-        lax.fori_loop(0, 66, widen, 0)
-
-    def plane(x, carry):
-        xi = chunk * XC + x
+        lax.fori_loop(0, 66 // SPAN, widen, 0)
+
+    def planes(j, carry):
         for tile in range(8):
             r = 8 * tile
-            fx, fy, fz = field[0, x, r : r + 8, :], field[1, x, r : r + 8, :], field[2, x, r : r + 8, :]
-            px, py, pz = fx > 0, fy > 0, fz > 0
-            wx, wy, wz = jnp.abs(fx), jnp.abs(fy), jnp.abs(fz)
-            per_x = []
-            for kx in range(3):
-                per_y = []
-                for ky in range(3):
+            seen = {}
+
+            def load(name, array, xi, ky):
+                if (name, xi, ky) not in seen:
                     y0 = 7 + r + ky
-                    here = near[xi + kx, y0 : y0 + 8, :]
-                    beside = jnp.where(pz, up[xi + kx, y0 : y0 + 8, :], down[xi + kx, y0 : y0 + 8, :])
-                    per_y.append((here, beside))
-                far = [jnp.where(py, per_y[2][i], per_y[0][i]) for i in range(2)]
-                per_x.append((per_y[1], far))
-            corner = [
-                [
-                    per_x[1][j][i] if s == 0 else jnp.where(px, per_x[2][j][i], per_x[0][j][i])
-                    for j in range(2)
-                    for i in range(2)
-                ]
-                for s in range(2)
-            ]
-            lines = []
-            for s in range(2):
-                c00, c01, c10, c11 = corner[s]
-                l0 = c00 + wz * (c01 - c00)
-                l1 = c10 + wz * (c11 - c10)
-                lines.append(l0 + wy * (l1 - l0))
-            warped = lines[0] + wx * (lines[1] - lines[0])
-            out[x, r : r + 8, :] = fixed[x, r : r + 8, :].astype(F32) - warped
+                    seen[name, xi, ky] = array[chunk * XC + 4 * j + xi, y0 : y0 + 8, :]
+                return seen[name, xi, ky]
+
+            for xo in range(4):
+                x = 4 * j + xo
+                fx, fy, fz = field[0, x, r : r + 8, :], field[1, x, r : r + 8, :], field[2, x, r : r + 8, :]
+                px, py, pz = fx > 0, fy > 0, fz > 0
+                wx, wy, wz = jnp.abs(fx), jnp.abs(fy), jnp.abs(fz)
+                per_x = []
+                for kx in range(3):
+                    per_y = []
+                    for ky in range(3):
+                        here = load("near", near, xo + kx, ky)
+                        beside = jnp.where(pz, load("up", up, xo + kx, ky), load("down", down, xo + kx, ky))
+                        per_y.append((here, beside))
+                    aside = [jnp.where(py, per_y[2][i], per_y[0][i]) for i in range(2)]
+                    per_x.append((per_y[1], aside))
+                lines = []
+                for s in range(2):
+                    c00, c01, c10, c11 = [
+                        per_x[1][v][i] if s == 0 else jnp.where(px, per_x[2][v][i], per_x[0][v][i])
+                        for v in range(2)
+                        for i in range(2)
+                    ]
+                    l0 = c00 + wz * (c01 - c00)
+                    l1 = c10 + wz * (c11 - c10)
+                    lines.append(l0 + wy * (l1 - l0))
+                warped = lines[0] + wx * (lines[1] - lines[0])
+                out[x, r : r + 8, :] = fixed[x, r : r + 8, :].astype(F32) - warped
         return carry
 
-    lax.fori_loop(0, XC, plane, 0)
-
-
-def warp(table, tab, t, slots, fixed, field):
-    rows = slots.shape[1]
-    tile_x, tile_y, tile_z = fixed.shape
-
+    lax.fori_loop(0, XC // 4, planes, 0)
+
+
+def warp(table, tab, t, received, fixed, field):
+    rows = received.shape[2]
+    tile_x = fixed.shape[0]
     block = pl.BlockSpec((XC, BLK, LANES), lambda b, c, r: (c, b, 0))
     return pl.pallas_call(
         functools.partial(warp_body, table, t),
@@ -265,18 +347,23 @@
             num_scalar_prefetch=1,
             grid=(2, tile_x // XC),
             in_specs=[
-                slot_spec(table, t, 0, rows),
-                slot_spec(table, t, 1, rows),
+                pl.BlockSpec(memory_space=pl.ANY),
                 block,
                 pl.BlockSpec((3, XC, BLK, LANES), lambda b, c, r: (0, c, b, 0)),
             ],
             out_specs=block,
-            scratch_shapes=[pltpu.VMEM((66, 80, LANES), F32)] * 3 + [pltpu.VMEM((2, 80, LANES), F32)],
+            scratch_shapes=[pltpu.VMEM((66, 80, LANES), F32)] * 3
+            + [
+                pltpu.VMEM((2, 80, LANES), F32),
+                pltpu.VMEM((384, 256), BF16),
+                pltpu.VMEM((4, rows, LANES), BF16),
+                pltpu.SemaphoreType.DMA((4,)),
+            ],
         ),
         compiler_params=pltpu.CompilerParams(vmem_limit_bytes=LIMIT),
         cost_estimate=pl.CostEstimate(flops=60 << 20, bytes_accessed=22 << 20, transcendentals=0),
         name="warp",
-    )(tab, slots, slots, fixed, field)
+    )(tab, received, fixed, field)
 
 
 def put_planes(is_warped, g, count, start, total, diff, value, value_y, fixed, fixed_y):
@@ -558,30 +645,71 @@
     return lax.ppermute(part(length - width), "gx", up), lax.ppermute(part(0), "gx", down)
 
 
-def shell_rows(moving, moving_y, low, high, g):
-    last, first = moving_y.shape[1] - 1, 0
-
-    def extend(main, rows_y):
-        below = jnp.where(g == 1, rows_y[:, last : last + 1], 0)
-        above = jnp.where(g == 0, rows_y[:, first : first + 1], 0)
-        return jnp.concatenate([below, main, above], axis=1)
-
-    planes = jnp.concatenate([low[:, :128], moving, high[:, :128]], axis=0)
-    planes_y = jnp.concatenate([low[:, 128:], moving_y, high[:, 128:]], axis=0)
-    ext = extend(planes, planes_y)
+def column_body(table, ref, low, main, high, rows_y, out):
+    g = table.row(ref)
+    lane = lane_of((128, LANES))
+    small = lane_of((16, LANES))
+
+    def put(i, acc, plane, plane_y):
+        shift = lax.rem(i + 256 - (BLK - 1), LANES)
+        got = pltpu.roll(plane, shift, 1)
+        got_y = pltpu.roll(plane_y, shift, 1)
+        return (
+            jnp.where(lane == i, got, acc[0]),
+            jnp.where(lane == i + 1, got, acc[1]),
+            jnp.where(small == i, got_y, acc[2]),
+            jnp.where(small == i + 1, got_y, acc[3]),
+        )
+
+    acc = (jnp.zeros((128, LANES), F32),) * 2 + (jnp.zeros((16, LANES), F32),) * 2
+    acc = put(0, acc, low[0].astype(F32), rows_y[0].astype(F32))
+    acc = put(65, acc, high[0].astype(F32), rows_y[65].astype(F32))
+
+    def step(x, acc):
+        return put(x + 1, acc, main[x].astype(F32), rows_y[x + 1].astype(F32))
+
+    acc = lax.fori_loop(0, 64, step, acc)
+    for k in range(2):
+        full, part = acc[k], acc[2 + k]
+        if k:
+            full, part = pltpu.roll(full, LANES - 1, 1), pltpu.roll(part, LANES - 1, 1)
+        out[k, 16:144, :] = full.astype(BF16)
+        out[k, 0:16, :] = jnp.where(g == 1, part, 0.0).astype(BF16)
+        out[k, 144:160, :] = jnp.where(g == 0, part, 0.0).astype(BF16)
+
+
+def columns(table, tab, low, main, high, rows_y):
+    args = (low, main, high, rows_y)
+    return pl.pallas_call(
+        functools.partial(column_body, table),
+        out_shape=jax.ShapeDtypeStruct((2, 160, LANES), BF16),
+        grid_spec=pltpu.PrefetchScalarGridSpec(
+            num_scalar_prefetch=1,
+            grid=(1,),
+            in_specs=[pl.BlockSpec(v.shape, lambda d, r: (0, 0, 0)) for v in args],
+            out_specs=pl.BlockSpec((2, 160, LANES), lambda d, r: (0, 0, 0)),
+        ),
+        compiler_params=pltpu.CompilerParams(vmem_limit_bytes=LIMIT),
+        cost_estimate=SMALL,
+        name="columns",
+    )(tab, *args)
+
+
+def shell_rows(low, main, high, rows_y, column, g):
+    def at(y):
+        return jnp.concatenate([low[:, y], main[:, y], high[:, y]])
+
+    below = [jnp.where(g == 1, rows_y[:, -1], 0), at(BLK - 1)]
+    above = [at(BLK), jnp.where(g == 0, rows_y[:, 0], 0)]
     faces = []
     for b in range(2):
+        y = slice(b * BLK, b * BLK + BLK)
         for c in range(2):
             z = slice(c * BLK, c * BLK + BLK)
-            y = slice(b * BLK + 1, b * BLK + 1 + BLK)
-            side_x = jnp.concatenate([ext[0, y, z], ext[65, y, z]], axis=1)
-            side_y = jnp.concatenate([ext[:, b * BLK, z], ext[:, b * BLK + BLK + 1, z]], axis=1)
-            side_z = ext[:, b * BLK : b * BLK + BLK + 2, BLK - c].T
-            faces.append(
-                jnp.concatenate(
-                    [side_x, jnp.pad(side_y, ((0, 14), (0, 0))), jnp.pad(side_z, ((7, 7), (0, 62)))], axis=0
-                )
-            )
+            side_x = jnp.concatenate([low[0, y, z], high[0, y, z]], axis=1)
+            side_y = jnp.concatenate([below[b][:, z], above[b][:, z]], axis=1)
+            side_z = column[1 - c, b * BLK + 8 : b * BLK + 88]
+            faces.append(jnp.concatenate([side_x, jnp.pad(side_y, ((0, 14), (0, 0))), side_z], axis=0))
     return jnp.stack(faces)
 
 
@@ -596,24 +724,40 @@
         ]
     )
     weights = band()
+    n = lax.axis_size("gx")
+    half = n // 2
+    opposite = [(i, (i + half) % n) for i in range(n)]
+    halves = [list(range(half)), list(range(half, n))]
 
     def send(slots):
-        return lax.all_to_all(slots, "gx", split_axis=0, concat_axis=0, tiled=True)
-
-    slots0 = send(pack(table, tab, 0, moving))
-
-    both = jnp.stack([fixed, moving])
-    both_y = swap_y(both, g, 16)
-    low, high = shift_x(both, both_y, 5)
-    fixed_y = both_y[0]
-    fixed_x = (low[0], high[0])
-    shells = shell_rows(moving, both_y[1], low[1, 4:], high[1, :1], g)
-    ready1 = pack(table, tab, 1, moving, shells)
-
-    slots0, ready1 = lax.optimization_barrier((slots0, ready1))
-    slots1 = send(ready1)
-
-    warped = pick(table, tab, 0, slots0, fixed.shape)
+        return lax.all_to_all(slots, "gx", split_axis=0, concat_axis=0, axis_index_groups=halves, tiled=True)
+
+    tile_x = fixed.shape[0]
+    mirror_a = lax.ppermute(moving[:PART], "gx", opposite)
+    up = [(i, i + 1) for i in range(n - 1)]
+    low = lax.ppermute(moving[-1:], "gx", up)
+    high = lax.ppermute(moving[:1], "gx", [(j, i) for i, j in up])
+    rest, low, high = lax.optimization_barrier((moving[PART:], low, high))
+    mirror_b = lax.ppermute(rest, "gx", opposite)
+    own0 = send(pack(table, tab, 0, False, [moving]))
+    rows_y = swap_y(jnp.concatenate([fixed, low, moving, high]), g, 16)
+    fixed_y, moving_y = rows_y[:tile_x], rows_y[tile_x:]
+    fixed_x = shift_x(fixed, fixed_y, 5)
+    column = columns(table, tab, low, moving, high, moving_y)
+    shells = shell_rows(low, moving, high, moving_y, column, g)
+    shells_far = lax.ppermute(shells, "gx", opposite)
+    slots1 = pack(table, tab, 1, False, [moving], shells)
+    far0_a = send(pack(table, tab, 0, True, [mirror_a]))
+    mirror_b, own0, far0_a, shells_far, slots1, fixed_x = lax.optimization_barrier(
+        (mirror_b, own0, far0_a, shells_far, slots1, fixed_x)
+    )
+
+    far0_b = send(pack(table, tab, 0, True, [mirror_b]))
+    slots1 = pack(table, tab, 1, True, [mirror_a, mirror_b], shells_far, slots1)
+    far0_b, slots1 = lax.optimization_barrier((far0_b, slots1))
+    slots1 = send(slots1)
+
+    warped = pick(table, tab, 0, own0, (far0_a, far0_b), fixed.shape)
     warped_y = swap_y(warped, g, 16)
     warped_x = shift_x(warped, warped_y, 5)
     field = inner(table, tab, weights, warped, warped_y, fixed, fixed_y)

time: 376 us -> 331 us (0.88)
  starting transfers between devices: 84.3 us -> 61.3 us
  waiting for transfers between devices: 93.7 us -> 76.3 us
  local copies, waits for them, and re-layouts: 33.9 us -> 29.3 us
    ppermute x0 -> x5, waiting for transfers between devices: none -> 32.8 us  [the longest x1 32.8 us: local(): mirror_a = lax.ppermute(moving[:PART], 'gx', opposite)]
    ppermute x4, waiting for transfers between devices: 64.1 us -> 34 us  [shift_x(): lax.ppermute(part(length - width), 'gx', up)]
    ppermute x4, starting transfers between devices: 35.9 us -> 8.21 us  [shift_x(): lax.ppermute(part(0), 'gx', down)]
    ppermute x4, waiting for transfers between devices: 27.7 us -> 2.07 us  [shift_x(): lax.ppermute(part(0), 'gx', down)]
    pallas_call x3 -> x7, Pallas kernels: 22.9 us -> 34 us  [the longest x5 21.3 us: pack(): pl.pallas_call(functools.partial(pack_body, table, t, far, count, shells...]
    all_to_all x2 -> x4, starting transfers between devices: 33.1 us -> 22.6 us  [send(): lax.all_to_all(slots, 'gx', split_axis=0, concat_axis=0, axis_index_group...]
    pallas_call x1, Pallas kernels: 31.3 us -> 21.3 us  [warp(): pl.pallas_call(functools.partial(warp_body, table, t), out_shape=jax.Shap...]
    ppermute x0 -> x5, starting transfers between devices: none -> 7.95 us  [the longest x1 4.05 us: local(): low = lax.ppermute(moving[-1:], 'gx', up)]
  transfers between devices with their start and end apart: 14 -> 21, of which waited for: 6 -> 7; matrix products, arithmetic and copies ran while one was open for 10% -> 9% of each run, Pallas kernels for 33% -> 40%
where the time goes in v2:
time: 331 us; the launch traced here: 327 us
  Pallas kernels  150 us (45%)
  waiting for transfers between devices  76.3 us (23%)
  starting transfers between devices  61.3 us (19%)
  local copies, waits for them, and re-layouts  29.3 us (9%)
  other arithmetic  9.24 us (3%)
    pallas_call x2, Pallas kernels, inner(): pl.pallas_call(functools.partial(inner_body, table, is_warped), out_shape...  64.2 us
    ppermute x4, waiting for transfers between devices, shift_x(): lax.ppermute(part(length - width), 'gx', up)  34 us
    ppermute x1, waiting for transfers between devices, local(): mirror_a = lax.ppermute(moving[:PART], 'gx', opposite)  32.8 us
    pallas_call x2, Pallas kernels, rim(): pl.pallas_call(functools.partial(rim_body, table, is_warped), out_shape=j...  30.5 us
    all_to_all x4, starting transfers between devices, send(): lax.all_to_all(slots, 'gx', split_axis=0, concat_axis=0, axis_index_group...  22.6 us
    pallas_call x1, Pallas kernels, warp(): pl.pallas_call(functools.partial(warp_body, table, t), out_shape=jax.Shap...  21.3 us
    pallas_call x5, Pallas kernels, pack(): pl.pallas_call(functools.partial(pack_body, table, t, far, count, shells...  21.3 us
    ppermute x4, starting transfers between devices, shift_x(): lax.ppermute(part(length - width), 'gx', up)  14 us
  transfers between devices with their start and end apart: 21, of which 7 were waited for; matrix products, arithmetic and copies ran while one was open for 9% of the time, Pallas kernels for 40%

profile of v2, /device:TPU:23, one launch (start us, length us, event | category | flops | bytes accessed | tf_op | source)
XLA Modules:
  0.0 327.3 jit_solution(6648848733564425564)
XLA Ops:
  7.0 4.0 %collective-permute-start = (bf16[1,128,128]{2,1,0:T(8,128)(2,1)S(1)}, bf16[1,128,128]{2,1,0:T(8,128)(2,1)S(1)}, u32[]{:S(2)}, u32[]{:S(2)}) collective-permute-start(bf16[1,128,128]{2,1,0:T(8,128)(2,1)S(1)} %get-tuple-element.39), channel_id=1, source_target_pairs={{0,2},{2,4},{4,6},{6,8},{8,10},{10,12},{12,14},{1,3},{3,5},{5,7},{... | collective-permute-start | bytes 98312 | tf_op jit(solution)/shard_map/ppermute | solution.py:738
  15.0 32.8 %collective-permute-done.3.refs_0_ = bf16[32,128,128]{2,1,0:T(8,128)(2,1)S(1)} collective-permute-done((bf16[32,128,128]{2,1,0:T(8,128)(2,1)S(1)}, bf16[32,128,128]{2,1,0:T(8,128)(2,1)S(1)}, u32[]{:S(2)}, u32[]{:S(2)}) %collective-permute-start.3) | collective-permute-done | bytes 1048608 | tf_op jit(solution)/shard_map/ppermute | solution.py:736
  48.8 3.8 %pack0far.2 = bf16[4,1024,128]{2,1,0:T(8,128)(2,1)} custom-call(s32[258]{0:T(512)} %pad_add_fusion.ref, bf16[32,128,128]{2,1,0:T(8,128)(2,1)} %copy-done.2), custom_call_target="tpu_custom_call" | custom-call | flops 65536 | bytes 65536 | tf_op jit(solution)/shard_map/pack0far/pallas_call | solution.py:131
  52.6 7.7 %all-to-all-start.1 = ((bf16[4,1024,128]{2,1,0:T(8,128)(2,1)}), bf16[4,1024,128]{2,1,0:T(8,128)(2,1)}, u32[]{:S(2)}, u32[]{:S(2)}) async-start(bf16[4,1024,128]{2,1,0:T(8,128)(2,1)} %pack0far.2), calls=%async_computation.1 | async-start | bytes 2097152 | tf_op jit(solution)/shard_map/all_to_all | solution.py:733
  60.3 3.3 %constant_dynamic-update-slice_fusion.3 = bf16[130,128,128]{2,1,0:T(8,128)(2,1)} fusion(bf16[64,128,128]{2,1,0:T(8,128)(2,1)} %fixed.9), kind=kLoop, calls=%fused_computation.53 | loop fusion | bytes 4194304
  63.6 4.5 %pack0own.1 = bf16[4,2048,128]{2,1,0:T(8,128)(2,1)} custom-call(s32[258]{0:T(512)} %pad_add_fusion.ref, bf16[64,128,128]{2,1,0:T(8,128)(2,1)} %refs_1_.3, bf16[64,128,128]{2,1,0:T(8,128)(2,1)} %refs_1_.3), custom_call_target="tpu_custom_call" | custom-call | flops 65536 | bytes 65536 | tf_op jit(solution)/shard_map/pack0own/pallas_call | solution.py:131
  75.3 3.6 %all-to-all-start = ((bf16[4,2048,128]{2,1,0:T(8,128)(2,1)}), bf16[4,2048,128]{2,1,0:T(8,128)(2,1)S(1)}, u32[]{:S(2)}, u32[]{:S(2)}) async-start(bf16[4,2048,128]{2,1,0:T(8,128)(2,1)} %pack0own.1), calls=%async_computation | async-start | bytes 4194304 | tf_op jit(solution)/shard_map/all_to_all | solution.py:733
  84.7 8.8 %columns.1 = bf16[2,160,128]{2,1,0:T(8,128)(2,1)} custom-call(s32[258]{0:T(512)} %pad_add_fusion.ref, bf16[1,128,128]{2,1,0:T(8,128)(2,1)} %copy-done.14, bf16[64,128,128]{2,1,0:T(8,128)(2,1)} %refs_1_.3, bf16[1,128,128]{2,1,0:T(8,128)(2,1)} %copy-done.13, bf16[66,16,128]{2,1,0:T(8,128)(2,1)} %slice.241.rows_y), custom_call_target="tpu_custom_call" | custom-call | flops 65536 | bytes 65536 | tf_op jit(solution)/shard_map/columns/pallas_call | solution.py:683
  101.0 4.6 %pack1own.1.refs_3_ = bf16[4,2,2272,128]{3,2,1,0:T(8,128)(2,1)} custom-call(s32[258]{0:T(512)} %pad_add_fusion.ref, bf16[64,128,128]{2,1,0:T(8,128)(2,1)} %refs_1_.3, bf16[64,128,128]{2,1,0:T(8,128)(2,1)} %refs_1_.3, bf16[4,224,128]{2,1,0:T(8,128)(2,1)} %copy-done.8), custom_call_target="tpu_custom_call" | custom-call | flops 65536 | bytes 65536 | tf_op jit(solution)/shard_map/pack1own/pallas_call | solution.py:131
  105.6 26.0 %collective-permute-done.6.refs_2_ = bf16[5,144,128]{2,1,0:T(8,128)(2,1)S(1)} collective-permute-done((bf16[5,144,128]{2,1,0:T(8,128)(2,1)S(1)}, bf16[5,144,128]{2,1,0:T(8,128)(2,1)S(1)}, u32[]{:S(2)}, u32[]{:S(2)}) %collective-permute-start.6) | collective-permute-done | bytes 184352 | tf_op jit(solution)/shard_map/ppermute | solution.py:645
  134.0 3.8 %pack0far.3 = bf16[4,1024,128]{2,1,0:T(8,128)(2,1)} custom-call(s32[258]{0:T(512)} %pad_add_fusion.ref, bf16[32,128,128]{2,1,0:T(8,128)(2,1)} %copy-done.3), custom_call_target="tpu_custom_call" | custom-call | flops 65536 | bytes 65536 | tf_op jit(solution)/shard_map/pack0far/pallas_call | solution.py:131
  137.8 4.6 %all-to-all-start.2 = ((bf16[4,1024,128]{2,1,0:T(8,128)(2,1)}), bf16[4,1024,128]{2,1,0:T(8,128)(2,1)S(1)}, u32[]{:S(2)}, u32[]{:S(2)}) async-start(bf16[4,1024,128]{2,1,0:T(8,128)(2,1)} %pack0far.3), calls=%async_computation.2 | async-start | bytes 2097152 | tf_op jit(solution)/shard_map/all_to_all | solution.py:733
  142.5 4.6 %pack1far.1 = bf16[4,2,2272,128]{3,2,1,0:T(8,128)(2,1)} custom-call(s32[258]{0:T(512)} %pad_add_fusion.ref, bf16[32,128,128]{2,1,0:T(8,128)(2,1)} %copy-done.2, bf16[32,128,128]{2,1,0:T(8,128)(2,1)} %copy-done.3, bf16[4,224,128]{2,1,0:T(8,128)(2,1)} %copy-done.17, bf16[4,2,2272,128]{3,2,1,0:T(8,128)(2,1)} %pack1own.1.refs_3_), custom_call_target="tpu_custom_call", output_to_operand_aliasing={{}: (4, {})} | custom-call | flops 65536 | bytes 65536 | tf_op jit(solution)/shard_map/pack1far/pallas_call | solution.py:131
  147.1 6.8 %all-to-all-done.2.far_b = bf16[4,1024,128]{2,1,0:T(8,128)(2,1)S(1)} async-done(((bf16[4,1024,128]{2,1,0:T(8,128)(2,1)}), bf16[4,1024,128]{2,1,0:T(8,128)(2,1)S(1)}, u32[]{:S(2)}, u32[]{:S(2)}) %all-to-all-start.2) | async-done | bytes 1048608 | tf_op jit(solution)/shard_map/all_to_all | solution.py:733
  154.9 6.6 %all-to-all-start.3 = ((bf16[4,2,2272,128]{3,2,1,0:T(8,128)(2,1)}), bf16[4,2,2272,128]{3,2,1,0:T(8,128)(2,1)}, u32[]{:S(2)}, u32[]{:S(2)}) async-start(bf16[4,2,2272,128]{3,2,1,0:T(8,128)(2,1)} %pack1far.1), calls=%async_computation.3 | async-start | bytes 9306112 | tf_op jit(solution)/shard_map/all_to_all | solution.py:733
  161.5 3.9 %pick.1.value = bf16[64,128,128]{2,1,0:T(8,128)(2,1)} custom-call(s32[258]{0:T(512)} %pad_add_fusion.ref, bf16[4,2048,128]{2,1,0:T(8,128)(2,1)} %copy-done.1, bf16[4,1024,128]{2,1,0:T(8,128)(2,1)} %all-to-all-done.1.far_a, bf16[4,1024,128]{2,1,0:T(8,128)(2,1)} %copy-done.4), custom_call_target="tpu_custom_call" | custom-call | flops 2097152 | bytes 4194304 | tf_op jit(solution)/shard_map/pick/pallas_call | solution.py:207
  177.3 31.5 %inner0.1.refs_4_ = f32[3,64,128,128]{3,2,1,0:T(8,128)} custom-call(s32[258]{0:T(512)} %pad_add_fusion.ref, bf16[256,256]{1,0:T(8,128)(2,1)} %constant.30.weights, bf16[64,128,128]{2,1,0:T(8,128)(2,1)} %pick.1.value, bf16[64,16,128]{2,1,0:T(8,128)(2,1)} %copy-done.7, bf16[64,128,128]{2,1,0:T(8,128)(2,1)} %fixed.9, bf16[64,16,128]{2,1,0:T(8,128)(2,1)} %slice.257.fixed_y), custom_call_target="tpu_custom_call" | custom-call | flops 209715200 | bytes 31457280 | tf_op jit(solution)/shard_map/inner0/pallas_call | solution.py:510
  208.8 8.0 %collective-permute-done.9.refs_0_ = bf16[5,144,128]{2,1,0:T(8,128)(2,1)S(1)} collective-permute-done((bf16[5,144,128]{2,1,0:T(8,128)(2,1)S(1)}, bf16[5,144,128]{2,1,0:T(8,128)(2,1)S(1)}, u32[]{:S(2)}, u32[]{:S(2)}) %collective-permute-start.9) | collective-permute-done | bytes 184352 | tf_op jit(solution)/shard_map/ppermute | solution.py:645
  219.5 14.4 %rim0.1.field.refs_0_.refs_4_ = f32[3,64,128,128]{3,2,1,0:T(8,128)} custom-call(s32[258]{0:T(512)} %pad_add_fusion.ref, bf16[256,256]{1,0:T(8,128)(2,1)} %constant.30.weights, bf16[64,128,128]{2,1,0:T(8,128)(2,1)} %pick.1.value, bf16[64,16,128]{2,1,0:T(8,128)(2,1)} %copy-done.7, bf16[64,128,128]{2,1,0:T(8,128)(2,1)} %fixed.9, ...), custom_call_target="tpu_custom_call", output_to_operand_aliasing={{}: (10, {})} | custom-call | flops 62914560 | bytes 10485760 | tf_op jit(solution)/shard_map/rim0/pallas_call | solution.py:609
  240.3 3.6 %collective-permute-start.15 = (f32[3,4,136,128]{3,2,1,0:T(8,128)S(1)}, f32[3,4,136,128]{3,2,1,0:T(8,128)S(1)}, u32[]{:S(2)}, u32[]{:S(2)}) collective-permute-start(f32[3,4,136,128]{3,2,1,0:T(8,128)S(1)} %pad_maximum_fusion), channel_id=1, source_target_pairs={{0,2},{2,4},{4,6},{6,8},{8,10},{10,12},{12,14},{1,3},{3,5},{5,7},{... | collective-permute-start | bytes 2506760 | tf_op jit(solution)/shard_map/ppermute | solution.py:645
  243.9 21.3 %warp.1.value = f32[64,128,128]{2,1,0:T(8,128)} custom-call(s32[258]{0:T(512)} %pad_add_fusion.ref, bf16[4,2,2272,128]{3,2,1,0:T(8,128)(2,1)} %all-to-all-done.3.received, bf16[64,128,128]{2,1,0:T(8,128)(2,1)} %fixed.9, f32[3,64,128,128]{3,2,1,0:T(8,128)} %rim0.1.field.refs_0_.refs_4_), custom_call_target="tpu_custom_call" | custom-call | flops 62914560 | bytes 23068672 | tf_op jit(solution)/shard_map/warp/pallas_call | solution.py:343
  270.2 4.3 %collective-permute-start.12 = (f32[5,136,128]{2,1,0:T(8,128)S(1)}, f32[5,136,128]{2,1,0:T(8,128)S(1)}, u32[]{:S(2)}, u32[]{:S(2)}) collective-permute-start(f32[5,136,128]{2,1,0:T(8,128)S(1)} %pad_maximum_fusion.2), channel_id=1, source_target_pairs={{0,2},{2,4},{4,6},{6,8},{8,10},{10,12},{12,14},{1,3},{3,5},{5,7},{... | collective-permute-start | bytes 1044488 | tf_op jit(solution)/shard_map/ppermute | solution.py:645
  276.5 32.7 %inner1.1.refs_8_ = f32[3,64,128,128]{3,2,1,0:T(8,128)} custom-call(s32[258]{0:T(512)} %pad_add_fusion.ref, bf16[256,256]{1,0:T(8,128)(2,1)} %constant.30.weights, f32[64,128,128]{2,1,0:T(8,128)} %warp.1.value, f32[64,8,128]{2,1,0:T(8,128)} %copy-done.6, bf16[64,128,128]{2,1,0:T(8,128)(2,1)} %fixed.9, bf16[64,16,128]{2,1,0:T(8,128)(2,1)} %slice.257.fixed_y, ...), custom_call_target="tpu_custom_call" | custom-call | flops 209715200 | bytes 31457280 | tf_op jit(solution)/shard_map/inner1/pallas_call | solution.py:510
  311.2 16.1 %rim1.1 = f32[3,64,128,128]{3,2,1,0:T(8,128)} custom-call(s32[258]{0:T(512)} %pad_add_fusion.ref, bf16[256,256]{1,0:T(8,128)(2,1)} %constant.30.weights, f32[64,128,128]{2,1,0:T(8,128)} %warp.1.value, f32[64,8,128]{2,1,0:T(8,128)} %copy-done.6, bf16[64,128,128]{2,1,0:T(8,128)(2,1)} %fixed.9, ...), custom_call_target="tpu_custom_call", output_to_operand_aliasing={{}: (14, {})} | custom-call | flops 62914560 | bytes 10485760 | tf_op jit(solution)/shard_map/rim1/pallas_call | solution.py:609
  (129 shorter events, 64.8 us)
Async XLA Ops:
  3.4 44.4 %collective-permute-start.3 = (bf16[32,128,128]{2,1,0:T(8,128)(2,1)S(1)}, bf16[32,128,128]{2,1,0:T(8,128)(2,1)S(1)}, u32[]{:S(2)}, u32[]{:S(2)}) collective-permute-start(bf16[32,128,128]{2,1,0:T(8,128)(2,1)S(1)} %get-tuple-element.36), channel_id=1, source_target_pairs={{0,8},{2,10},{4,12},{6,14},{8,0},{10,2},{12,4},{14,6},{1,9},{3,11}... | collective-permute-start | bytes 3145736 | tf_op jit(solution)/shard_map/ppermute | solution.py:736
  4.8 63.3 %collective-permute-start.1 = (bf16[1,128,128]{2,1,0:T(8,128)(2,1)}, bf16[1,128,128]{2,1,0:T(8,128)(2,1)S(1)}, u32[]{:S(2)}, u32[]{:S(2)}) collective-permute-start(bf16[1,128,128]{2,1,0:T(8,128)(2,1)} %get-tuple-element.38), channel_id=1, source_target_pairs={{2,0},{4,2},{6,4},{8,6},{10,8},{12,10},{14,12},{3,1},{5,3},{7,5},{... | collective-permute-start | bytes 98312 | tf_op jit(solution)/shard_map/ppermute | solution.py:739
  7.0 61.2 %collective-permute-start = (bf16[1,128,128]{2,1,0:T(8,128)(2,1)S(1)}, bf16[1,128,128]{2,1,0:T(8,128)(2,1)S(1)}, u32[]{:S(2)}, u32[]{:S(2)}) collective-permute-start(bf16[1,128,128]{2,1,0:T(8,128)(2,1)S(1)} %get-tuple-element.39), channel_id=1, source_target_pairs={{0,2},{2,4},{4,6},{6,8},{8,10},{10,12},{12,14},{1,3},{3,5},{5,7},{... | collective-permute-start | bytes 98312 | tf_op jit(solution)/shard_map/ppermute | solution.py:738
  52.6 22.8 %all-to-all-start.1 = ((bf16[4,1024,128]{2,1,0:T(8,128)(2,1)}), bf16[4,1024,128]{2,1,0:T(8,128)(2,1)}, u32[]{:S(2)}, u32[]{:S(2)}) async-start(bf16[4,1024,128]{2,1,0:T(8,128)(2,1)} %pack0far.2), calls=%async_computation.1 | async-start | bytes 2097152 | tf_op jit(solution)/shard_map/all_to_all | solution.py:733
  68.1 64.9 %collective-permute-start.2 = (bf16[32,128,128]{2,1,0:T(8,128)(2,1)}, bf16[32,128,128]{2,1,0:T(8,128)(2,1)S(1)}, u32[]{:S(2)}, u32[]{:S(2)}) collective-permute-start(bf16[32,128,128]{2,1,0:T(8,128)(2,1)} %get-tuple-element.14), channel_id=1, source_target_pairs={{0,8},{2,10},{4,12},{6,14},{8,0},{10,2},{12,4},{14,6},{1,9},{3,11}... | collective-permute-start | bytes 3145736 | tf_op jit(solution)/shard_map/ppermute | solution.py:741
  73.0 6.2 %collective-permute-start.4 = (bf16[130,16,128]{2,1,0:T(8,128)(2,1)}, bf16[130,16,128]{2,1,0:T(8,128)(2,1)}, u32[]{:S(2)}, u32[]{:S(2)}) collective-permute-start(bf16[130,16,128]{2,1,0:T(8,128)(2,1)} %slice_select_fusion.1), channel_id=1, source_target_pairs={{0,1},{1,0},{2,3},{3,2},{4,5},{5,4},{6,7},{7,6},{8,9},{9,8},{10,11... | collective-permute-start | bytes 1597448 | tf_op jit(solution)/shard_map/ppermute | solution.py:630
  75.3 57.7 %all-to-all-start = ((bf16[4,2048,128]{2,1,0:T(8,128)(2,1)}), bf16[4,2048,128]{2,1,0:T(8,128)(2,1)S(1)}, u32[]{:S(2)}, u32[]{:S(2)}) async-start(bf16[4,2048,128]{2,1,0:T(8,128)(2,1)} %pack0own.1), calls=%async_computation | async-start | bytes 4194304 | tf_op jit(solution)/shard_map/all_to_all | solution.py:733
  81.6 50.0 %collective-permute-start.6 = (bf16[5,144,128]{2,1,0:T(8,128)(2,1)S(1)}, bf16[5,144,128]{2,1,0:T(8,128)(2,1)S(1)}, u32[]{:S(2)}, u32[]{:S(2)}) collective-permute-start(bf16[5,144,128]{2,1,0:T(8,128)(2,1)S(1)} %pad_maximum_fusion.5), channel_id=1, source_target_pairs={{0,2},{2,4},{4,6},{6,8},{8,10},{10,12},{12,14},{1,3},{3,5},{5,7},{... | collective-permute-start | bytes 552968 | tf_op jit(solution)/shard_map/ppermute | solution.py:645
  96.2 35.4 %collective-permute-start.5 = (bf16[4,224,128]{2,1,0:T(8,128)(2,1)S(1)}, bf16[4,224,128]{2,1,0:T(8,128)(2,1)S(1)}, u32[]{:S(2)}, u32[]{:S(2)}) collective-permute-start(bf16[4,224,128]{2,1,0:T(8,128)(2,1)S(1)} %pad_maximum_fusion.4.refs_2_), channel_id=1, source_target_pairs={{0,8},{2,10},{4,12},{6,14},{8,0},{10,2},{12,4},{14,6},{1,9},{3,11}... | collective-permute-start | bytes 688136 | tf_op jit(solution)/shard_map/ppermute | solution.py:748
  98.8 32.8 %collective-permute-start.7 = (bf16[5,144,128]{2,1,0:T(8,128)(2,1)S(1)}, bf16[5,144,128]{2,1,0:T(8,128)(2,1)S(1)}, u32[]{:S(2)}, u32[]{:S(2)}) collective-permute-start(bf16[5,144,128]{2,1,0:T(8,128)(2,1)S(1)} %pad_maximum_fusion.6), channel_id=1, source_target_pairs={{2,0},{4,2},{6,4},{8,6},{10,8},{12,10},{14,12},{3,1},{5,3},{7,5},{... | collective-permute-start | bytes 552968 | tf_op jit(solution)/shard_map/ppermute | solution.py:645
  131.6 33.8 %copy-start.11 = (bf16[5,144,128]{2,1,0:T(8,128)(2,1)}, bf16[5,144,128]{2,1,0:T(8,128)(2,1)S(1)}, u32[]{:S(2)}) copy-start(bf16[5,144,128]{2,1,0:T(8,128)(2,1)S(1)} %collective-permute-done.6.refs_2_) | copy-start | bytes 552964
  134.0 13.1 %copy-start.1 = (bf16[4,2048,128]{2,1,0:T(8,128)(2,1)}, bf16[4,2048,128]{2,1,0:T(8,128)(2,1)S(1)}, u32[]{:S(2)}) copy-start(bf16[4,2048,128]{2,1,0:T(8,128)(2,1)S(1)} %all-to-all-done.own_ref) | copy-start | bytes 6291460
  137.8 16.1 %all-to-all-start.2 = ((bf16[4,1024,128]{2,1,0:T(8,128)(2,1)}), bf16[4,1024,128]{2,1,0:T(8,128)(2,1)S(1)}, u32[]{:S(2)}, u32[]{:S(2)}) async-start(bf16[4,1024,128]{2,1,0:T(8,128)(2,1)} %pack0far.3), calls=%async_computation.2 | async-start | bytes 2097152 | tf_op jit(solution)/shard_map/all_to_all | solution.py:733
  154.9 89.0 %all-to-all-start.3 = ((bf16[4,2,2272,128]{3,2,1,0:T(8,128)(2,1)}), bf16[4,2,2272,128]{3,2,1,0:T(8,128)(2,1)}, u32[]{:S(2)}, u32[]{:S(2)}) async-start(bf16[4,2,2272,128]{3,2,1,0:T(8,128)(2,1)} %pack1far.1), calls=%async_computation.3 | async-start | bytes 9306112 | tf_op jit(solution)/shard_map/all_to_all | solution.py:733
  166.5 3.8 %collective-permute-start.8 = (bf16[64,16,128]{2,1,0:T(8,128)(2,1)S(1)}, bf16[64,16,128]{2,1,0:T(8,128)(2,1)S(1)}, u32[]{:S(2)}, u32[]{:S(2)}) collective-permute-start(bf16[64,16,128]{2,1,0:T(8,128)(2,1)S(1)} %slice_select_fusion.3), channel_id=1, source_target_pairs={{0,1},{1,0},{2,3},{3,2},{4,5},{5,4},{6,7},{7,6},{8,9},{9,8},{10,11... | collective-permute-start | bytes 786440 | tf_op jit(solution)/shard_map/ppermute | solution.py:630
  170.3 46.5 %collective-permute-start.9 = (bf16[5,144,128]{2,1,0:T(8,128)(2,1)S(1)}, bf16[5,144,128]{2,1,0:T(8,128)(2,1)S(1)}, u32[]{:S(2)}, u32[]{:S(2)}) collective-permute-start(bf16[5,144,128]{2,1,0:T(8,128)(2,1)S(1)} %pad_maximum_fusion.7), channel_id=1, source_target_pairs={{0,2},{2,4},{4,6},{6,8},{8,10},{10,12},{12,14},{1,3},{3,5},{5,7},{... | collective-permute-start | bytes 552968 | tf_op jit(solution)/shard_map/ppermute | solution.py:645
  173.4 45.4 %collective-permute-start.10 = (bf16[5,144,128]{2,1,0:T(8,128)(2,1)S(1)}, bf16[5,144,128]{2,1,0:T(8,128)(2,1)S(1)}, u32[]{:S(2)}, u32[]{:S(2)}) collective-permute-start(bf16[5,144,128]{2,1,0:T(8,128)(2,1)S(1)} %pad_maximum_fusion.8), channel_id=1, source_target_pairs={{2,0},{4,2},{6,4},{8,6},{10,8},{12,10},{14,12},{3,1},{5,3},{7,5},{... | collective-permute-start | bytes 552968 | tf_op jit(solution)/shard_map/ppermute | solution.py:645
  235.4 4.9 %collective-permute-start.14 = (f32[3,64,8,128]{3,2,1,0:T(8,128)S(1)}, f32[3,64,8,128]{3,2,1,0:T(8,128)S(1)}, u32[]{:S(2)}, u32[]{:S(2)}) collective-permute-start(f32[3,64,8,128]{3,2,1,0:T(8,128)S(1)} %slice_select_fusion), channel_id=1, source_target_pairs={{0,1},{1,0},{2,3},{3,2},{4,5},{5,4},{6,7},{7,6},{8,9},{9,8},{10,11... | collective-permute-start | bytes 2359304 | tf_op jit(solution)/shard_map/ppermute | solution.py:630
  240.2 25.0 %copy-start.5 = (f32[3,64,8,128]{3,2,1,0:T(8,128)}, f32[3,64,8,128]{3,2,1,0:T(8,128)S(1)}, u32[]{:S(2)}) copy-start(f32[3,64,8,128]{3,2,1,0:T(8,128)S(1)} %collective-permute-done.14.refs_1_.refs_5_) | copy-start | bytes 2359300
  240.3 68.8 %collective-permute-start.15 = (f32[3,4,136,128]{3,2,1,0:T(8,128)S(1)}, f32[3,4,136,128]{3,2,1,0:T(8,128)S(1)}, u32[]{:S(2)}, u32[]{:S(2)}) collective-permute-start(f32[3,4,136,128]{3,2,1,0:T(8,128)S(1)} %pad_maximum_fusion), channel_id=1, source_target_pairs={{0,2},{2,4},{4,6},{6,8},{8,10},{10,12},{12,14},{1,3},{3,5},{5,7},{... | collective-permute-start | bytes 2506760 | tf_op jit(solution)/shard_map/ppermute | solution.py:645
  266.3 3.8 %collective-permute-start.11 = (f32[64,8,128]{2,1,0:T(8,128)S(1)}, f32[64,8,128]{2,1,0:T(8,128)S(1)}, u32[]{:S(2)}, u32[]{:S(2)}) collective-permute-start(f32[64,8,128]{2,1,0:T(8,128)S(1)} %slice_select_fusion.2), channel_id=1, source_target_pairs={{0,1},{1,0},{2,3},{3,2},{4,5},{5,4},{6,7},{7,6},{8,9},{9,8},{10,11... | collective-permute-start | bytes 786440 | tf_op jit(solution)/shard_map/ppermute | solution.py:630
  267.1 42.1 %collective-permute-start.16 = (f32[3,4,136,128]{3,2,1,0:T(8,128)S(1)}, f32[3,4,136,128]{3,2,1,0:T(8,128)S(1)}, u32[]{:S(2)}, u32[]{:S(2)}) collective-permute-start(f32[3,4,136,128]{3,2,1,0:T(8,128)S(1)} %pad_maximum_fusion.1), channel_id=1, source_target_pairs={{2,0},{4,2},{6,4},{8,6},{10,8},{12,10},{14,12},{3,1},{5,3},{7,5},{... | collective-permute-start | bytes 2506760 | tf_op jit(solution)/shard_map/ppermute | solution.py:645
  270.2 39.0 %collective-permute-start.12 = (f32[5,136,128]{2,1,0:T(8,128)S(1)}, f32[5,136,128]{2,1,0:T(8,128)S(1)}, u32[]{:S(2)}, u32[]{:S(2)}) collective-permute-start(f32[5,136,128]{2,1,0:T(8,128)S(1)} %pad_maximum_fusion.2), channel_id=1, source_target_pairs={{0,2},{2,4},{4,6},{6,8},{8,10},{10,12},{12,14},{1,3},{3,5},{5,7},{... | collective-permute-start | bytes 1044488 | tf_op jit(solution)/shard_map/ppermute | solution.py:645
  274.5 34.7 %collective-permute-start.13 = (f32[5,136,128]{2,1,0:T(8,128)S(1)}, f32[5,136,128]{2,1,0:T(8,128)S(1)}, u32[]{:S(2)}, u32[]{:S(2)}) collective-permute-start(f32[5,136,128]{2,1,0:T(8,128)S(1)} %pad_maximum_fusion.3), channel_id=1, source_target_pairs={{2,0},{4,2},{6,4},{8,6},{10,8},{12,10},{14,12},{3,1},{5,3},{7,5},{... | collective-permute-start | bytes 1044488 | tf_op jit(solution)/shard_map/ppermute | solution.py:645
  (19 other events, 80.8 us)

commit v3 on v2

--- a/solution.py
+++ b/solution.py
@@ -13,6 +13,7 @@
 STIFF = 0.05
 LANES = 128
 CH = 8
+LARGE = pl.CostEstimate(flops=1 << 27, bytes_accessed=1 << 27, transcendentals=0)
 SMALL = pl.CostEstimate(flops=1 << 16, bytes_accessed=1 << 16, transcendentals=0)
 LIMIT = 56 * 1024 * 1024
 F32 = jnp.float32
@@ -89,8 +90,6 @@
     column = a if not far else jnp.where(a >= half, a - half, a + half)
     blk_y, blk_z, out_z = wanted_block(table, ref, t, here * half + pl.program_id(0), column)
     parts, out = refs[:count], refs[-1]
-    if shell:
-        out = out.at[0]
     y0 = pl.multiple_of(blk_y * BLK, BLK)
     keep = (lane_of((GROUP, BLK, LANES)) < 64) == (blk_z == 0)
     turn = jnp.where(blk_z == out_z, 0, PART // 2)
@@ -106,7 +105,7 @@
         out[0, MAIN:, :] = refs[count][blk_y * 2 + blk_z]
 
 
-def pack(table, tab, t, far, parts, shells=None, into=None):
+def pack(table, tab, t, far, parts, shells=None):
     half = table.shape[1] // 2
     args, specs = [], []
     for part in parts:
@@ -115,28 +114,21 @@
             specs.append(pl.BlockSpec((PART,) + part.shape[1:], lambda d, r, i=i: (i, 0, 0)))
     count = len(args)
     rows = count * PART // 2 * BLK
-    shape = (half, rows, LANES)
-    out_spec = pl.BlockSpec((1, rows, LANES), lambda d, r: (d, 0, 0))
-    aliases = {}
     if shells is not None:
         rows = rows + shells.shape[1]
-        shape = (half, 2, rows, LANES)
         args.append(shells)
         specs.append(pl.BlockSpec(shells.shape, lambda d, r: (0, 0, 0)))
-        out_spec = pl.BlockSpec((1, 1, rows, LANES), lambda d, r: (d, int(far), 0, 0))
-    if into is not None:
-        aliases = {1 + len(args): 0}
-        args.append(into)
-        specs.append(pl.BlockSpec(memory_space=pl.ANY))
     return pl.pallas_call(
         functools.partial(pack_body, table, t, far, count, shells is not None),
-        out_shape=jax.ShapeDtypeStruct(shape, BF16),
+        out_shape=jax.ShapeDtypeStruct((half, rows, LANES), BF16),
         grid_spec=pltpu.PrefetchScalarGridSpec(
-            num_scalar_prefetch=1, grid=(half,), in_specs=specs, out_specs=out_spec
+            num_scalar_prefetch=1,
+            grid=(half,),
+            in_specs=specs,
+            out_specs=pl.BlockSpec((1, rows, LANES), lambda d, r: (d, 0, 0)),
         ),
-        input_output_aliases=aliases,
         compiler_params=pltpu.CompilerParams(vmem_limit_bytes=LIMIT),
-        cost_estimate=SMALL,
+        cost_estimate=LARGE if t == 1 and far else SMALL,
         name="pack%d%s" % (t, "far" if far else "own"),
     )(tab, *args)
 
@@ -158,11 +150,7 @@
 
             @pl.when(jnp.logical_not(near))
             def _():
-                start = 0
-                for array in far(index):
-                    piece = slots.at[k, start : start + array.shape[0]]
-                    pltpu.make_async_copy(array, piece, sems.at[k]).start()
-                    start += array.shape[0]
+                pltpu.make_async_copy(far(index), slots.at[k], sems.at[k]).start()
 
 
 def await_slot(own, slots, sems, k):
@@ -185,9 +173,9 @@
     lax.fori_loop(0, 32 // GROUP, step, 0)
 
 
-def pick_body(table, t, ref, own_ref, far_a, far_b, out, slots, sems):
+def pick_body(table, t, ref, own_ref, far_ref, out, slots, sems):
     b = pl.program_id(0)
-    own, far = lambda i: own_ref.at[i], lambda i: [far_a.at[i], far_b.at[i]]
+    own, far = lambda i: own_ref.at[i], lambda i: far_ref.at[i]
 
     @pl.when(b == 0)
     def _():
@@ -210,27 +198,44 @@
         grid_spec=pltpu.PrefetchScalarGridSpec(
             num_scalar_prefetch=1,
             grid=(2,),
-            in_specs=[pl.BlockSpec(memory_space=pl.ANY)] * 3,
+            in_specs=[pl.BlockSpec(memory_space=pl.ANY)] * 2,
             out_specs=pl.BlockSpec((64, BLK, LANES), lambda b, r: (0, b, 0)),
             scratch_shapes=[pltpu.VMEM((4, rows, LANES), BF16), pltpu.SemaphoreType.DMA((4,))],
         ),
         compiler_params=pltpu.CompilerParams(vmem_limit_bytes=LIMIT),
         cost_estimate=pl.CostEstimate(flops=2 * 64 * 128 * 128, bytes_accessed=4 << 20, transcendentals=0),
         name="pick",
-    )(tab, own, *far)
+    )(tab, own, far)
 
 
 XC = 16
-SPAN = 6
-
-
-def warp_body(table, t, ref, received, fixed, field, out, near, up, down, edge, turn, slots, sems):
+SPAN = 8
+
+
+def warp_body(table, t, ref, own_ref, far_ref, fixed, field, out, near, up, down, edge, turn, slots, sems):
     b, chunk = pl.program_id(0), pl.program_id(1)
-    own, far = lambda i: received.at[i, 0], lambda i: [received.at[i, 1]]
+    own, far = lambda i: own_ref.at[i], lambda i: far_ref.at[i]
 
     @pl.when((b == 0) & (chunk == 0))
     def _():
         fetch(table, t, ref, own, far, slots, sems)
+
+    def widen(first, count):
+        face_p = slots[2 * b, MAIN + 144 : MAIN + 224, :].astype(F32)
+        face_q = slots[2 * b + 1, MAIN + 144 : MAIN + 224, :].astype(F32)
+        lane = lane_of((80, LANES))
+        parts = []
+        for k in range(count):
+            i = first + k
+            near[i, 7:8, :] = edge[0, pl.ds(i, 1), :]
+            near[i, 72:73, :] = edge[1, pl.ds(i, 1), :]
+            here = lane == i
+            sides = [jnp.where(here, face, 0.0).astype(BF16) for face in (face_p, face_q)]
+            parts.append(jnp.concatenate([near[i].astype(BF16)] + sides, axis=1))
+        got = jnp.dot(jnp.concatenate(parts, axis=0), turn[...], preferred_element_type=F32)
+        got = got.reshape(count, 80, 256)
+        up[pl.ds(first, count)] = got[:, :, :LANES]
+        down[pl.ds(first, count)] = got[:, :, LANES:]
 
     @pl.when(chunk == 0)
     def _():
@@ -262,37 +267,13 @@
         row = lax.broadcasted_iota(jnp.int32, (128, 256), 0)
         col = lax.broadcasted_iota(jnp.int32, (128, 256), 1)
         inside = ((row == col + 1) & (col != 63)) | ((row == col - 129) & (col != 192))
-        turn[0:128, :] = jnp.where(inside & ((col < 128) | (col > 128)), 1.0, 0.0).astype(BF16)
+        turn[0:128, :] = jnp.where(inside, 1.0, 0.0).astype(BF16)
         turn[128:256, :] = jnp.where(col == jnp.where(z_p == 0, 63, 128), 1.0, 0.0).astype(BF16)
         turn[256:384, :] = jnp.where(col == jnp.where(z_q == 0, 127, 192), 1.0, 0.0).astype(BF16)
-        face_p = p[MAIN + 144 : MAIN + 224, :].astype(F32)
-        face_q = q[MAIN + 144 : MAIN + 224, :].astype(F32)
-        lane = lane_of((80, LANES))
-
-        def widen(j, carry):
-            parts = []
-            for k in range(SPAN):
-                i = j * SPAN + k
-                near[i, 7:8, :] = edge[0, pl.ds(i, 1), :]
-                near[i, 72:73, :] = edge[1, pl.ds(i, 1), :]
-                here = lane == i
-                parts.append(
-                    jnp.concatenate(
-                        [
-                            near[i].astype(BF16),
-                            jnp.where(here, face_p, 0.0).astype(BF16),
-                            jnp.where(here, face_q, 0.0).astype(BF16),
-                        ],
-                        axis=1,
-                    )
-                )
-            got = jnp.dot(jnp.concatenate(parts, axis=0), turn[...], preferred_element_type=F32)
-            got = got.reshape(SPAN, 80, 256)
-            up[pl.ds(j * SPAN, SPAN)] = got[:, :, :LANES]
-            down[pl.ds(j * SPAN, SPAN)] = got[:, :, LANES:]
-            return carry
-
-        lax.fori_loop(0, 66 // SPAN, widen, 0)
+        widen(0, 2)
+
+    for start in range(0, XC, SPAN):
+        widen(chunk * XC + 2 + start, SPAN)
 
     def planes(j, carry):
         for tile in range(8):
@@ -336,8 +317,8 @@
     lax.fori_loop(0, XC // 4, planes, 0)
 
 
-def warp(table, tab, t, received, fixed, field):
-    rows = received.shape[2]
+def warp(table, tab, t, own, far, fixed, field):
+    rows = own.shape[1]
     tile_x = fixed.shape[0]
     block = pl.BlockSpec((XC, BLK, LANES), lambda b, c, r: (c, b, 0))
     return pl.pallas_call(
@@ -347,6 +328,7 @@
             num_scalar_prefetch=1,
             grid=(2, tile_x // XC),
             in_specs=[
+                pl.BlockSpec(memory_space=pl.ANY),
                 pl.BlockSpec(memory_space=pl.ANY),
                 block,
                 pl.BlockSpec((3, XC, BLK, LANES), lambda b, c, r: (0, c, b, 0)),
@@ -363,7 +345,7 @@
         compiler_params=pltpu.CompilerParams(vmem_limit_bytes=LIMIT),
         cost_estimate=pl.CostEstimate(flops=60 << 20, bytes_accessed=22 << 20, transcendentals=0),
         name="warp",
-    )(tab, received, fixed, field)
+    )(tab, own, far, fixed, field)
 
 
 def put_planes(is_warped, g, count, start, total, diff, value, value_y, fixed, fixed_y):
@@ -419,7 +401,7 @@
                 summed[c, base + i, r - 8 : r, :] = value
         return carry
 
-    lax.fori_loop(0, count, step, 0)
+    lax.fori_loop(0, count, step, 0, unroll=4)
 
 
 def smooth_planes(before, after, summed, along, wide, weights, out):
@@ -440,23 +422,21 @@
                 along[c, o, r, :] = tap_sum(planes[o : o + 2 * RADIUS + 1])
         return carry
 
-    lax.fori_loop(0, 18, rows, 0)
-
-    def plane(o, carry):
+    lax.fori_loop(0, 18, rows, 0, unroll=2)
+
+    for o in range(CH):
+        lhs = wide.at[o]
         for c in range(3):
             for t in range(8):
                 r = 16 * t + 4
                 acc = tap_sum([along[c, o, r + k : r + k + 16, :] for k in range(2 * RADIUS + 1)])
                 high = acc.astype(BF16)
-                wide[c * 128 + 16 * t : c * 128 + 16 * t + 16, 0:LANES] = high
-                wide[c * 128 + 16 * t : c * 128 + 16 * t + 16, LANES:] = (acc - high.astype(F32)).astype(BF16)
-        got = jnp.dot(wide[...], weights[...], preferred_element_type=F32)
+                lhs[c * 128 + 16 * t : c * 128 + 16 * t + 16, 0:LANES] = high
+                lhs[c * 128 + 16 * t : c * 128 + 16 * t + 16, LANES:] = (acc - high.astype(F32)).astype(BF16)
+        got = jnp.dot(lhs[...], weights[...], preferred_element_type=F32)
         for c in range(3):
             part = got[c * 128 : c * 128 + 128]
             out[c, o] = part[:, :LANES] + part[:, LANES:]
-        return carry
-
-    lax.fori_loop(0, CH, plane, 0)
 
 
 def scratch(planes):
@@ -465,7 +445,7 @@
         pltpu.VMEM((planes, 160, LANES), F32),
         pltpu.VMEM((3, 16, 144, LANES), F32),
         pltpu.VMEM((3, CH, 144, LANES), F32),
-        pltpu.VMEM((384, 256), BF16),
+        pltpu.VMEM((CH, 384, 256), BF16),
     ]
 
 
@@ -623,11 +603,15 @@
     )(tab, *args)
 
 
-def swap_y(value, g, rows):
-    length = value.shape[-2]
-    first = lax.slice_in_dim(value, 0, rows, axis=value.ndim - 2)
-    last = lax.slice_in_dim(value, length - rows, length, axis=value.ndim - 2)
-    return lax.ppermute(jnp.where(g == 0, last, first), "gy", [(0, 1), (1, 0)])
+def swap_y(values, g, rows):
+    def edge(value):
+        axis, length = value.ndim - 2, value.shape[-2]
+        first = lax.slice_in_dim(value, 0, rows, axis=axis)
+        last = lax.slice_in_dim(value, length - rows, length, axis=axis)
+        return jnp.where(g == 0, last, first)
+
+    edges = [edge(value) for value in values]
+    return lax.ppermute(jnp.concatenate(edges) if len(edges) > 1 else edges[0], "gy", [(0, 1), (1, 0)])
 
 
 def shift_x(value, value_y, width):
@@ -733,40 +717,45 @@
         return lax.all_to_all(slots, "gx", split_axis=0, concat_axis=0, axis_index_groups=halves, tiled=True)
 
     tile_x = fixed.shape[0]
-    mirror_a = lax.ppermute(moving[:PART], "gx", opposite)
+    hold = lax.optimization_barrier
     up = [(i, i + 1) for i in range(n - 1)]
     low = lax.ppermute(moving[-1:], "gx", up)
     high = lax.ppermute(moving[:1], "gx", [(j, i) for i, j in up])
-    rest, low, high = lax.optimization_barrier((moving[PART:], low, high))
-    mirror_b = lax.ppermute(rest, "gx", opposite)
-    own0 = send(pack(table, tab, 0, False, [moving]))
-    rows_y = swap_y(jnp.concatenate([fixed, low, moving, high]), g, 16)
-    fixed_y, moving_y = rows_y[:tile_x], rows_y[tile_x:]
-    fixed_x = shift_x(fixed, fixed_y, 5)
+    rows_y = swap_y([fixed, moving], g, 16)
+    own0 = pack(table, tab, 0, False, [moving])
+    first, low, high, rows_y, own0 = hold((moving, low, high, rows_y, own0))
+
+    mirror_a = lax.ppermute(first[:PART], "gx", opposite)
+    own0 = send(own0)
+    rows_x = swap_y([low, high], g, 16)
+    fixed_y = rows_y[:tile_x]
+    moving_y = jnp.concatenate([rows_x[:1], rows_y[tile_x:], rows_x[1:]])
     column = columns(table, tab, low, moving, high, moving_y)
     shells = shell_rows(low, moving, high, moving_y, column, g)
+    own1 = pack(table, tab, 1, False, [moving], shells)
+    mirror_a, own0, own1, shells, rest = hold((mirror_a, own0, own1, shells, first[PART:]))
+
+    mirror_b = lax.ppermute(rest, "gx", opposite)
     shells_far = lax.ppermute(shells, "gx", opposite)
-    slots1 = pack(table, tab, 1, False, [moving], shells)
-    far0_a = send(pack(table, tab, 0, True, [mirror_a]))
-    mirror_b, own0, far0_a, shells_far, slots1, fixed_x = lax.optimization_barrier(
-        (mirror_b, own0, far0_a, shells_far, slots1, fixed_x)
-    )
-
-    far0_b = send(pack(table, tab, 0, True, [mirror_b]))
-    slots1 = pack(table, tab, 1, True, [mirror_a, mirror_b], shells_far, slots1)
-    far0_b, slots1 = lax.optimization_barrier((far0_b, slots1))
-    slots1 = send(slots1)
-
-    warped = pick(table, tab, 0, own0, (far0_a, far0_b), fixed.shape)
-    warped_y = swap_y(warped, g, 16)
+    own1 = send(own1)
+    fixed_x = shift_x(fixed, fixed_y, 5)
+    mirror_b, shells_far, own1 = hold((mirror_b, shells_far, own1))
+
+    far0 = send(pack(table, tab, 0, True, [mirror_a, mirror_b]))
+    far1 = pack(table, tab, 1, True, [mirror_a, mirror_b], shells_far)
+    _, far1 = hold((far0, far1))
+    far1 = send(far1)
+
+    warped = pick(table, tab, 0, own0, far0, fixed.shape)
+    warped_y = swap_y([warped], g, 16)
     warped_x = shift_x(warped, warped_y, 5)
     field = inner(table, tab, weights, warped, warped_y, fixed, fixed_y)
     field = rim(table, tab, weights, field, warped, warped_y, fixed, fixed_y, (*warped_x, *fixed_x))
-    field_y = swap_y(field, g, 8)
+    field_y = swap_y([field], g, 8)
     field_x = shift_x(field, field_y, 4)
 
-    mismatch = warp(table, tab, 1, slots1, fixed, field)
-    mismatch_y = swap_y(mismatch, g, 8)
+    mismatch = warp(table, tab, 1, own1, far1, fixed, field)
+    mismatch_y = swap_y([mismatch], g, 8)
     mismatch_x = shift_x(mismatch, mismatch_y, 5)
     last = inner(table, tab, weights, mismatch, mismatch_y, fixed, fixed_y, field, field_y)
     last = rim(

time: 331 us -> 313 us (0.946)
  Pallas kernels: 150 us -> 116 us
  waiting for transfers between devices: 76.3 us -> 102 us
  local copies, waits for them, and re-layouts: 29.3 us -> 21 us
    ppermute x1, waiting for transfers between devices: 0.01 us -> 50.1 us  [local(): shells_far = lax.ppermute(shells, 'gx', opposite)]
    ppermute x4, waiting for transfers between devices: 34 us -> 5.98 us  [shift_x(): lax.ppermute(part(length - width), 'gx', up)]
    pallas_call x2, Pallas kernels: 64.2 us -> 44.3 us  [inner(): pl.pallas_call(functools.partial(inner_body, table, is_warped), out_shape...]
    all_to_all x4, waiting for transfers between devices: 6.8 us -> 18 us  [send(): lax.all_to_all(slots, 'gx', split_axis=0, concat_axis=0, axis_index_group...]
    pallas_call x2, Pallas kernels: 30.5 us -> 22.6 us  [rim(): pl.pallas_call(functools.partial(rim_body, table, is_warped), out_shape=j...]
    ppermute x5 -> x6, waiting for transfers between devices: 33.4 us -> 28.3 us  [the longest x1 28.3 us: local(): mirror_a = lax.ppermute(first[:PART], 'gx', opposite)]
    ppermute x5 -> x6, starting transfers between devices: 8.58 us -> 3.88 us  [the longest x5 3.82 us: swap_y(): lax.ppermute(jnp.concatenate(edges) if len(edges) > 1 else edges[0], 'gy'...]
    slice x3, local copies, waits for them, and re-layouts: 6.08 us -> 1.87 us  [the longest x1 1.13 us: local(): first[PART:]]
  transfers between devices with their start and end apart: 21 -> 22, of which waited for: 7 -> 4; matrix products, arithmetic and copies ran while one was open for 9% -> 6% of each run, Pallas kernels for 40% -> 32%
where the time goes in v3:
time: 313 us; the launch traced here: 311 us
  Pallas kernels  116 us (37%)
  waiting for transfers between devices  102 us (33%)
  starting transfers between devices  61.5 us (20%)
  local copies, waits for them, and re-layouts  21 us (7%)
  other arithmetic  9.23 us (3%)
    ppermute x1, waiting for transfers between devices, local(): shells_far = lax.ppermute(shells, 'gx', opposite)  50.1 us
    pallas_call x2, Pallas kernels, inner(): pl.pallas_call(functools.partial(inner_body, table, is_warped), out_shape...  44.3 us
    ppermute x1, waiting for transfers between devices, local(): mirror_a = lax.ppermute(first[:PART], 'gx', opposite)  28.3 us
    all_to_all x4, starting transfers between devices, send(): lax.all_to_all(slots, 'gx', split_axis=0, concat_axis=0, axis_index_group...  24.4 us
    pallas_call x2, Pallas kernels, rim(): pl.pallas_call(functools.partial(rim_body, table, is_warped), out_shape=j...  22.6 us
    pallas_call x4, Pallas kernels, pack(): pl.pallas_call(functools.partial(pack_body, table, t, far, count, shells...  18.3 us
    pallas_call x1, Pallas kernels, warp(): pl.pallas_call(functools.partial(warp_body, table, t), out_shape=jax.Shap...  18 us
    all_to_all x4, waiting for transfers between devices, send(): lax.all_to_all(slots, 'gx', split_axis=0, concat_axis=0, axis_index_group...  18 us
  transfers between devices with their start and end apart: 22, of which 4 were waited for; matrix products, arithmetic and copies ran while one was open for 6% of the time, Pallas kernels for 32%

profile of v3, /device:TPU:23, one launch (start us, length us, event | category | flops | bytes accessed | tf_op | source)
XLA Modules:
  0.0 311.1 jit_solution(6885317630344820127)
XLA Ops:
  3.6 4.0 %collective-permute-start = (bf16[1,128,128]{2,1,0:T(8,128)(2,1)S(1)}, bf16[1,128,128]{2,1,0:T(8,128)(2,1)S(1)}, u32[]{:S(2)}, u32[]{:S(2)}) collective-permute-start(bf16[1,128,128]{2,1,0:T(8,128)(2,1)S(1)} %get-tuple-element.43), channel_id=1, source_target_pairs={{0,2},{2,4},{4,6},{6,8},{8,10},{10,12},{12,14},{1,3},{3,5},{5,7},{... | collective-permute-start | bytes 98312 | tf_op jit(solution)/shard_map/ppermute | solution.py:722
  13.4 4.5 %pack0own.1 = bf16[4,2048,128]{2,1,0:T(8,128)(2,1)} custom-call(s32[258]{0:T(512)} %pad_add_fusion.ref, bf16[64,128,128]{2,1,0:T(8,128)(2,1)} %refs_1_.3, bf16[64,128,128]{2,1,0:T(8,128)(2,1)} %refs_1_.3), custom_call_target="tpu_custom_call" | custom-call | flops 65536 | bytes 65536 | tf_op jit(solution)/shard_map/pack0own/pallas_call | solution.py:121
  18.7 4.6 %all-to-all-start = ((bf16[4,2048,128]{2,1,0:T(8,128)(2,1)}), bf16[4,2048,128]{2,1,0:T(8,128)(2,1)}, u32[]{:S(2)}, u32[]{:S(2)}) async-start(bf16[4,2048,128]{2,1,0:T(8,128)(2,1)} %pack0own.1), calls=%async_computation | async-start | bytes 4194304 | tf_op jit(solution)/shard_map/all_to_all | solution.py:717
  26.3 8.8 %columns.1 = bf16[2,160,128]{2,1,0:T(8,128)(2,1)} custom-call(s32[258]{0:T(512)} %pad_add_fusion.ref, bf16[1,128,128]{2,1,0:T(8,128)(2,1)} %copy-done.16, bf16[64,128,128]{2,1,0:T(8,128)(2,1)} %refs_1_.3, bf16[1,128,128]{2,1,0:T(8,128)(2,1)} %copy-done.15, bf16[66,16,128]{2,1,0:T(8,128)(2,1)} %copy-done.8), custom_call_target="tpu_custom_call" | custom-call | flops 65536 | bytes 65536 | tf_op jit(solution)/shard_map/columns/pallas_call | solution.py:667
  37.1 4.6 %pack1own.1 = bf16[4,2272,128]{2,1,0:T(8,128)(2,1)} custom-call(s32[258]{0:T(512)} %pad_add_fusion.ref, bf16[64,128,128]{2,1,0:T(8,128)(2,1)} %refs_1_.3, bf16[64,128,128]{2,1,0:T(8,128)(2,1)} %refs_1_.3, bf16[4,224,128]{2,1,0:T(8,128)(2,1)} %pad_maximum_fusion.6.refs_2_), custom_call_target="tpu_custom_call" | custom-call | flops 65536 | bytes 65536 | tf_op jit(solution)/shard_map/pack1own/pallas_call | solution.py:121
  41.6 28.3 %collective-permute-done.3.refs_0_ = bf16[32,128,128]{2,1,0:T(8,128)(2,1)S(1)} collective-permute-done((bf16[32,128,128]{2,1,0:T(8,128)(2,1)S(1)}, bf16[32,128,128]{2,1,0:T(8,128)(2,1)S(1)}, u32[]{:S(2)}, u32[]{:S(2)}) %collective-permute-start.3) | collective-permute-done | bytes 1048608 | tf_op jit(solution)/shard_map/ppermute | solution.py:728
  70.9 6.7 %all-to-all-start.1 = ((bf16[4,2272,128]{2,1,0:T(8,128)(2,1)}), bf16[4,2272,128]{2,1,0:T(8,128)(2,1)S(1)}, u32[]{:S(2)}, u32[]{:S(2)}) async-start(bf16[4,2272,128]{2,1,0:T(8,128)(2,1)} %pack1own.1), calls=%async_computation.1 | async-start | bytes 4653056 | tf_op jit(solution)/shard_map/all_to_all | solution.py:717
  80.0 50.1 %collective-permute-done.6.refs_2_ = bf16[4,224,128]{2,1,0:T(8,128)(2,1)S(1)} collective-permute-done((bf16[4,224,128]{2,1,0:T(8,128)(2,1)}, bf16[4,224,128]{2,1,0:T(8,128)(2,1)S(1)}, u32[]{:S(2)}, u32[]{:S(2)}) %collective-permute-start.6) | collective-permute-done | bytes 229408 | tf_op jit(solution)/shard_map/ppermute | solution.py:739
  131.8 4.6 %pack0far.1 = bf16[4,2048,128]{2,1,0:T(8,128)(2,1)} custom-call(s32[258]{0:T(512)} %pad_add_fusion.ref, bf16[32,128,128]{2,1,0:T(8,128)(2,1)} %copy-done.4, bf16[32,128,128]{2,1,0:T(8,128)(2,1)} %copy-done.5), custom_call_target="tpu_custom_call" | custom-call | flops 65536 | bytes 65536 | tf_op jit(solution)/shard_map/pack0far/pallas_call | solution.py:121
  136.4 7.8 %all-to-all-start.2 = ((bf16[4,2048,128]{2,1,0:T(8,128)(2,1)}), bf16[4,2048,128]{2,1,0:T(8,128)(2,1)S(1)}, u32[]{:S(2)}, u32[]{:S(2)}) async-start(bf16[4,2048,128]{2,1,0:T(8,128)(2,1)} %pack0far.1), calls=%async_computation.2 | async-start | bytes 4194304 | tf_op jit(solution)/shard_map/all_to_all | solution.py:717
  144.2 4.6 %pack1far.1 = bf16[4,2272,128]{2,1,0:T(8,128)(2,1)} custom-call(s32[258]{0:T(512)} %pad_add_fusion.ref, bf16[32,128,128]{2,1,0:T(8,128)(2,1)} %copy-done.4, bf16[32,128,128]{2,1,0:T(8,128)(2,1)} %copy-done.5, bf16[4,224,128]{2,1,0:T(8,128)(2,1)} %copy-done.19), custom_call_target="tpu_custom_call" | custom-call | flops 134217728 | bytes 134217728 | tf_op jit(solution)/shard_map/pack1far/pallas_call | solution.py:121
  148.8 18.0 %all-to-all-done.2.far_ref = bf16[4,2048,128]{2,1,0:T(8,128)(2,1)S(1)} async-done(((bf16[4,2048,128]{2,1,0:T(8,128)(2,1)}), bf16[4,2048,128]{2,1,0:T(8,128)(2,1)S(1)}, u32[]{:S(2)}, u32[]{:S(2)}) %all-to-all-start.2) | async-done | bytes 2097184 | tf_op jit(solution)/shard_map/all_to_all | solution.py:717
  168.1 5.3 %all-to-all-start.3 = ((bf16[4,2272,128]{2,1,0:T(8,128)(2,1)}), bf16[4,2272,128]{2,1,0:T(8,128)(2,1)S(1)}, u32[]{:S(2)}, u32[]{:S(2)}) async-start(bf16[4,2272,128]{2,1,0:T(8,128)(2,1)} %pack1far.1), calls=%async_computation.3 | async-start | bytes 4653056 | tf_op jit(solution)/shard_map/all_to_all | solution.py:717
  175.2 3.8 %collective-permute-start.10 = (bf16[5,144,128]{2,1,0:T(8,128)(2,1)S(1)}, bf16[5,144,128]{2,1,0:T(8,128)(2,1)S(1)}, u32[]{:S(2)}, u32[]{:S(2)}) collective-permute-start(bf16[5,144,128]{2,1,0:T(8,128)(2,1)S(1)} %pad_maximum_fusion.9), channel_id=1, source_target_pairs={{0,2},{2,4},{4,6},{6,8},{8,10},{10,12},{12,14},{1,3},{3,5},{5,7},{... | collective-permute-start | bytes 552968 | tf_op jit(solution)/shard_map/ppermute | solution.py:629
  179.1 3.9 %pick.1.value = bf16[64,128,128]{2,1,0:T(8,128)(2,1)} custom-call(s32[258]{0:T(512)} %pad_add_fusion.ref, bf16[4,2048,128]{2,1,0:T(8,128)(2,1)} %all-to-all-done.own_ref, bf16[4,2048,128]{2,1,0:T(8,128)(2,1)} %copy-done.3), custom_call_target="tpu_custom_call" | custom-call | flops 2097152 | bytes 4194304 | tf_op jit(solution)/shard_map/pick/pallas_call | solution.py:195
  188.8 4.0 %collective-permute-start.8 = (bf16[5,144,128]{2,1,0:T(8,128)(2,1)S(1)}, bf16[5,144,128]{2,1,0:T(8,128)(2,1)S(1)}, u32[]{:S(2)}, u32[]{:S(2)}) collective-permute-start(bf16[5,144,128]{2,1,0:T(8,128)(2,1)S(1)} %pad_maximum_fusion.7), channel_id=1, source_target_pairs={{0,2},{2,4},{4,6},{6,8},{8,10},{10,12},{12,14},{1,3},{3,5},{5,7},{... | collective-permute-start | bytes 552968 | tf_op jit(solution)/shard_map/ppermute | solution.py:629
  194.7 21.6 %inner0.1.refs_4_ = f32[3,64,128,128]{3,2,1,0:T(8,128)} custom-call(s32[258]{0:T(512)} %pad_add_fusion.ref, bf16[256,256]{1,0:T(8,128)(2,1)} %constant.30.weights, bf16[64,128,128]{2,1,0:T(8,128)(2,1)} %pick.1.value, bf16[64,16,128]{2,1,0:T(8,128)(2,1)} %copy-done.10, bf16[64,128,128]{2,1,0:T(8,128)(2,1)} %fixed.9, ...), custom_call_target="tpu_custom_call" | custom-call | flops 209715200 | bytes 31457280 | tf_op jit(solution)/shard_map/inner0/pallas_call | solution.py:490
  217.8 10.4 %rim0.1.field.refs_0_.refs_4_ = f32[3,64,128,128]{3,2,1,0:T(8,128)} custom-call(s32[258]{0:T(512)} %pad_add_fusion.ref, bf16[256,256]{1,0:T(8,128)(2,1)} %constant.30.weights, bf16[64,128,128]{2,1,0:T(8,128)(2,1)} %pick.1.value, bf16[64,16,128]{2,1,0:T(8,128)(2,1)} %copy-done.10, bf16[64,128,128]{2,1,0:T(8,128)(2,1)} %fixed.9, ...), custom_call_target="tpu_custom_call", output_to_operand_aliasing={{}: (10, {})} | custom-call | flops 62914560 | bytes 10485760 | tf_op jit(solution)/shard_map/rim0/pallas_call | solution.py:589
  233.8 4.5 %collective-permute-start.16 = (f32[3,4,136,128]{3,2,1,0:T(8,128)}, f32[3,4,136,128]{3,2,1,0:T(8,128)}, u32[]{:S(2)}, u32[]{:S(2)}) collective-permute-start(f32[3,4,136,128]{3,2,1,0:T(8,128)} %pad_maximum_fusion), channel_id=1, source_target_pairs={{0,2},{2,4},{4,6},{6,8},{8,10},{10,12},{12,14},{1,3},{3,5},{5,7},{... | collective-permute-start | bytes 2506760 | tf_op jit(solution)/shard_map/ppermute | solution.py:629
  239.7 18.0 %warp.1.value = f32[64,128,128]{2,1,0:T(8,128)} custom-call(s32[258]{0:T(512)} %pad_add_fusion.ref, bf16[4,2272,128]{2,1,0:T(8,128)(2,1)} %copy-done.1, bf16[4,2272,128]{2,1,0:T(8,128)(2,1)} %copy-done.2, bf16[64,128,128]{2,1,0:T(8,128)(2,1)} %fixed.9, f32[3,64,128,128]{3,2,1,0:T(8,128)} %rim0.1.field.refs_0_.refs_4_), custom_call_target="tpu_custom_call" | custom-call | flops 62914560 | bytes 23068672 | tf_op jit(solution)/shard_map/warp/pallas_call | solution.py:324
  262.3 4.3 %collective-permute-start.13 = (f32[5,136,128]{2,1,0:T(8,128)S(1)}, f32[5,136,128]{2,1,0:T(8,128)S(1)}, u32[]{:S(2)}, u32[]{:S(2)}) collective-permute-start(f32[5,136,128]{2,1,0:T(8,128)S(1)} %pad_maximum_fusion.3), channel_id=1, source_target_pairs={{0,2},{2,4},{4,6},{6,8},{8,10},{10,12},{12,14},{1,3},{3,5},{5,7},{... | collective-permute-start | bytes 1044488 | tf_op jit(solution)/shard_map/ppermute | solution.py:629
  268.7 22.7 %inner1.1.refs_8_ = f32[3,64,128,128]{3,2,1,0:T(8,128)} custom-call(s32[258]{0:T(512)} %pad_add_fusion.ref, bf16[256,256]{1,0:T(8,128)(2,1)} %constant.30.weights, f32[64,128,128]{2,1,0:T(8,128)} %warp.1.value, f32[64,8,128]{2,1,0:T(8,128)} %copy-done.9, bf16[64,128,128]{2,1,0:T(8,128)(2,1)} %fixed.9, bf16[64,16,128]{2,1,0:T(8,128)(2,1)} %get-tuple-element.48.fixed_y, ...), custom_call_target="tpu_custom_call" | custom-call | flops 209715200 | bytes 31457280 | tf_op jit(solution)/shard_map/inner1/pallas_call | solution.py:490
  291.5 6.0 %collective-permute-done.13.refs_0_ = f32[5,136,128]{2,1,0:T(8,128)S(1)} collective-permute-done((f32[5,136,128]{2,1,0:T(8,128)S(1)}, f32[5,136,128]{2,1,0:T(8,128)S(1)}, u32[]{:S(2)}, u32[]{:S(2)}) %collective-permute-start.13) | collective-permute-done | bytes 348192 | tf_op jit(solution)/shard_map/ppermute | solution.py:629
  298.9 12.2 %rim1.1 = f32[3,64,128,128]{3,2,1,0:T(8,128)} custom-call(s32[258]{0:T(512)} %pad_add_fusion.ref, bf16[256,256]{1,0:T(8,128)(2,1)} %constant.30.weights, f32[64,128,128]{2,1,0:T(8,128)} %warp.1.value, f32[64,8,128]{2,1,0:T(8,128)} %copy-done.9, bf16[64,128,128]{2,1,0:T(8,128)(2,1)} %fixed.9, ...), custom_call_target="tpu_custom_call", output_to_operand_aliasing={{}: (14, {})} | custom-call | flops 62914560 | bytes 10485760 | tf_op jit(solution)/shard_map/rim1/pallas_call | solution.py:589
  (138 shorter events, 46.7 us)
Async XLA Ops:
  1.4 16.5 %collective-permute-start.1 = (bf16[1,128,128]{2,1,0:T(8,128)(2,1)S(1)}, bf16[1,128,128]{2,1,0:T(8,128)(2,1)S(1)}, u32[]{:S(2)}, u32[]{:S(2)}) collective-permute-start(bf16[1,128,128]{2,1,0:T(8,128)(2,1)S(1)} %get-tuple-element.42), channel_id=1, source_target_pairs={{2,0},{4,2},{6,4},{8,6},{10,8},{12,10},{14,12},{3,1},{5,3},{7,5},{... | collective-permute-start | bytes 98312 | tf_op jit(solution)/shard_map/ppermute | solution.py:723
  3.6 14.4 %collective-permute-start = (bf16[1,128,128]{2,1,0:T(8,128)(2,1)S(1)}, bf16[1,128,128]{2,1,0:T(8,128)(2,1)S(1)}, u32[]{:S(2)}, u32[]{:S(2)}) collective-permute-start(bf16[1,128,128]{2,1,0:T(8,128)(2,1)S(1)} %get-tuple-element.43), channel_id=1, source_target_pairs={{0,2},{2,4},{4,6},{6,8},{8,10},{10,12},{12,14},{1,3},{3,5},{5,7},{... | collective-permute-start | bytes 98312 | tf_op jit(solution)/shard_map/ppermute | solution.py:722
  9.9 8.1 %collective-permute-start.2 = (bf16[128,16,128]{2,1,0:T(8,128)(2,1)S(1)}, bf16[128,16,128]{2,1,0:T(8,128)(2,1)S(1)}, u32[]{:S(2)}, u32[]{:S(2)}) collective-permute-start(bf16[128,16,128]{2,1,0:T(8,128)(2,1)S(1)} %pad_maximum_fusion.2), channel_id=1, source_target_pairs={{0,1},{1,0},{2,3},{3,2},{4,5},{5,4},{6,7},{7,6},{8,9},{9,8},{10,11... | collective-permute-start | bytes 1572872 | tf_op jit(solution)/shard_map/ppermute | solution.py:614
  18.7 51.2 %all-to-all-start = ((bf16[4,2048,128]{2,1,0:T(8,128)(2,1)}), bf16[4,2048,128]{2,1,0:T(8,128)(2,1)}, u32[]{:S(2)}, u32[]{:S(2)}) async-start(bf16[4,2048,128]{2,1,0:T(8,128)(2,1)} %pack0own.1), calls=%async_computation | async-start | bytes 4194304 | tf_op jit(solution)/shard_map/all_to_all | solution.py:717
  23.3 2.2 collective-permute-start.4
  25.4 44.5 %collective-permute-start.3 = (bf16[32,128,128]{2,1,0:T(8,128)(2,1)S(1)}, bf16[32,128,128]{2,1,0:T(8,128)(2,1)S(1)}, u32[]{:S(2)}, u32[]{:S(2)}) collective-permute-start(bf16[32,128,128]{2,1,0:T(8,128)(2,1)S(1)} %get-tuple-element.39), channel_id=1, source_target_pairs={{0,8},{2,10},{4,12},{6,14},{8,0},{10,2},{12,4},{14,6},{1,9},{3,11}... | collective-permute-start | bytes 3145736 | tf_op jit(solution)/shard_map/ppermute | solution.py:728
  70.9 59.9 %all-to-all-start.1 = ((bf16[4,2272,128]{2,1,0:T(8,128)(2,1)}), bf16[4,2272,128]{2,1,0:T(8,128)(2,1)S(1)}, u32[]{:S(2)}, u32[]{:S(2)}) async-start(bf16[4,2272,128]{2,1,0:T(8,128)(2,1)} %pack1own.1), calls=%async_computation.1 | async-start | bytes 4653056 | tf_op jit(solution)/shard_map/all_to_all | solution.py:717
  77.6 53.2 %collective-permute-start.5 = (bf16[32,128,128]{2,1,0:T(8,128)(2,1)}, bf16[32,128,128]{2,1,0:T(8,128)(2,1)S(1)}, u32[]{:S(2)}, u32[]{:S(2)}) collective-permute-start(bf16[32,128,128]{2,1,0:T(8,128)(2,1)} %get-tuple-element.21), channel_id=1, source_target_pairs={{0,8},{2,10},{4,12},{6,14},{8,0},{10,2},{12,4},{14,6},{1,9},{3,11}... | collective-permute-start | bytes 3145736 | tf_op jit(solution)/shard_map/ppermute | solution.py:738
  77.9 52.2 %collective-permute-start.6 = (bf16[4,224,128]{2,1,0:T(8,128)(2,1)}, bf16[4,224,128]{2,1,0:T(8,128)(2,1)S(1)}, u32[]{:S(2)}, u32[]{:S(2)}) collective-permute-start(bf16[4,224,128]{2,1,0:T(8,128)(2,1)} %pad_maximum_fusion.6.refs_2_), channel_id=1, source_target_pairs={{0,8},{2,10},{4,12},{6,14},{8,0},{10,2},{12,4},{14,6},{1,9},{3,11}... | collective-permute-start | bytes 688136 | tf_op jit(solution)/shard_map/ppermute | solution.py:739
  136.4 30.4 %all-to-all-start.2 = ((bf16[4,2048,128]{2,1,0:T(8,128)(2,1)}), bf16[4,2048,128]{2,1,0:T(8,128)(2,1)S(1)}, u32[]{:S(2)}, u32[]{:S(2)}) async-start(bf16[4,2048,128]{2,1,0:T(8,128)(2,1)} %pack0far.1), calls=%async_computation.2 | async-start | bytes 4194304 | tf_op jit(solution)/shard_map/all_to_all | solution.py:717
  168.1 70.2 %all-to-all-start.3 = ((bf16[4,2272,128]{2,1,0:T(8,128)(2,1)}), bf16[4,2272,128]{2,1,0:T(8,128)(2,1)S(1)}, u32[]{:S(2)}, u32[]{:S(2)}) async-start(bf16[4,2272,128]{2,1,0:T(8,128)(2,1)} %pack1far.1), calls=%async_computation.3 | async-start | bytes 4653056 | tf_op jit(solution)/shard_map/all_to_all | solution.py:717
  175.2 41.0 %collective-permute-start.10 = (bf16[5,144,128]{2,1,0:T(8,128)(2,1)S(1)}, bf16[5,144,128]{2,1,0:T(8,128)(2,1)S(1)}, u32[]{:S(2)}, u32[]{:S(2)}) collective-permute-start(bf16[5,144,128]{2,1,0:T(8,128)(2,1)S(1)} %pad_maximum_fusion.9), channel_id=1, source_target_pairs={{0,2},{2,4},{4,6},{6,8},{8,10},{10,12},{12,14},{1,3},{3,5},{5,7},{... | collective-permute-start | bytes 552968 | tf_op jit(solution)/shard_map/ppermute | solution.py:629
  184.0 4.7 %collective-permute-start.7 = (bf16[64,16,128]{2,1,0:T(8,128)(2,1)S(1)}, bf16[64,16,128]{2,1,0:T(8,128)(2,1)S(1)}, u32[]{:S(2)}, u32[]{:S(2)}) collective-permute-start(bf16[64,16,128]{2,1,0:T(8,128)(2,1)S(1)} %slice_select_fusion.2), channel_id=1, source_target_pairs={{0,1},{1,0},{2,3},{3,2},{4,5},{5,4},{6,7},{7,6},{8,9},{9,8},{10,11... | collective-permute-start | bytes 786440 | tf_op jit(solution)/shard_map/ppermute | solution.py:614
  185.5 30.8 %collective-permute-start.11 = (bf16[5,144,128]{2,1,0:T(8,128)(2,1)S(1)}, bf16[5,144,128]{2,1,0:T(8,128)(2,1)S(1)}, u32[]{:S(2)}, u32[]{:S(2)}) collective-permute-start(bf16[5,144,128]{2,1,0:T(8,128)(2,1)S(1)} %pad_maximum_fusion.10), channel_id=1, source_target_pairs={{2,0},{4,2},{6,4},{8,6},{10,8},{12,10},{14,12},{3,1},{5,3},{7,5},{... | collective-permute-start | bytes 552968 | tf_op jit(solution)/shard_map/ppermute | solution.py:629
  188.8 27.5 %collective-permute-start.8 = (bf16[5,144,128]{2,1,0:T(8,128)(2,1)S(1)}, bf16[5,144,128]{2,1,0:T(8,128)(2,1)S(1)}, u32[]{:S(2)}, u32[]{:S(2)}) collective-permute-start(bf16[5,144,128]{2,1,0:T(8,128)(2,1)S(1)} %pad_maximum_fusion.7), channel_id=1, source_target_pairs={{0,2},{2,4},{4,6},{6,8},{8,10},{10,12},{12,14},{1,3},{3,5},{5,7},{... | collective-permute-start | bytes 552968 | tf_op jit(solution)/shard_map/ppermute | solution.py:629
  192.8 23.5 %collective-permute-start.9 = (bf16[5,144,128]{2,1,0:T(8,128)(2,1)S(1)}, bf16[5,144,128]{2,1,0:T(8,128)(2,1)S(1)}, u32[]{:S(2)}, u32[]{:S(2)}) collective-permute-start(bf16[5,144,128]{2,1,0:T(8,128)(2,1)S(1)} %pad_maximum_fusion.8), channel_id=1, source_target_pairs={{2,0},{4,2},{6,4},{8,6},{10,8},{12,10},{14,12},{3,1},{5,3},{7,5},{... | collective-permute-start | bytes 552968 | tf_op jit(solution)/shard_map/ppermute | solution.py:629
  229.7 3.0 collective-permute-start.15
  232.7 25.0 %copy-start.6 = (f32[3,64,8,128]{3,2,1,0:T(8,128)}, f32[3,64,8,128]{3,2,1,0:T(8,128)S(1)}, u32[]{:S(2)}) copy-start(f32[3,64,8,128]{3,2,1,0:T(8,128)S(1)} %collective-permute-done.15.refs_1_.refs_5_) | copy-start | bytes 2359300
  233.8 57.7 %collective-permute-start.16 = (f32[3,4,136,128]{3,2,1,0:T(8,128)}, f32[3,4,136,128]{3,2,1,0:T(8,128)}, u32[]{:S(2)}, u32[]{:S(2)}) collective-permute-start(f32[3,4,136,128]{3,2,1,0:T(8,128)} %pad_maximum_fusion), channel_id=1, source_target_pairs={{0,2},{2,4},{4,6},{6,8},{8,10},{10,12},{12,14},{1,3},{3,5},{5,7},{... | collective-permute-start | bytes 2506760 | tf_op jit(solution)/shard_map/ppermute | solution.py:629
  239.7 19.4 %copy-start.7 = (f32[3,4,128,128]{3,2,1,0:T(8,128)S(1)}, f32[3,4,128,128]{3,2,1,0:T(8,128)}, u32[]{:S(2)}) copy-start(f32[3,4,128,128]{3,2,1,0:T(8,128)} %get-tuple-element.30) | copy-start | bytes 2359300
  258.8 3.5 %collective-permute-start.12 = (f32[64,8,128]{2,1,0:T(8,128)S(1)}, f32[64,8,128]{2,1,0:T(8,128)S(1)}, u32[]{:S(2)}, u32[]{:S(2)}) collective-permute-start(f32[64,8,128]{2,1,0:T(8,128)S(1)} %slice_select_fusion.1), channel_id=1, source_target_pairs={{0,1},{1,0},{2,3},{3,2},{4,5},{5,4},{6,7},{7,6},{8,9},{9,8},{10,11... | collective-permute-start | bytes 786440 | tf_op jit(solution)/shard_map/ppermute | solution.py:614
  259.2 32.3 %collective-permute-start.17 = (f32[3,4,136,128]{3,2,1,0:T(8,128)S(1)}, f32[3,4,136,128]{3,2,1,0:T(8,128)S(1)}, u32[]{:S(2)}, u32[]{:S(2)}) collective-permute-start(f32[3,4,136,128]{3,2,1,0:T(8,128)S(1)} %pad_maximum_fusion.1), channel_id=1, source_target_pairs={{2,0},{4,2},{6,4},{8,6},{10,8},{12,10},{14,12},{3,1},{5,3},{7,5},{... | collective-permute-start | bytes 2506760 | tf_op jit(solution)/shard_map/ppermute | solution.py:629
  262.3 35.1 %collective-permute-start.13 = (f32[5,136,128]{2,1,0:T(8,128)S(1)}, f32[5,136,128]{2,1,0:T(8,128)S(1)}, u32[]{:S(2)}, u32[]{:S(2)}) collective-permute-start(f32[5,136,128]{2,1,0:T(8,128)S(1)} %pad_maximum_fusion.3), channel_id=1, source_target_pairs={{0,2},{2,4},{4,6},{6,8},{8,10},{10,12},{12,14},{1,3},{3,5},{5,7},{... | collective-permute-start | bytes 1044488 | tf_op jit(solution)/shard_map/ppermute | solution.py:629
  266.6 30.8 %collective-permute-start.14 = (f32[5,136,128]{2,1,0:T(8,128)S(1)}, f32[5,136,128]{2,1,0:T(8,128)S(1)}, u32[]{:S(2)}, u32[]{:S(2)}) collective-permute-start(f32[5,136,128]{2,1,0:T(8,128)S(1)} %pad_maximum_fusion.4), channel_id=1, source_target_pairs={{2,0},{4,2},{6,4},{8,6},{10,8},{12,10},{14,12},{3,1},{5,3},{7,5},{... | collective-permute-start | bytes 1044488 | tf_op jit(solution)/shard_map/ppermute | solution.py:629
  (23 other events, 78.0 us)

commit v4 on v3

--- a/solution.py
+++ b/solution.py
@@ -517,8 +517,8 @@
     put_planes(is_warped, g, 13, 5 * (1 - k), total, diff, value, value_y, fixed, fixed_y)
 
     def side(at, value_x, fixed_x):
-        v_main, v_y = value_x.at[:, :128, :], value_x.at[:, 128:, :]
-        f_main, f_y = fixed_x.at[:, :128, :], fixed_x.at[:, 128:, :]
+        v_main, v_y = value_x.at[:5, :128, :], value_x.at[:5, 128:, :]
+        f_main, f_y = fixed_x.at[5:, :128, :], fixed_x.at[5:, 128:, :]
         put_planes(is_warped, g, 5, at, total, diff, v_main, v_y, f_main, f_y)
 
     @pl.when(k == 0)
@@ -614,19 +614,21 @@
     return lax.ppermute(jnp.concatenate(edges) if len(edges) > 1 else edges[0], "gy", [(0, 1), (1, 0)])
 
 
-def shift_x(value, value_y, width):
+def shift_x(pairs, width):
     size = lax.axis_size("gx")
-    axis = value.ndim - 3
-    length = value.shape[axis]
     up = [(i, i + 1) for i in range(size - 1)]
     down = [(j, i) for i, j in up]
 
-    def part(start):
-        return jnp.concatenate(
-            [lax.slice_in_dim(v, start, start + width, axis=axis) for v in (value, value_y)], axis=value.ndim - 2
-        )
-
-    return lax.ppermute(part(length - width), "gx", up), lax.ppermute(part(0), "gx", down)
+    def part(end):
+        faces = []
+        for pair in pairs:
+            axis = pair[0].ndim - 3
+            start = pair[0].shape[axis] - width if end else 0
+            rows = [lax.slice_in_dim(v, start, start + width, axis=axis) for v in pair]
+            faces.append(jnp.concatenate(rows, axis=axis + 1))
+        return jnp.concatenate(faces) if len(faces) > 1 else faces[0]
+
+    return lax.ppermute(part(True), "gx", up), lax.ppermute(part(False), "gx", down)
 
 
 def column_body(table, ref, low, main, high, rows_y, out):
@@ -738,7 +740,6 @@
     mirror_b = lax.ppermute(rest, "gx", opposite)
     shells_far = lax.ppermute(shells, "gx", opposite)
     own1 = send(own1)
-    fixed_x = shift_x(fixed, fixed_y, 5)
     mirror_b, shells_far, own1 = hold((mirror_b, shells_far, own1))
 
     far0 = send(pack(table, tab, 0, True, [mirror_a, mirror_b]))
@@ -748,18 +749,18 @@
 
     warped = pick(table, tab, 0, own0, far0, fixed.shape)
     warped_y = swap_y([warped], g, 16)
-    warped_x = shift_x(warped, warped_y, 5)
+    faces_x = shift_x([(warped, warped_y), (fixed, fixed_y)], 5)
     field = inner(table, tab, weights, warped, warped_y, fixed, fixed_y)
-    field = rim(table, tab, weights, field, warped, warped_y, fixed, fixed_y, (*warped_x, *fixed_x))
+    field = rim(table, tab, weights, field, warped, warped_y, fixed, fixed_y, (*faces_x, *faces_x))
     field_y = swap_y([field], g, 8)
-    field_x = shift_x(field, field_y, 4)
+    field_x = shift_x([(field, field_y)], 4)
 
     mismatch = warp(table, tab, 1, own1, far1, fixed, field)
     mismatch_y = swap_y([mismatch], g, 8)
-    mismatch_x = shift_x(mismatch, mismatch_y, 5)
+    mismatch_x = shift_x([(mismatch, mismatch_y)], 5)
     last = inner(table, tab, weights, mismatch, mismatch_y, fixed, fixed_y, field, field_y)
     last = rim(
-        table, tab, weights, last, mismatch, mismatch_y, fixed, fixed_y, (*mismatch_x, *fixed_x), field, field_y, field_x
+        table, tab, weights, last, mismatch, mismatch_y, fixed, fixed_y, (*mismatch_x, *faces_x), field, field_y, field_x
     )
     return (last, mismatch)
 

time: 313 us -> 312 us (level)
  starting transfers between devices: 61.5 us -> 55.9 us
  waiting for transfers between devices: 102 us -> 106 us
    ppermute x8 -> x6, starting transfers between devices: 24.7 us -> 17.1 us  [the longest x3 10.9 us: shift_x(): lax.ppermute(part(True), 'gx', up)]
    ppermute x8 -> x6, waiting for transfers between devices: 5.99 us -> 9.83 us  [the longest x3 9.82 us: shift_x(): lax.ppermute(part(True), 'gx', up)]
    unnamed x54 -> x50, local copies, waits for them, and re-layouts: 8.87 us -> 8.95 us
  transfers between devices with their start and end apart: 22 -> 20, of which waited for: 4 -> 5; matrix products, arithmetic and copies ran while one was open for 6% -> 6% of each run, Pallas kernels for 32% -> 32%
where the time goes in v4:
time: 312 us; the launch traced here: 310 us
  Pallas kernels  117 us (38%)
  waiting for transfers between devices  106 us (34%)
  starting transfers between devices  55.9 us (18%)
  local copies, waits for them, and re-layouts  21 us (7%)
  other arithmetic  9.23 us (3%)
    ppermute x1, waiting for transfers between devices, local(): shells_far = lax.ppermute(shells, 'gx', opposite)  50.1 us
    pallas_call x2, Pallas kernels, inner(): pl.pallas_call(functools.partial(inner_body, table, is_warped), out_shape...  44.3 us
    ppermute x1, waiting for transfers between devices, local(): mirror_a = lax.ppermute(first[:PART], 'gx', opposite)  28.3 us
    all_to_all x4, starting transfers between devices, send(): lax.all_to_all(slots, 'gx', split_axis=0, concat_axis=0, axis_index_group...  24.4 us
    pallas_call x2, Pallas kernels, rim(): pl.pallas_call(functools.partial(rim_body, table, is_warped), out_shape=j...  23.4 us
    pallas_call x4, Pallas kernels, pack(): pl.pallas_call(functools.partial(pack_body, table, t, far, count, shells...  18.3 us
    pallas_call x1, Pallas kernels, warp(): pl.pallas_call(functools.partial(warp_body, table, t), out_shape=jax.Shap...  18 us
    all_to_all x4, waiting for transfers between devices, send(): lax.all_to_all(slots, 'gx', split_axis=0, concat_axis=0, axis_index_group...  18 us
  transfers between devices with their start and end apart: 20, of which 5 were waited for; matrix products, arithmetic and copies ran while one was open for 6% of the time, Pallas kernels for 32%

profile of v4, /device:TPU:23, one launch (start us, length us, event | category | flops | bytes accessed | tf_op | source)
XLA Modules:
  0.0 310.0 jit_solution(3564118514248150027)
XLA Ops:
  3.6 4.0 %collective-permute-start = (bf16[1,128,128]{2,1,0:T(8,128)(2,1)S(1)}, bf16[1,128,128]{2,1,0:T(8,128)(2,1)S(1)}, u32[]{:S(2)}, u32[]{:S(2)}) collective-permute-start(bf16[1,128,128]{2,1,0:T(8,128)(2,1)S(1)} %get-tuple-element.43), channel_id=1, source_target_pairs={{0,2},{2,4},{4,6},{6,8},{8,10},{10,12},{12,14},{1,3},{3,5},{5,7},{... | collective-permute-start | bytes 98312 | tf_op jit(solution)/shard_map/ppermute | solution.py:724
  13.4 4.5 %pack0own.1 = bf16[4,2048,128]{2,1,0:T(8,128)(2,1)} custom-call(s32[258]{0:T(512)} %pad_add_fusion.ref, bf16[64,128,128]{2,1,0:T(8,128)(2,1)} %refs_1_.3, bf16[64,128,128]{2,1,0:T(8,128)(2,1)} %refs_1_.3), custom_call_target="tpu_custom_call" | custom-call | flops 65536 | bytes 65536 | tf_op jit(solution)/shard_map/pack0own/pallas_call | solution.py:121
  18.7 4.6 %all-to-all-start = ((bf16[4,2048,128]{2,1,0:T(8,128)(2,1)}), bf16[4,2048,128]{2,1,0:T(8,128)(2,1)}, u32[]{:S(2)}, u32[]{:S(2)}) async-start(bf16[4,2048,128]{2,1,0:T(8,128)(2,1)} %pack0own.1), calls=%async_computation | async-start | bytes 4194304 | tf_op jit(solution)/shard_map/all_to_all | solution.py:719
  26.2 8.8 %columns.1 = bf16[2,160,128]{2,1,0:T(8,128)(2,1)} custom-call(s32[258]{0:T(512)} %pad_add_fusion.ref, bf16[1,128,128]{2,1,0:T(8,128)(2,1)} %copy-done.16, bf16[64,128,128]{2,1,0:T(8,128)(2,1)} %refs_1_.3, bf16[1,128,128]{2,1,0:T(8,128)(2,1)} %copy-done.15, bf16[66,16,128]{2,1,0:T(8,128)(2,1)} %copy-done.10), custom_call_target="tpu_custom_call" | custom-call | flops 65536 | bytes 65536 | tf_op jit(solution)/shard_map/columns/pallas_call | solution.py:669
  37.0 4.6 %pack1own.1 = bf16[4,2272,128]{2,1,0:T(8,128)(2,1)} custom-call(s32[258]{0:T(512)} %pad_add_fusion.ref, bf16[64,128,128]{2,1,0:T(8,128)(2,1)} %refs_1_.3, bf16[64,128,128]{2,1,0:T(8,128)(2,1)} %refs_1_.3, bf16[4,224,128]{2,1,0:T(8,128)(2,1)} %pad_maximum_fusion.6.refs_2_), custom_call_target="tpu_custom_call" | custom-call | flops 65536 | bytes 65536 | tf_op jit(solution)/shard_map/pack1own/pallas_call | solution.py:121
  41.6 28.3 %collective-permute-done.3.refs_0_ = bf16[32,128,128]{2,1,0:T(8,128)(2,1)S(1)} collective-permute-done((bf16[32,128,128]{2,1,0:T(8,128)(2,1)S(1)}, bf16[32,128,128]{2,1,0:T(8,128)(2,1)S(1)}, u32[]{:S(2)}, u32[]{:S(2)}) %collective-permute-start.3) | collective-permute-done | bytes 1048608 | tf_op jit(solution)/shard_map/ppermute | solution.py:730
  70.9 6.7 %all-to-all-start.1 = ((bf16[4,2272,128]{2,1,0:T(8,128)(2,1)}), bf16[4,2272,128]{2,1,0:T(8,128)(2,1)S(1)}, u32[]{:S(2)}, u32[]{:S(2)}) async-start(bf16[4,2272,128]{2,1,0:T(8,128)(2,1)} %pack1own.1), calls=%async_computation.1 | async-start | bytes 4653056 | tf_op jit(solution)/shard_map/all_to_all | solution.py:719
  79.9 50.1 %collective-permute-done.6.refs_2_ = bf16[4,224,128]{2,1,0:T(8,128)(2,1)S(1)} collective-permute-done((bf16[4,224,128]{2,1,0:T(8,128)(2,1)}, bf16[4,224,128]{2,1,0:T(8,128)(2,1)S(1)}, u32[]{:S(2)}, u32[]{:S(2)}) %collective-permute-start.6) | collective-permute-done | bytes 229408 | tf_op jit(solution)/shard_map/ppermute | solution.py:741
  131.8 4.6 %pack0far.1 = bf16[4,2048,128]{2,1,0:T(8,128)(2,1)} custom-call(s32[258]{0:T(512)} %pad_add_fusion.ref, bf16[32,128,128]{2,1,0:T(8,128)(2,1)} %copy-done.4, bf16[32,128,128]{2,1,0:T(8,128)(2,1)} %copy-done.5), custom_call_target="tpu_custom_call" | custom-call | flops 65536 | bytes 65536 | tf_op jit(solution)/shard_map/pack0far/pallas_call | solution.py:121
  136.4 7.8 %all-to-all-start.2 = ((bf16[4,2048,128]{2,1,0:T(8,128)(2,1)}), bf16[4,2048,128]{2,1,0:T(8,128)(2,1)S(1)}, u32[]{:S(2)}, u32[]{:S(2)}) async-start(bf16[4,2048,128]{2,1,0:T(8,128)(2,1)} %pack0far.1), calls=%async_computation.2 | async-start | bytes 4194304 | tf_op jit(solution)/shard_map/all_to_all | solution.py:719
  144.2 4.6 %pack1far.1 = bf16[4,2272,128]{2,1,0:T(8,128)(2,1)} custom-call(s32[258]{0:T(512)} %pad_add_fusion.ref, bf16[32,128,128]{2,1,0:T(8,128)(2,1)} %copy-done.4, bf16[32,128,128]{2,1,0:T(8,128)(2,1)} %copy-done.5, bf16[4,224,128]{2,1,0:T(8,128)(2,1)} %copy-done.19), custom_call_target="tpu_custom_call" | custom-call | flops 134217728 | bytes 134217728 | tf_op jit(solution)/shard_map/pack1far/pallas_call | solution.py:121
  148.8 18.0 %all-to-all-done.2.far_ref = bf16[4,2048,128]{2,1,0:T(8,128)(2,1)S(1)} async-done(((bf16[4,2048,128]{2,1,0:T(8,128)(2,1)}), bf16[4,2048,128]{2,1,0:T(8,128)(2,1)S(1)}, u32[]{:S(2)}, u32[]{:S(2)}) %all-to-all-start.2) | async-done | bytes 2097184 | tf_op jit(solution)/shard_map/all_to_all | solution.py:719
  168.1 5.3 %all-to-all-start.3 = ((bf16[4,2272,128]{2,1,0:T(8,128)(2,1)}), bf16[4,2272,128]{2,1,0:T(8,128)(2,1)S(1)}, u32[]{:S(2)}, u32[]{:S(2)}) async-start(bf16[4,2272,128]{2,1,0:T(8,128)(2,1)} %pack1far.1), calls=%async_computation.3 | async-start | bytes 4653056 | tf_op jit(solution)/shard_map/all_to_all | solution.py:719
  174.5 3.9 %pick.1.value = bf16[64,128,128]{2,1,0:T(8,128)(2,1)} custom-call(s32[258]{0:T(512)} %pad_add_fusion.ref, bf16[4,2048,128]{2,1,0:T(8,128)(2,1)} %all-to-all-done.own_ref, bf16[4,2048,128]{2,1,0:T(8,128)(2,1)} %copy-done.3), custom_call_target="tpu_custom_call" | custom-call | flops 2097152 | bytes 4194304 | tf_op jit(solution)/shard_map/pick/pallas_call | solution.py:195
  183.1 3.1 collective-permute-start.8
  188.5 21.6 %inner0.1.refs_4_ = f32[3,64,128,128]{3,2,1,0:T(8,128)} custom-call(s32[258]{0:T(512)} %pad_add_fusion.ref, bf16[256,256]{1,0:T(8,128)(2,1)} %constant.30.weights, bf16[64,128,128]{2,1,0:T(8,128)(2,1)} %pick.1.value, bf16[64,16,128]{2,1,0:T(8,128)(2,1)} %copy-done.12, bf16[64,128,128]{2,1,0:T(8,128)(2,1)} %fixed.9, ...), custom_call_target="tpu_custom_call" | custom-call | flops 209715200 | bytes 31457280 | tf_op jit(solution)/shard_map/inner0/pallas_call | solution.py:490
  210.0 3.9 %collective-permute-done.8.refs_0_.refs_2_ = bf16[10,144,128]{2,1,0:T(8,128)(2,1)S(1)} collective-permute-done((bf16[10,144,128]{2,1,0:T(8,128)(2,1)S(1)}, bf16[10,144,128]{2,1,0:T(8,128)(2,1)S(1)}, u32[]{:S(2)}, u32[]{:S(2)}) %collective-permute-start.8) | collective-permute-done | bytes 368672 | tf_op jit(solution)/shard_map/ppermute | solution.py:631
  215.4 10.9 %rim0.1.field.refs_0_.refs_4_ = f32[3,64,128,128]{3,2,1,0:T(8,128)} custom-call(s32[258]{0:T(512)} %pad_add_fusion.ref, bf16[256,256]{1,0:T(8,128)(2,1)} %constant.30.weights, bf16[64,128,128]{2,1,0:T(8,128)(2,1)} %pick.1.value, bf16[64,16,128]{2,1,0:T(8,128)(2,1)} %copy-done.12, bf16[64,128,128]{2,1,0:T(8,128)(2,1)} %fixed.9, ...), custom_call_target="tpu_custom_call", output_to_operand_aliasing={{}: (10, {})} | custom-call | flops 62914560 | bytes 10485760 | tf_op jit(solution)/shard_map/rim0/pallas_call | solution.py:589
  233.4 3.5 %collective-permute-start.14 = (f32[3,4,136,128]{3,2,1,0:T(8,128)}, f32[3,4,136,128]{3,2,1,0:T(8,128)}, u32[]{:S(2)}, u32[]{:S(2)}) collective-permute-start(f32[3,4,136,128]{3,2,1,0:T(8,128)} %pad_maximum_fusion), channel_id=1, source_target_pairs={{0,2},{2,4},{4,6},{6,8},{8,10},{10,12},{12,14},{1,3},{3,5},{5,7},{... | collective-permute-start | bytes 2506760 | tf_op jit(solution)/shard_map/ppermute | solution.py:631
  238.3 18.0 %warp.1.value = f32[64,128,128]{2,1,0:T(8,128)} custom-call(s32[258]{0:T(512)} %pad_add_fusion.ref, bf16[4,2272,128]{2,1,0:T(8,128)(2,1)} %copy-done.1, bf16[4,2272,128]{2,1,0:T(8,128)(2,1)} %copy-done.2, bf16[64,128,128]{2,1,0:T(8,128)(2,1)} %fixed.9, f32[3,64,128,128]{3,2,1,0:T(8,128)} %rim0.1.field.refs_0_.refs_4_), custom_call_target="tpu_custom_call" | custom-call | flops 62914560 | bytes 23068672 | tf_op jit(solution)/shard_map/warp/pallas_call | solution.py:324
  260.9 4.3 %collective-permute-start.11 = (f32[5,136,128]{2,1,0:T(8,128)S(1)}, f32[5,136,128]{2,1,0:T(8,128)S(1)}, u32[]{:S(2)}, u32[]{:S(2)}) collective-permute-start(f32[5,136,128]{2,1,0:T(8,128)S(1)} %pad_maximum_fusion.3), channel_id=1, source_target_pairs={{0,2},{2,4},{4,6},{6,8},{8,10},{10,12},{12,14},{1,3},{3,5},{5,7},{... | collective-permute-start | bytes 1044488 | tf_op jit(solution)/shard_map/ppermute | solution.py:631
  267.4 22.7 %inner1.1.refs_8_ = f32[3,64,128,128]{3,2,1,0:T(8,128)} custom-call(s32[258]{0:T(512)} %pad_add_fusion.ref, bf16[256,256]{1,0:T(8,128)(2,1)} %constant.30.weights, f32[64,128,128]{2,1,0:T(8,128)} %warp.1.value, f32[64,8,128]{2,1,0:T(8,128)} %copy-done.11, bf16[64,128,128]{2,1,0:T(8,128)(2,1)} %fixed.9, bf16[64,16,128]{2,1,0:T(8,128)(2,1)} %get-tuple-element.48.fixed_y, ...), custom_call_target="tpu_custom_call" | custom-call | flops 209715200 | bytes 31457280 | tf_op jit(solution)/shard_map/inner1/pallas_call | solution.py:490
  290.1 6.0 %collective-permute-done.11.refs_0_ = f32[5,136,128]{2,1,0:T(8,128)S(1)} collective-permute-done((f32[5,136,128]{2,1,0:T(8,128)S(1)}, f32[5,136,128]{2,1,0:T(8,128)S(1)}, u32[]{:S(2)}, u32[]{:S(2)}) %collective-permute-start.11) | collective-permute-done | bytes 348192 | tf_op jit(solution)/shard_map/ppermute | solution.py:631
  297.6 12.4 %rim1.1 = f32[3,64,128,128]{3,2,1,0:T(8,128)} custom-call(s32[258]{0:T(512)} %pad_add_fusion.ref, bf16[256,256]{1,0:T(8,128)(2,1)} %constant.30.weights, f32[64,128,128]{2,1,0:T(8,128)} %warp.1.value, f32[64,8,128]{2,1,0:T(8,128)} %copy-done.11, bf16[64,128,128]{2,1,0:T(8,128)(2,1)} %fixed.9, ...), custom_call_target="tpu_custom_call", output_to_operand_aliasing={{}: (14, {})} | custom-call | flops 62914560 | bytes 10485760 | tf_op jit(solution)/shard_map/rim1/pallas_call | solution.py:589
  (128 shorter events, 46.9 us)
Async XLA Ops:
  0.6 10.8 %copy-start.22 = (s32[2,8,4,2]{1,3,2,0:T(2,128)S(1)}, s32[2,8,4,2]{1,3,2,0:T(2,128)}, u32[]{:S(2)}) copy-start(s32[2,8,4,2]{1,3,2,0:T(2,128)} %param.8) | copy-start | bytes 1540
  1.4 16.5 %collective-permute-start.1 = (bf16[1,128,128]{2,1,0:T(8,128)(2,1)S(1)}, bf16[1,128,128]{2,1,0:T(8,128)(2,1)S(1)}, u32[]{:S(2)}, u32[]{:S(2)}) collective-permute-start(bf16[1,128,128]{2,1,0:T(8,128)(2,1)S(1)} %get-tuple-element.42), channel_id=1, source_target_pairs={{2,0},{4,2},{6,4},{8,6},{10,8},{12,10},{14,12},{3,1},{5,3},{7,5},{... | collective-permute-start | bytes 98312 | tf_op jit(solution)/shard_map/ppermute | solution.py:725
  3.6 14.4 %collective-permute-start = (bf16[1,128,128]{2,1,0:T(8,128)(2,1)S(1)}, bf16[1,128,128]{2,1,0:T(8,128)(2,1)S(1)}, u32[]{:S(2)}, u32[]{:S(2)}) collective-permute-start(bf16[1,128,128]{2,1,0:T(8,128)(2,1)S(1)} %get-tuple-element.43), channel_id=1, source_target_pairs={{0,2},{2,4},{4,6},{6,8},{8,10},{10,12},{12,14},{1,3},{3,5},{5,7},{... | collective-permute-start | bytes 98312 | tf_op jit(solution)/shard_map/ppermute | solution.py:724
  9.9 8.1 %collective-permute-start.2 = (bf16[128,16,128]{2,1,0:T(8,128)(2,1)S(1)}, bf16[128,16,128]{2,1,0:T(8,128)(2,1)S(1)}, u32[]{:S(2)}, u32[]{:S(2)}) collective-permute-start(bf16[128,16,128]{2,1,0:T(8,128)(2,1)S(1)} %pad_maximum_fusion.2), channel_id=1, source_target_pairs={{0,1},{1,0},{2,3},{3,2},{4,5},{5,4},{6,7},{7,6},{8,9},{9,8},{10,11... | collective-permute-start | bytes 1572872 | tf_op jit(solution)/shard_map/ppermute | solution.py:614
  18.7 51.2 %all-to-all-start = ((bf16[4,2048,128]{2,1,0:T(8,128)(2,1)}), bf16[4,2048,128]{2,1,0:T(8,128)(2,1)}, u32[]{:S(2)}, u32[]{:S(2)}) async-start(bf16[4,2048,128]{2,1,0:T(8,128)(2,1)} %pack0own.1), calls=%async_computation | async-start | bytes 4194304 | tf_op jit(solution)/shard_map/all_to_all | solution.py:719
  23.3 2.2 collective-permute-start.4
  25.3 10.6 %copy-start.20 = (bf16[64,64]{1,0:T(8,128)(2,1)S(1)}, bf16[64,64]{1,0:T(8,128)(2,1)}, u32[]{:S(2)}) copy-start(bf16[64,64]{1,0:T(8,128)(2,1)} %get-tuple-element.87) | copy-start | bytes 24580
  25.4 44.5 %collective-permute-start.3 = (bf16[32,128,128]{2,1,0:T(8,128)(2,1)S(1)}, bf16[32,128,128]{2,1,0:T(8,128)(2,1)S(1)}, u32[]{:S(2)}, u32[]{:S(2)}) collective-permute-start(bf16[32,128,128]{2,1,0:T(8,128)(2,1)S(1)} %get-tuple-element.39), channel_id=1, source_target_pairs={{0,8},{2,10},{4,12},{6,14},{8,0},{10,2},{12,4},{14,6},{1,9},{3,11}... | collective-permute-start | bytes 3145736 | tf_op jit(solution)/shard_map/ppermute | solution.py:730
  70.9 59.9 %all-to-all-start.1 = ((bf16[4,2272,128]{2,1,0:T(8,128)(2,1)}), bf16[4,2272,128]{2,1,0:T(8,128)(2,1)S(1)}, u32[]{:S(2)}, u32[]{:S(2)}) async-start(bf16[4,2272,128]{2,1,0:T(8,128)(2,1)} %pack1own.1), calls=%async_computation.1 | async-start | bytes 4653056 | tf_op jit(solution)/shard_map/all_to_all | solution.py:719
  77.6 53.2 %collective-permute-start.5 = (bf16[32,128,128]{2,1,0:T(8,128)(2,1)}, bf16[32,128,128]{2,1,0:T(8,128)(2,1)S(1)}, u32[]{:S(2)}, u32[]{:S(2)}) collective-permute-start(bf16[32,128,128]{2,1,0:T(8,128)(2,1)} %get-tuple-element.21), channel_id=1, source_target_pairs={{0,8},{2,10},{4,12},{6,14},{8,0},{10,2},{12,4},{14,6},{1,9},{3,11}... | collective-permute-start | bytes 3145736 | tf_op jit(solution)/shard_map/ppermute | solution.py:740
  77.8 52.2 %collective-permute-start.6 = (bf16[4,224,128]{2,1,0:T(8,128)(2,1)}, bf16[4,224,128]{2,1,0:T(8,128)(2,1)S(1)}, u32[]{:S(2)}, u32[]{:S(2)}) collective-permute-start(bf16[4,224,128]{2,1,0:T(8,128)(2,1)} %pad_maximum_fusion.6.refs_2_), channel_id=1, source_target_pairs={{0,8},{2,10},{4,12},{6,14},{8,0},{10,2},{12,4},{14,6},{1,9},{3,11}... | collective-permute-start | bytes 688136 | tf_op jit(solution)/shard_map/ppermute | solution.py:741
  136.4 30.4 %all-to-all-start.2 = ((bf16[4,2048,128]{2,1,0:T(8,128)(2,1)}), bf16[4,2048,128]{2,1,0:T(8,128)(2,1)S(1)}, u32[]{:S(2)}, u32[]{:S(2)}) async-start(bf16[4,2048,128]{2,1,0:T(8,128)(2,1)} %pack0far.1), calls=%async_computation.2 | async-start | bytes 4194304 | tf_op jit(solution)/shard_map/all_to_all | solution.py:719
  168.1 68.8 %all-to-all-start.3 = ((bf16[4,2272,128]{2,1,0:T(8,128)(2,1)}), bf16[4,2272,128]{2,1,0:T(8,128)(2,1)S(1)}, u32[]{:S(2)}, u32[]{:S(2)}) async-start(bf16[4,2272,128]{2,1,0:T(8,128)(2,1)} %pack1far.1), calls=%async_computation.3 | async-start | bytes 4653056 | tf_op jit(solution)/shard_map/all_to_all | solution.py:719
  179.4 3.6 %collective-permute-start.7 = (bf16[64,16,128]{2,1,0:T(8,128)(2,1)S(1)}, bf16[64,16,128]{2,1,0:T(8,128)(2,1)S(1)}, u32[]{:S(2)}, u32[]{:S(2)}) collective-permute-start(bf16[64,16,128]{2,1,0:T(8,128)(2,1)S(1)} %slice_select_fusion.2), channel_id=1, source_target_pairs={{0,1},{1,0},{2,3},{3,2},{4,5},{5,4},{6,7},{7,6},{8,9},{9,8},{10,11... | collective-permute-start | bytes 786440 | tf_op jit(solution)/shard_map/ppermute | solution.py:614
  183.1 30.8 %collective-permute-start.8 = (bf16[10,144,128]{2,1,0:T(8,128)(2,1)S(1)}, bf16[10,144,128]{2,1,0:T(8,128)(2,1)S(1)}, u32[]{:S(2)}, u32[]{:S(2)}) collective-permute-start(bf16[10,144,128]{2,1,0:T(8,128)(2,1)S(1)} %maximum_maximum_fusion), channel_id=1, source_target_pairs={{0,2},{2,4},{4,6},{6,8},{8,10},{10,12},{12,14},{1,3},{3,5},{5,7},{... | collective-permute-start | bytes 1105928 | tf_op jit(solution)/shard_map/ppermute | solution.py:631
  186.3 27.6 %collective-permute-start.9 = (bf16[10,144,128]{2,1,0:T(8,128)(2,1)S(1)}, bf16[10,144,128]{2,1,0:T(8,128)(2,1)S(1)}, u32[]{:S(2)}, u32[]{:S(2)}) collective-permute-start(bf16[10,144,128]{2,1,0:T(8,128)(2,1)S(1)} %maximum_maximum_fusion.1), channel_id=1, source_target_pairs={{2,0},{4,2},{6,4},{8,6},{10,8},{12,10},{14,12},{3,1},{5,3},{7,5},{... | collective-permute-start | bytes 1105928 | tf_op jit(solution)/shard_map/ppermute | solution.py:631
  227.8 4.6 %collective-permute-start.13 = (f32[3,64,8,128]{3,2,1,0:T(8,128)S(1)}, f32[3,64,8,128]{3,2,1,0:T(8,128)S(1)}, u32[]{:S(2)}, u32[]{:S(2)}) collective-permute-start(f32[3,64,8,128]{3,2,1,0:T(8,128)S(1)} %slice_select_fusion), channel_id=1, source_target_pairs={{0,1},{1,0},{2,3},{3,2},{4,5},{5,4},{6,7},{7,6},{8,9},{9,8},{10,11... | collective-permute-start | bytes 2359304 | tf_op jit(solution)/shard_map/ppermute | solution.py:614
  232.3 24.0 %copy-start.6 = (f32[3,64,8,128]{3,2,1,0:T(8,128)}, f32[3,64,8,128]{3,2,1,0:T(8,128)S(1)}, u32[]{:S(2)}) copy-start(f32[3,64,8,128]{3,2,1,0:T(8,128)S(1)} %collective-permute-done.13.refs_1_.refs_5_) | copy-start | bytes 2359300
  233.4 56.7 %collective-permute-start.14 = (f32[3,4,136,128]{3,2,1,0:T(8,128)}, f32[3,4,136,128]{3,2,1,0:T(8,128)}, u32[]{:S(2)}, u32[]{:S(2)}) collective-permute-start(f32[3,4,136,128]{3,2,1,0:T(8,128)} %pad_maximum_fusion), channel_id=1, source_target_pairs={{0,2},{2,4},{4,6},{6,8},{8,10},{10,12},{12,14},{1,3},{3,5},{5,7},{... | collective-permute-start | bytes 2506760 | tf_op jit(solution)/shard_map/ppermute | solution.py:631
  238.3 19.4 %copy-start.9 = (f32[3,4,128,128]{3,2,1,0:T(8,128)S(1)}, f32[3,4,128,128]{3,2,1,0:T(8,128)}, u32[]{:S(2)}) copy-start(f32[3,4,128,128]{3,2,1,0:T(8,128)} %get-tuple-element.30) | copy-start | bytes 2359300
  257.4 3.5 %collective-permute-start.10 = (f32[64,8,128]{2,1,0:T(8,128)S(1)}, f32[64,8,128]{2,1,0:T(8,128)S(1)}, u32[]{:S(2)}, u32[]{:S(2)}) collective-permute-start(f32[64,8,128]{2,1,0:T(8,128)S(1)} %slice_select_fusion.1), channel_id=1, source_target_pairs={{0,1},{1,0},{2,3},{3,2},{4,5},{5,4},{6,7},{7,6},{8,9},{9,8},{10,11... | collective-permute-start | bytes 786440 | tf_op jit(solution)/shard_map/ppermute | solution.py:614
  257.8 32.3 %collective-permute-start.15 = (f32[3,4,136,128]{3,2,1,0:T(8,128)S(1)}, f32[3,4,136,128]{3,2,1,0:T(8,128)S(1)}, u32[]{:S(2)}, u32[]{:S(2)}) collective-permute-start(f32[3,4,136,128]{3,2,1,0:T(8,128)S(1)} %pad_maximum_fusion.1), channel_id=1, source_target_pairs={{2,0},{4,2},{6,4},{8,6},{10,8},{12,10},{14,12},{3,1},{5,3},{7,5},{... | collective-permute-start | bytes 2506760 | tf_op jit(solution)/shard_map/ppermute | solution.py:631
  260.9 35.1 %collective-permute-start.11 = (f32[5,136,128]{2,1,0:T(8,128)S(1)}, f32[5,136,128]{2,1,0:T(8,128)S(1)}, u32[]{:S(2)}, u32[]{:S(2)}) collective-permute-start(f32[5,136,128]{2,1,0:T(8,128)S(1)} %pad_maximum_fusion.3), channel_id=1, source_target_pairs={{0,2},{2,4},{4,6},{6,8},{8,10},{10,12},{12,14},{1,3},{3,5},{5,7},{... | collective-permute-start | bytes 1044488 | tf_op jit(solution)/shard_map/ppermute | solution.py:631
  265.3 30.8 %collective-permute-start.12 = (f32[5,136,128]{2,1,0:T(8,128)S(1)}, f32[5,136,128]{2,1,0:T(8,128)S(1)}, u32[]{:S(2)}, u32[]{:S(2)}) collective-permute-start(f32[5,136,128]{2,1,0:T(8,128)S(1)} %pad_maximum_fusion.4), channel_id=1, source_target_pairs={{2,0},{4,2},{6,4},{8,6},{10,8},{12,10},{14,12},{3,1},{5,3},{7,5},{... | collective-permute-start | bytes 1044488 | tf_op jit(solution)/shard_map/ppermute | solution.py:631
  (19 other events, 54.6 us)

commit v5 on v4

--- a/solution.py
+++ b/solution.py
@@ -369,7 +369,7 @@
         diff[j, 144:152, :] = jnp.where(g == 0, my, zero)
         return carry
 
-    lax.fori_loop(0, count, step, 0)
+    lax.fori_loop(0, count, step, 0, unroll=count)
 
 
 def update_planes(g, count, base, start, total, diff, summed, prior, prior_y, source):

time: 312 us -> 312 us (level)
  no operation moved by 1% of the time
where the time goes in v5:
time: 312 us; the launch traced here: 310 us
  Pallas kernels  116 us (37%)
  waiting for transfers between devices  107 us (34%)
  starting transfers between devices  55.9 us (18%)
  local copies, waits for them, and re-layouts  21 us (7%)
  other arithmetic  9.23 us (3%)
    ppermute x1, waiting for transfers between devices, local(): shells_far = lax.ppermute(shells, 'gx', opposite)  50.1 us
    pallas_call x2, Pallas kernels, inner(): pl.pallas_call(functools.partial(inner_body, table, is_warped), out_shape...  43.9 us
    ppermute x1, waiting for transfers between devices, local(): mirror_a = lax.ppermute(first[:PART], 'gx', opposite)  28.3 us
    all_to_all x4, starting transfers between devices, send(): lax.all_to_all(slots, 'gx', split_axis=0, concat_axis=0, axis_index_group...  24.4 us
    pallas_call x2, Pallas kernels, rim(): pl.pallas_call(functools.partial(rim_body, table, is_warped), out_shape=j...  23 us
    pallas_call x4, Pallas kernels, pack(): pl.pallas_call(functools.partial(pack_body, table, t, far, count, shells...  18.3 us
    pallas_call x1, Pallas kernels, warp(): pl.pallas_call(functools.partial(warp_body, table, t), out_shape=jax.Shap...  18 us
    all_to_all x4, waiting for transfers between devices, send(): lax.all_to_all(slots, 'gx', split_axis=0, concat_axis=0, axis_index_group...  18 us
  transfers between devices with their start and end apart: 20, of which 5 were waited for; matrix products, arithmetic and copies ran while one was open for 6% of the time, Pallas kernels for 32%

profile of v5, /device:TPU:23, one launch (start us, length us, event | category | flops | bytes accessed | tf_op | source)
XLA Modules:
  0.0 309.7 jit_solution(4799453629218562875)
XLA Ops:
  3.6 4.0 %collective-permute-start = (bf16[1,128,128]{2,1,0:T(8,128)(2,1)S(1)}, bf16[1,128,128]{2,1,0:T(8,128)(2,1)S(1)}, u32[]{:S(2)}, u32[]{:S(2)}) collective-permute-start(bf16[1,128,128]{2,1,0:T(8,128)(2,1)S(1)} %get-tuple-element.43), channel_id=1, source_target_pairs={{0,2},{2,4},{4,6},{6,8},{8,10},{10,12},{12,14},{1,3},{3,5},{5,7},{... | collective-permute-start | bytes 98312 | tf_op jit(solution)/shard_map/ppermute | solution.py:724
  13.4 4.5 %pack0own.1 = bf16[4,2048,128]{2,1,0:T(8,128)(2,1)} custom-call(s32[258]{0:T(512)} %pad_add_fusion.ref, bf16[64,128,128]{2,1,0:T(8,128)(2,1)} %refs_1_.3, bf16[64,128,128]{2,1,0:T(8,128)(2,1)} %refs_1_.3), custom_call_target="tpu_custom_call" | custom-call | flops 65536 | bytes 65536 | tf_op jit(solution)/shard_map/pack0own/pallas_call | solution.py:121
  18.7 4.6 %all-to-all-start = ((bf16[4,2048,128]{2,1,0:T(8,128)(2,1)}), bf16[4,2048,128]{2,1,0:T(8,128)(2,1)}, u32[]{:S(2)}, u32[]{:S(2)}) async-start(bf16[4,2048,128]{2,1,0:T(8,128)(2,1)} %pack0own.1), calls=%async_computation | async-start | bytes 4194304 | tf_op jit(solution)/shard_map/all_to_all | solution.py:719
  26.2 8.8 %columns.1 = bf16[2,160,128]{2,1,0:T(8,128)(2,1)} custom-call(s32[258]{0:T(512)} %pad_add_fusion.ref, bf16[1,128,128]{2,1,0:T(8,128)(2,1)} %copy-done.16, bf16[64,128,128]{2,1,0:T(8,128)(2,1)} %refs_1_.3, bf16[1,128,128]{2,1,0:T(8,128)(2,1)} %copy-done.15, bf16[66,16,128]{2,1,0:T(8,128)(2,1)} %copy-done.10), custom_call_target="tpu_custom_call" | custom-call | flops 65536 | bytes 65536 | tf_op jit(solution)/shard_map/columns/pallas_call | solution.py:669
  37.0 4.6 %pack1own.1 = bf16[4,2272,128]{2,1,0:T(8,128)(2,1)} custom-call(s32[258]{0:T(512)} %pad_add_fusion.ref, bf16[64,128,128]{2,1,0:T(8,128)(2,1)} %refs_1_.3, bf16[64,128,128]{2,1,0:T(8,128)(2,1)} %refs_1_.3, bf16[4,224,128]{2,1,0:T(8,128)(2,1)} %pad_maximum_fusion.6.refs_2_), custom_call_target="tpu_custom_call" | custom-call | flops 65536 | bytes 65536 | tf_op jit(solution)/shard_map/pack1own/pallas_call | solution.py:121
  41.6 28.3 %collective-permute-done.3.refs_0_ = bf16[32,128,128]{2,1,0:T(8,128)(2,1)S(1)} collective-permute-done((bf16[32,128,128]{2,1,0:T(8,128)(2,1)S(1)}, bf16[32,128,128]{2,1,0:T(8,128)(2,1)S(1)}, u32[]{:S(2)}, u32[]{:S(2)}) %collective-permute-start.3) | collective-permute-done | bytes 1048608 | tf_op jit(solution)/shard_map/ppermute | solution.py:730
  70.9 6.7 %all-to-all-start.1 = ((bf16[4,2272,128]{2,1,0:T(8,128)(2,1)}), bf16[4,2272,128]{2,1,0:T(8,128)(2,1)S(1)}, u32[]{:S(2)}, u32[]{:S(2)}) async-start(bf16[4,2272,128]{2,1,0:T(8,128)(2,1)} %pack1own.1), calls=%async_computation.1 | async-start | bytes 4653056 | tf_op jit(solution)/shard_map/all_to_all | solution.py:719
  79.9 50.1 %collective-permute-done.6.refs_2_ = bf16[4,224,128]{2,1,0:T(8,128)(2,1)S(1)} collective-permute-done((bf16[4,224,128]{2,1,0:T(8,128)(2,1)}, bf16[4,224,128]{2,1,0:T(8,128)(2,1)S(1)}, u32[]{:S(2)}, u32[]{:S(2)}) %collective-permute-start.6) | collective-permute-done | bytes 229408 | tf_op jit(solution)/shard_map/ppermute | solution.py:741
  131.8 4.6 %pack0far.1 = bf16[4,2048,128]{2,1,0:T(8,128)(2,1)} custom-call(s32[258]{0:T(512)} %pad_add_fusion.ref, bf16[32,128,128]{2,1,0:T(8,128)(2,1)} %copy-done.4, bf16[32,128,128]{2,1,0:T(8,128)(2,1)} %copy-done.5), custom_call_target="tpu_custom_call" | custom-call | flops 65536 | bytes 65536 | tf_op jit(solution)/shard_map/pack0far/pallas_call | solution.py:121
  136.4 7.8 %all-to-all-start.2 = ((bf16[4,2048,128]{2,1,0:T(8,128)(2,1)}), bf16[4,2048,128]{2,1,0:T(8,128)(2,1)S(1)}, u32[]{:S(2)}, u32[]{:S(2)}) async-start(bf16[4,2048,128]{2,1,0:T(8,128)(2,1)} %pack0far.1), calls=%async_computation.2 | async-start | bytes 4194304 | tf_op jit(solution)/shard_map/all_to_all | solution.py:719
  144.2 4.6 %pack1far.1 = bf16[4,2272,128]{2,1,0:T(8,128)(2,1)} custom-call(s32[258]{0:T(512)} %pad_add_fusion.ref, bf16[32,128,128]{2,1,0:T(8,128)(2,1)} %copy-done.4, bf16[32,128,128]{2,1,0:T(8,128)(2,1)} %copy-done.5, bf16[4,224,128]{2,1,0:T(8,128)(2,1)} %copy-done.19), custom_call_target="tpu_custom_call" | custom-call | flops 134217728 | bytes 134217728 | tf_op jit(solution)/shard_map/pack1far/pallas_call | solution.py:121
  148.8 18.0 %all-to-all-done.2.far_ref = bf16[4,2048,128]{2,1,0:T(8,128)(2,1)S(1)} async-done(((bf16[4,2048,128]{2,1,0:T(8,128)(2,1)}), bf16[4,2048,128]{2,1,0:T(8,128)(2,1)S(1)}, u32[]{:S(2)}, u32[]{:S(2)}) %all-to-all-start.2) | async-done | bytes 2097184 | tf_op jit(solution)/shard_map/all_to_all | solution.py:719
  168.1 5.3 %all-to-all-start.3 = ((bf16[4,2272,128]{2,1,0:T(8,128)(2,1)}), bf16[4,2272,128]{2,1,0:T(8,128)(2,1)S(1)}, u32[]{:S(2)}, u32[]{:S(2)}) async-start(bf16[4,2272,128]{2,1,0:T(8,128)(2,1)} %pack1far.1), calls=%async_computation.3 | async-start | bytes 4653056 | tf_op jit(solution)/shard_map/all_to_all | solution.py:719
  174.5 3.9 %pick.1.value = bf16[64,128,128]{2,1,0:T(8,128)(2,1)} custom-call(s32[258]{0:T(512)} %pad_add_fusion.ref, bf16[4,2048,128]{2,1,0:T(8,128)(2,1)} %all-to-all-done.own_ref, bf16[4,2048,128]{2,1,0:T(8,128)(2,1)} %copy-done.3), custom_call_target="tpu_custom_call" | custom-call | flops 2097152 | bytes 4194304 | tf_op jit(solution)/shard_map/pick/pallas_call | solution.py:195
  183.1 3.1 collective-permute-start.8
  188.5 21.2 %inner0.1.refs_4_ = f32[3,64,128,128]{3,2,1,0:T(8,128)} custom-call(s32[258]{0:T(512)} %pad_add_fusion.ref, bf16[256,256]{1,0:T(8,128)(2,1)} %constant.30.weights, bf16[64,128,128]{2,1,0:T(8,128)(2,1)} %pick.1.value, bf16[64,16,128]{2,1,0:T(8,128)(2,1)} %copy-done.12, bf16[64,128,128]{2,1,0:T(8,128)(2,1)} %fixed.9, ...), custom_call_target="tpu_custom_call" | custom-call | flops 209715200 | bytes 31457280 | tf_op jit(solution)/shard_map/inner0/pallas_call | solution.py:490
  209.7 4.2 %collective-permute-done.8.refs_0_.refs_2_ = bf16[10,144,128]{2,1,0:T(8,128)(2,1)S(1)} collective-permute-done((bf16[10,144,128]{2,1,0:T(8,128)(2,1)S(1)}, bf16[10,144,128]{2,1,0:T(8,128)(2,1)S(1)}, u32[]{:S(2)}, u32[]{:S(2)}) %collective-permute-start.8) | collective-permute-done | bytes 368672 | tf_op jit(solution)/shard_map/ppermute | solution.py:631
  215.4 10.7 %rim0.1.field.refs_0_.refs_4_ = f32[3,64,128,128]{3,2,1,0:T(8,128)} custom-call(s32[258]{0:T(512)} %pad_add_fusion.ref, bf16[256,256]{1,0:T(8,128)(2,1)} %constant.30.weights, bf16[64,128,128]{2,1,0:T(8,128)(2,1)} %pick.1.value, bf16[64,16,128]{2,1,0:T(8,128)(2,1)} %copy-done.12, bf16[64,128,128]{2,1,0:T(8,128)(2,1)} %fixed.9, ...), custom_call_target="tpu_custom_call", output_to_operand_aliasing={{}: (10, {})} | custom-call | flops 62914560 | bytes 10485760 | tf_op jit(solution)/shard_map/rim0/pallas_call | solution.py:589
  233.2 3.5 %collective-permute-start.14 = (f32[3,4,136,128]{3,2,1,0:T(8,128)}, f32[3,4,136,128]{3,2,1,0:T(8,128)}, u32[]{:S(2)}, u32[]{:S(2)}) collective-permute-start(f32[3,4,136,128]{3,2,1,0:T(8,128)} %pad_maximum_fusion), channel_id=1, source_target_pairs={{0,2},{2,4},{4,6},{6,8},{8,10},{10,12},{12,14},{1,3},{3,5},{5,7},{... | collective-permute-start | bytes 2506760 | tf_op jit(solution)/shard_map/ppermute | solution.py:631
  238.1 18.0 %warp.1.value = f32[64,128,128]{2,1,0:T(8,128)} custom-call(s32[258]{0:T(512)} %pad_add_fusion.ref, bf16[4,2272,128]{2,1,0:T(8,128)(2,1)} %copy-done.1, bf16[4,2272,128]{2,1,0:T(8,128)(2,1)} %copy-done.2, bf16[64,128,128]{2,1,0:T(8,128)(2,1)} %fixed.9, f32[3,64,128,128]{3,2,1,0:T(8,128)} %rim0.1.field.refs_0_.refs_4_), custom_call_target="tpu_custom_call" | custom-call | flops 62914560 | bytes 23068672 | tf_op jit(solution)/shard_map/warp/pallas_call | solution.py:324
  260.8 4.3 %collective-permute-start.11 = (f32[5,136,128]{2,1,0:T(8,128)S(1)}, f32[5,136,128]{2,1,0:T(8,128)S(1)}, u32[]{:S(2)}, u32[]{:S(2)}) collective-permute-start(f32[5,136,128]{2,1,0:T(8,128)S(1)} %pad_maximum_fusion.3), channel_id=1, source_target_pairs={{0,2},{2,4},{4,6},{6,8},{8,10},{10,12},{12,14},{1,3},{3,5},{5,7},{... | collective-permute-start | bytes 1044488 | tf_op jit(solution)/shard_map/ppermute | solution.py:631
  267.2 22.7 %inner1.1.refs_8_ = f32[3,64,128,128]{3,2,1,0:T(8,128)} custom-call(s32[258]{0:T(512)} %pad_add_fusion.ref, bf16[256,256]{1,0:T(8,128)(2,1)} %constant.30.weights, f32[64,128,128]{2,1,0:T(8,128)} %warp.1.value, f32[64,8,128]{2,1,0:T(8,128)} %copy-done.11, bf16[64,128,128]{2,1,0:T(8,128)(2,1)} %fixed.9, bf16[64,16,128]{2,1,0:T(8,128)(2,1)} %get-tuple-element.48.fixed_y, ...), custom_call_target="tpu_custom_call" | custom-call | flops 209715200 | bytes 31457280 | tf_op jit(solution)/shard_map/inner1/pallas_call | solution.py:490
  289.9 6.0 %collective-permute-done.11.refs_0_ = f32[5,136,128]{2,1,0:T(8,128)S(1)} collective-permute-done((f32[5,136,128]{2,1,0:T(8,128)S(1)}, f32[5,136,128]{2,1,0:T(8,128)S(1)}, u32[]{:S(2)}, u32[]{:S(2)}) %collective-permute-start.11) | collective-permute-done | bytes 348192 | tf_op jit(solution)/shard_map/ppermute | solution.py:631
  297.4 12.3 %rim1.1 = f32[3,64,128,128]{3,2,1,0:T(8,128)} custom-call(s32[258]{0:T(512)} %pad_add_fusion.ref, bf16[256,256]{1,0:T(8,128)(2,1)} %constant.30.weights, f32[64,128,128]{2,1,0:T(8,128)} %warp.1.value, f32[64,8,128]{2,1,0:T(8,128)} %copy-done.11, bf16[64,128,128]{2,1,0:T(8,128)(2,1)} %fixed.9, ...), custom_call_target="tpu_custom_call", output_to_operand_aliasing={{}: (14, {})} | custom-call | flops 62914560 | bytes 10485760 | tf_op jit(solution)/shard_map/rim1/pallas_call | solution.py:589
  (128 shorter events, 46.9 us)
Async XLA Ops:
  0.6 10.8 %copy-start.22 = (s32[2,8,4,2]{1,3,2,0:T(2,128)S(1)}, s32[2,8,4,2]{1,3,2,0:T(2,128)}, u32[]{:S(2)}) copy-start(s32[2,8,4,2]{1,3,2,0:T(2,128)} %param.8) | copy-start | bytes 1540
  1.4 16.5 %collective-permute-start.1 = (bf16[1,128,128]{2,1,0:T(8,128)(2,1)S(1)}, bf16[1,128,128]{2,1,0:T(8,128)(2,1)S(1)}, u32[]{:S(2)}, u32[]{:S(2)}) collective-permute-start(bf16[1,128,128]{2,1,0:T(8,128)(2,1)S(1)} %get-tuple-element.42), channel_id=1, source_target_pairs={{2,0},{4,2},{6,4},{8,6},{10,8},{12,10},{14,12},{3,1},{5,3},{7,5},{... | collective-permute-start | bytes 98312 | tf_op jit(solution)/shard_map/ppermute | solution.py:725
  3.6 14.4 %collective-permute-start = (bf16[1,128,128]{2,1,0:T(8,128)(2,1)S(1)}, bf16[1,128,128]{2,1,0:T(8,128)(2,1)S(1)}, u32[]{:S(2)}, u32[]{:S(2)}) collective-permute-start(bf16[1,128,128]{2,1,0:T(8,128)(2,1)S(1)} %get-tuple-element.43), channel_id=1, source_target_pairs={{0,2},{2,4},{4,6},{6,8},{8,10},{10,12},{12,14},{1,3},{3,5},{5,7},{... | collective-permute-start | bytes 98312 | tf_op jit(solution)/shard_map/ppermute | solution.py:724
  9.9 8.1 %collective-permute-start.2 = (bf16[128,16,128]{2,1,0:T(8,128)(2,1)S(1)}, bf16[128,16,128]{2,1,0:T(8,128)(2,1)S(1)}, u32[]{:S(2)}, u32[]{:S(2)}) collective-permute-start(bf16[128,16,128]{2,1,0:T(8,128)(2,1)S(1)} %pad_maximum_fusion.2), channel_id=1, source_target_pairs={{0,1},{1,0},{2,3},{3,2},{4,5},{5,4},{6,7},{7,6},{8,9},{9,8},{10,11... | collective-permute-start | bytes 1572872 | tf_op jit(solution)/shard_map/ppermute | solution.py:614
  18.7 51.2 %all-to-all-start = ((bf16[4,2048,128]{2,1,0:T(8,128)(2,1)}), bf16[4,2048,128]{2,1,0:T(8,128)(2,1)}, u32[]{:S(2)}, u32[]{:S(2)}) async-start(bf16[4,2048,128]{2,1,0:T(8,128)(2,1)} %pack0own.1), calls=%async_computation | async-start | bytes 4194304 | tf_op jit(solution)/shard_map/all_to_all | solution.py:719
  23.3 2.2 collective-permute-start.4
  25.3 10.6 %copy-start.20 = (bf16[64,64]{1,0:T(8,128)(2,1)S(1)}, bf16[64,64]{1,0:T(8,128)(2,1)}, u32[]{:S(2)}) copy-start(bf16[64,64]{1,0:T(8,128)(2,1)} %get-tuple-element.87) | copy-start | bytes 24580
  25.4 44.5 %collective-permute-start.3 = (bf16[32,128,128]{2,1,0:T(8,128)(2,1)S(1)}, bf16[32,128,128]{2,1,0:T(8,128)(2,1)S(1)}, u32[]{:S(2)}, u32[]{:S(2)}) collective-permute-start(bf16[32,128,128]{2,1,0:T(8,128)(2,1)S(1)} %get-tuple-element.39), channel_id=1, source_target_pairs={{0,8},{2,10},{4,12},{6,14},{8,0},{10,2},{12,4},{14,6},{1,9},{3,11}... | collective-permute-start | bytes 3145736 | tf_op jit(solution)/shard_map/ppermute | solution.py:730
  70.9 59.9 %all-to-all-start.1 = ((bf16[4,2272,128]{2,1,0:T(8,128)(2,1)}), bf16[4,2272,128]{2,1,0:T(8,128)(2,1)S(1)}, u32[]{:S(2)}, u32[]{:S(2)}) async-start(bf16[4,2272,128]{2,1,0:T(8,128)(2,1)} %pack1own.1), calls=%async_computation.1 | async-start | bytes 4653056 | tf_op jit(solution)/shard_map/all_to_all | solution.py:719
  77.6 53.2 %collective-permute-start.5 = (bf16[32,128,128]{2,1,0:T(8,128)(2,1)}, bf16[32,128,128]{2,1,0:T(8,128)(2,1)S(1)}, u32[]{:S(2)}, u32[]{:S(2)}) collective-permute-start(bf16[32,128,128]{2,1,0:T(8,128)(2,1)} %get-tuple-element.21), channel_id=1, source_target_pairs={{0,8},{2,10},{4,12},{6,14},{8,0},{10,2},{12,4},{14,6},{1,9},{3,11}... | collective-permute-start | bytes 3145736 | tf_op jit(solution)/shard_map/ppermute | solution.py:740
  77.8 52.2 %collective-permute-start.6 = (bf16[4,224,128]{2,1,0:T(8,128)(2,1)}, bf16[4,224,128]{2,1,0:T(8,128)(2,1)S(1)}, u32[]{:S(2)}, u32[]{:S(2)}) collective-permute-start(bf16[4,224,128]{2,1,0:T(8,128)(2,1)} %pad_maximum_fusion.6.refs_2_), channel_id=1, source_target_pairs={{0,8},{2,10},{4,12},{6,14},{8,0},{10,2},{12,4},{14,6},{1,9},{3,11}... | collective-permute-start | bytes 688136 | tf_op jit(solution)/shard_map/ppermute | solution.py:741
  136.4 30.4 %all-to-all-start.2 = ((bf16[4,2048,128]{2,1,0:T(8,128)(2,1)}), bf16[4,2048,128]{2,1,0:T(8,128)(2,1)S(1)}, u32[]{:S(2)}, u32[]{:S(2)}) async-start(bf16[4,2048,128]{2,1,0:T(8,128)(2,1)} %pack0far.1), calls=%async_computation.2 | async-start | bytes 4194304 | tf_op jit(solution)/shard_map/all_to_all | solution.py:719
  168.1 68.7 %all-to-all-start.3 = ((bf16[4,2272,128]{2,1,0:T(8,128)(2,1)}), bf16[4,2272,128]{2,1,0:T(8,128)(2,1)S(1)}, u32[]{:S(2)}, u32[]{:S(2)}) async-start(bf16[4,2272,128]{2,1,0:T(8,128)(2,1)} %pack1far.1), calls=%async_computation.3 | async-start | bytes 4653056 | tf_op jit(solution)/shard_map/all_to_all | solution.py:719
  179.4 3.6 %collective-permute-start.7 = (bf16[64,16,128]{2,1,0:T(8,128)(2,1)S(1)}, bf16[64,16,128]{2,1,0:T(8,128)(2,1)S(1)}, u32[]{:S(2)}, u32[]{:S(2)}) collective-permute-start(bf16[64,16,128]{2,1,0:T(8,128)(2,1)S(1)} %slice_select_fusion.2), channel_id=1, source_target_pairs={{0,1},{1,0},{2,3},{3,2},{4,5},{5,4},{6,7},{7,6},{8,9},{9,8},{10,11... | collective-permute-start | bytes 786440 | tf_op jit(solution)/shard_map/ppermute | solution.py:614
  183.1 30.8 %collective-permute-start.8 = (bf16[10,144,128]{2,1,0:T(8,128)(2,1)S(1)}, bf16[10,144,128]{2,1,0:T(8,128)(2,1)S(1)}, u32[]{:S(2)}, u32[]{:S(2)}) collective-permute-start(bf16[10,144,128]{2,1,0:T(8,128)(2,1)S(1)} %maximum_maximum_fusion), channel_id=1, source_target_pairs={{0,2},{2,4},{4,6},{6,8},{8,10},{10,12},{12,14},{1,3},{3,5},{5,7},{... | collective-permute-start | bytes 1105928 | tf_op jit(solution)/shard_map/ppermute | solution.py:631
  186.3 27.6 %collective-permute-start.9 = (bf16[10,144,128]{2,1,0:T(8,128)(2,1)S(1)}, bf16[10,144,128]{2,1,0:T(8,128)(2,1)S(1)}, u32[]{:S(2)}, u32[]{:S(2)}) collective-permute-start(bf16[10,144,128]{2,1,0:T(8,128)(2,1)S(1)} %maximum_maximum_fusion.1), channel_id=1, source_target_pairs={{2,0},{4,2},{6,4},{8,6},{10,8},{12,10},{14,12},{3,1},{5,3},{7,5},{... | collective-permute-start | bytes 1105928 | tf_op jit(solution)/shard_map/ppermute | solution.py:631
  227.6 4.6 %collective-permute-start.13 = (f32[3,64,8,128]{3,2,1,0:T(8,128)S(1)}, f32[3,64,8,128]{3,2,1,0:T(8,128)S(1)}, u32[]{:S(2)}, u32[]{:S(2)}) collective-permute-start(f32[3,64,8,128]{3,2,1,0:T(8,128)S(1)} %slice_select_fusion), channel_id=1, source_target_pairs={{0,1},{1,0},{2,3},{3,2},{4,5},{5,4},{6,7},{7,6},{8,9},{9,8},{10,11... | collective-permute-start | bytes 2359304 | tf_op jit(solution)/shard_map/ppermute | solution.py:614
  232.2 24.0 %copy-start.6 = (f32[3,64,8,128]{3,2,1,0:T(8,128)}, f32[3,64,8,128]{3,2,1,0:T(8,128)S(1)}, u32[]{:S(2)}) copy-start(f32[3,64,8,128]{3,2,1,0:T(8,128)S(1)} %collective-permute-done.13.refs_1_.refs_5_) | copy-start | bytes 2359300
  233.2 56.6 %collective-permute-start.14 = (f32[3,4,136,128]{3,2,1,0:T(8,128)}, f32[3,4,136,128]{3,2,1,0:T(8,128)}, u32[]{:S(2)}, u32[]{:S(2)}) collective-permute-start(f32[3,4,136,128]{3,2,1,0:T(8,128)} %pad_maximum_fusion), channel_id=1, source_target_pairs={{0,2},{2,4},{4,6},{6,8},{8,10},{10,12},{12,14},{1,3},{3,5},{5,7},{... | collective-permute-start | bytes 2506760 | tf_op jit(solution)/shard_map/ppermute | solution.py:631
  238.1 19.4 %copy-start.9 = (f32[3,4,128,128]{3,2,1,0:T(8,128)S(1)}, f32[3,4,128,128]{3,2,1,0:T(8,128)}, u32[]{:S(2)}) copy-start(f32[3,4,128,128]{3,2,1,0:T(8,128)} %get-tuple-element.30) | copy-start | bytes 2359300
  257.2 3.5 %collective-permute-start.10 = (f32[64,8,128]{2,1,0:T(8,128)S(1)}, f32[64,8,128]{2,1,0:T(8,128)S(1)}, u32[]{:S(2)}, u32[]{:S(2)}) collective-permute-start(f32[64,8,128]{2,1,0:T(8,128)S(1)} %slice_select_fusion.1), channel_id=1, source_target_pairs={{0,1},{1,0},{2,3},{3,2},{4,5},{5,4},{6,7},{7,6},{8,9},{9,8},{10,11... | collective-permute-start | bytes 786440 | tf_op jit(solution)/shard_map/ppermute | solution.py:614
  257.6 32.2 %collective-permute-start.15 = (f32[3,4,136,128]{3,2,1,0:T(8,128)S(1)}, f32[3,4,136,128]{3,2,1,0:T(8,128)S(1)}, u32[]{:S(2)}, u32[]{:S(2)}) collective-permute-start(f32[3,4,136,128]{3,2,1,0:T(8,128)S(1)} %pad_maximum_fusion.1), channel_id=1, source_target_pairs={{2,0},{4,2},{6,4},{8,6},{10,8},{12,10},{14,12},{3,1},{5,3},{7,5},{... | collective-permute-start | bytes 2506760 | tf_op jit(solution)/shard_map/ppermute | solution.py:631
  260.8 35.1 %collective-permute-start.11 = (f32[5,136,128]{2,1,0:T(8,128)S(1)}, f32[5,136,128]{2,1,0:T(8,128)S(1)}, u32[]{:S(2)}, u32[]{:S(2)}) collective-permute-start(f32[5,136,128]{2,1,0:T(8,128)S(1)} %pad_maximum_fusion.3), channel_id=1, source_target_pairs={{0,2},{2,4},{4,6},{6,8},{8,10},{10,12},{12,14},{1,3},{3,5},{5,7},{... | collective-permute-start | bytes 1044488 | tf_op jit(solution)/shard_map/ppermute | solution.py:631
  265.1 30.8 %collective-permute-start.12 = (f32[5,136,128]{2,1,0:T(8,128)S(1)}, f32[5,136,128]{2,1,0:T(8,128)S(1)}, u32[]{:S(2)}, u32[]{:S(2)}) collective-permute-start(f32[5,136,128]{2,1,0:T(8,128)S(1)} %pad_maximum_fusion.4), channel_id=1, source_target_pairs={{2,0},{4,2},{6,4},{8,6},{10,8},{12,10},{14,12},{3,1},{5,3},{7,5},{... | collective-permute-start | bytes 1044488 | tf_op jit(solution)/shard_map/ppermute | solution.py:631
  (19 other events, 54.7 us)
